TPU v7x, 1024 devices: a whole 8x8x8 slice. The times are simulated.
1024 devices in a mesh: sx: 64 (over y, x), sy: 16 (over z, core).
Axes of the slice: x: 8, y: 8, z: 8, core: 2. Of those that a mesh axis runs over, the one named last changes fastest.
Arguments:
- strain_rate: float32 [1024, 256, 128], P('sx', 'sy'), may hold values from 0.1 to 10
- deflation: float32 [8, 1024, 256, 128], P(None, 'sx', 'sy'), may hold values from -1.5 to 1.5
- residual: float32 [1024, 256, 128], P('sx', 'sy'), may hold values from -6 to 6
Outputs:
- coarse_blocks: float32 [64, 16, 5, 8, 8], P('sx', 'sy')
- coarse_solution: float32 [64, 16, 8], P('sx', 'sy')
All inputs are finite; a program needn't handle non-finite values.
Results may differ from a plain program's by a relative error of at most 0.0003.
Values sent between devices are 32-bit elements; how exact they have to be, the bound alone decides.
No kernel may reach another device: no remote copies, remote signals or barrier semaphores. Data moves between devices by JAX's collectives and lax.ppermute only.
A program may use at most 32 MiB of HBM per device.

v0:
```python
import jax
import jax.numpy as jnp
from jax import lax
from jax.sharding import PartitionSpec as P

NVEC = 8
ITERS = 6


SIGMA = 0.05
OMEGA = 0.6
HIGH = lax.Precision.HIGHEST


def extended(x, sides, width):
    for axis, dim in sides:
        devices, length = (lax.axis_size(axis), x.shape[dim])
        up = [(i, (i + 1) % devices) for i in range(devices - 1)]
        down = [(j, i) for i, j in up]
        last = lax.slice_in_dim(x, length - width, length, axis=dim)
        first = lax.slice_in_dim(x, 0, width, axis=dim)
        before = lax.ppermute(last, axis, up)
        after = lax.ppermute(first, axis, down)
        x = jnp.concatenate([before, x, after], axis=dim)
    return x


def viscosity(rate):
    return lax.rsqrt(rate) + 0.5 * (1.0 - jnp.exp(-10.0 * rate)) / rate


def block_inverse(self_blocks):
    factor = jnp.linalg.cholesky(self_blocks)
    identity = jnp.eye(self_blocks.shape[-1], dtype=self_blocks.dtype)
    lower_inv = jax.scipy.linalg.solve_triangular(factor, identity, lower=True)
    return jnp.einsum("...ka,...kb->...ab", lower_inv, lower_inv, precision=HIGH)


def coarse_update(blocks, inverse, rhs_values, current, lower_row, upper_row, lower_col, upper_col):

    def product_of(index, vector):
        return jnp.einsum("...ab,...b->...a", blocks[..., index, :, :], vector, precision=HIGH)

    remainder = (
        rhs_values - product_of(0, current) - product_of(1, lower_row) - product_of(2, upper_row)
    )
    remainder = remainder - product_of(3, lower_col) - product_of(4, upper_col)
    return current + OMEGA * jnp.einsum("...ab,...b->...a", inverse, remainder, precision=HIGH)


def per_device(strain_rate, deflation, residual):
    viscous = viscosity(strain_rate)
    stacked = jnp.concatenate([deflation, viscous[None]], 0)
    padded = extended(stacked, (("sx", 1), ("sy", 2)), 1)
    ghosts = padded[:NVEC]
    ghost_visc = padded[NVEC]
    index_x = lax.axis_index("sx")
    index_y = lax.axis_index("sy")
    count_x = lax.axis_size("sx")
    count_y = lax.axis_size("sy")
    face_x = 0.5 * (viscous[1:] + viscous[:-1])
    face_y = 0.5 * (viscous[:, 1:] + viscous[:, :-1])
    face_z = 0.5 * (viscous[:, :, 1:] + viscous[:, :, :-1])
    low_face_x = jnp.where(index_x > 0, 0.5 * (viscous[:1] + ghost_visc[:1, 1:-1]), viscous[:1])
    high_face_x = jnp.where(
        index_x < count_x - 1, 0.5 * (ghost_visc[-1:, 1:-1] + viscous[-1:]), viscous[-1:]
    )
    low_face_y = jnp.where(
        index_y > 0, 0.5 * (viscous[:, :1] + ghost_visc[1:-1, :1]), viscous[:, :1]
    )
    high_face_y = jnp.where(
        index_y < count_y - 1, 0.5 * (ghost_visc[1:-1, -1:] + viscous[:, -1:]), viscous[:, -1:]
    )
    wall_x = jnp.concatenate([low_face_x, face_x, high_face_x], 0)
    wall_y = jnp.concatenate([low_face_y, face_y, high_face_y], 1)
    wall_z = jnp.concatenate([viscous[:, :, :1], face_z, viscous[:, :, -1:]], 2)
    diagonal = (
        SIGMA
        + (wall_x[:-1] + wall_x[1:])
        + (wall_y[:, :-1] + wall_y[:, 1:])
        + (wall_z[:, :, :-1] + wall_z[:, :, 1:])
    )
    nearby = jnp.pad(face_x * deflation[:, 1:], ((0, 0), (0, 1), (0, 0), (0, 0))) + jnp.pad(
        face_x * deflation[:, :-1], ((0, 0), (1, 0), (0, 0), (0, 0))
    )
    nearby = (
        nearby
        + jnp.pad(face_y * deflation[:, :, 1:], ((0, 0), (0, 0), (0, 1), (0, 0)))
        + jnp.pad(face_y * deflation[:, :, :-1], ((0, 0), (0, 0), (1, 0), (0, 0)))
    )
    nearby = (
        nearby
        + jnp.pad(face_z * deflation[:, :, :, 1:], ((0, 0), (0, 0), (0, 0), (0, 1)))
        + jnp.pad(face_z * deflation[:, :, :, :-1], ((0, 0), (0, 0), (0, 0), (1, 0)))
    )
    image = diagonal * deflation - nearby
    self_block = jnp.einsum("aijz,bijz->ab", deflation, image, precision=HIGH)
    block_xlo = -jnp.einsum(
        "ajz,jz,bjz->ab", deflation[:, 0], wall_x[0], ghosts[:, 0, 1:-1], precision=HIGH
    )
    block_xhi = -jnp.einsum(
        "ajz,jz,bjz->ab", deflation[:, -1], wall_x[-1], ghosts[:, -1, 1:-1], precision=HIGH
    )
    block_ylo = -jnp.einsum(
        "aiz,iz,biz->ab", deflation[:, :, 0], wall_y[:, 0], ghosts[:, 1:-1, 0], precision=HIGH
    )
    block_yhi = -jnp.einsum(
        "aiz,iz,biz->ab", deflation[:, :, -1], wall_y[:, -1], ghosts[:, 1:-1, -1], precision=HIGH
    )
    blocks = jnp.stack([self_block, block_xlo, block_xhi, block_ylo, block_yhi], 0)
    rhs_values = jnp.einsum("aijz,ijz->a", deflation, residual, precision=HIGH)
    inverse = block_inverse(blocks[0])
    coarse = jnp.zeros((NVEC,), jnp.float32)
    for repeat in range(ITERS):
        beside_all = extended(coarse.reshape(1, 1, NVEC), (("sx", 0), ("sy", 1)), 1)
        coarse = coarse_update(
            blocks,
            inverse,
            rhs_values,
            coarse,
            beside_all[0, 1],
            beside_all[2, 1],
            beside_all[1, 0],
            beside_all[1, 2],
        )
    owned = coarse.reshape(1, 1, NVEC)
    return (blocks.reshape(1, 1, 5, NVEC, NVEC), owned)


def solution(mesh):
    placed = (P("sx", "sy", None), P(None, "sx", "sy", None), P("sx", "sy", None))
    return jax.shard_map(
        per_device,
        mesh=mesh,
        in_specs=placed,
        out_specs=(P("sx", "sy", None, None, None), P("sx", "sy", None)),
        check_vma=False,
    )
```

profile of v0, /device:TPU:449, one launch (start us, length us, event | category | flops | bytes accessed | tf_op | source)
XLA Modules:
  0.0 167.8 jit_solution(12609725124094602020)
XLA Ops:
  0.7 4.4 %collective-permute-start.5 = (f32[1,1,8]{2,1,0:T(1,128)S(1)}, f32[1,1,8]{2,1,0:T(1,128)S(1)}, u32[]{:S(2)}, u32[]{:S(2)}) collective-permute-start(f32[1,1,8]{2,1,0:T(1,128)S(1)} %broadcast.95), channel_id=1, source_target_pairs={{16,0},{32,16},{48,32},{64,48},{80,64},{96,80},{112,96},{128,112},... | collective-permute-start | bytes 104 | tf_op jit(solution)/shard_map/ppermute | solution.py:23
  5.1 1.9 %collective-permute-start.4 = (f32[1,1,8]{2,1,0:T(1,128)S(1)}, f32[1,1,8]{2,1,0:T(1,128)S(1)}, u32[]{:S(2)}, u32[]{:S(2)}) collective-permute-start(f32[1,1,8]{2,1,0:T(1,128)S(1)} %broadcast.95), channel_id=1, source_target_pairs={{0,16},{16,32},{32,48},{48,64},{64,80},{80,96},{96,112},{112,128},... | collective-permute-start | bytes 104 | tf_op jit(solution)/shard_map/ppermute | solution.py:22
  7.0 1.0 fusion.107
  8.0 1.5 pad_maximum_fusion.10
  9.5 2.2 %collective-permute-start = (f32[9,1,16,128]{3,2,1,0:T(8,128)}, f32[9,1,16,128]{3,2,1,0:T(8,128)}, u32[]{:S(2)}, u32[]{:S(2)}) collective-permute-start(f32[9,1,16,128]{3,2,1,0:T(8,128)} %get-tuple-element.4), channel_id=1, source_target_pairs={{0,16},{16,32},{32,48},{48,64},{64,80},{80,96},{96,112},{112,128},... | collective-permute-start | bytes 221192 | tf_op jit(solution)/shard_map/ppermute | solution.py:22
  11.7 6.4 %collective-permute-start.1 = (f32[9,1,16,128]{3,2,1,0:T(8,128)}, f32[9,1,16,128]{3,2,1,0:T(8,128)}, u32[]{:S(2)}, u32[]{:S(2)}) collective-permute-start(f32[9,1,16,128]{3,2,1,0:T(8,128)} %get-tuple-element.5), channel_id=1, source_target_pairs={{16,0},{32,16},{48,32},{64,48},{80,64},{96,80},{112,96},{128,112},... | collective-permute-start | bytes 221192 | tf_op jit(solution)/shard_map/ppermute | solution.py:23
  19.8 1.5 slice_multiply_fusion.5
  21.7 1.6 slice_multiply_fusion.3
  23.3 3.1 %convolution_bitcast_fusion.5 = f32[8]{0:T(128)} fusion(f32[16,16,128,1]{2,3,1,0:T(1,128)S(1)} %bitcast.474, f32[8,16,16,128]{3,2,1,0:T(8,128)S(1)} %copy-done.1), kind=kOutput, calls=%fused_computation.13 | convolution fusion | flops 3145728 | bytes 1179680 | tf_op jit(solution)/shard_map/aijz,ijz->a/dot_general | solution.py:111
  26.4 1.6 copy.50
  28.0 0.9 pad_maximum_fusion.8
  28.9 3.4 %collective-permute-start.3 = (f32[9,18,1,128]{3,1,2,0:T(8,128)S(1)}, f32[9,18,1,128]{3,1,2,0:T(8,128)S(1)}, u32[]{:S(2)}, u32[]{:S(2)}) collective-permute-start(f32[9,18,1,128]{3,1,2,0:T(8,128)S(1)} %copy.46), channel_id=1, source_target_pairs={{1,0},{2,1},{3,2},{4,3},{5,4},{6,5},{7,6},{8,7},{9,8},{10,9},{11,1... | collective-permute-start | bytes 248840 | tf_op jit(solution)/shard_map/ppermute | solution.py:23
  32.4 6.0 %collective-permute-start.2 = (f32[9,18,1,128]{3,1,2,0:T(8,128)S(1)}, f32[9,18,1,128]{3,1,2,0:T(8,128)S(1)}, u32[]{:S(2)}, u32[]{:S(2)}) collective-permute-start(f32[9,18,1,128]{3,1,2,0:T(8,128)S(1)} %copy.45), channel_id=1, source_target_pairs={{0,1},{1,2},{2,3},{3,4},{4,5},{5,6},{6,7},{7,8},{8,9},{9,10},{10,1... | collective-permute-start | bytes 248840 | tf_op jit(solution)/shard_map/ppermute | solution.py:22
  39.0 1.9 %collective-permute-start.7 = (f32[3,1,8]{2,1,0:T(1,128)}, f32[3,1,8]{2,1,0:T(1,128)}, u32[]{:S(2)}, u32[]{:S(2)}) collective-permute-start(f32[3,1,8]{2,1,0:T(1,128)} %pad_maximum_fusion.11), channel_id=1, source_target_pairs={{1,0},{2,1},{3,2},{4,3},{5,4},{6,5},{7,6},{8,7},{9,8},{10,9},{11,1... | collective-permute-start | bytes 296 | tf_op jit(solution)/shard_map/ppermute | solution.py:23
  41.0 4.9 %collective-permute-start.6 = (f32[3,1,8]{2,1,0:T(1,128)}, f32[3,1,8]{2,1,0:T(1,128)}, u32[]{:S(2)}, u32[]{:S(2)}) collective-permute-start(f32[3,1,8]{2,1,0:T(1,128)} %pad_maximum_fusion.11), channel_id=1, source_target_pairs={{0,1},{1,2},{2,3},{3,4},{4,5},{5,6},{6,7},{7,8},{8,9},{9,10},{10,1... | collective-permute-start | bytes 296 | tf_op jit(solution)/shard_map/ppermute | solution.py:22
  50.6 0.8 fusion.66
  51.4 1.0 fusion.5
  52.6 0.9 fusion.67
  53.4 1.7 %fusion.7 = f32[8,8]{0,1:T(8,128)} fusion(f32[8,16,16,128]{3,0,2,1:T(8,128)} %copy.50, f32[8,16,128]{2,1,0:T(8,128)S(1)} %fusion.67), kind=kOutput, calls=%fused_computation.11 | convolution fusion | flops 1572928 | bytes 131328 | tf_op jit(solution)/shard_map/ajz,jz,bjz->ab/dot_general | solution.py:98
  55.8 1.3 fusion.62
  57.1 2.7 %add_subtract_fusion = f32[8,16,16,128]{3,2,1,0:T(8,128)S(1)} fusion(f32[8,16,16,127]{3,2,1,0:T(8,128)S(1)} %get-tuple-element.9, f32[8,16,16,127]{3,2,1,0:T(8,128)S(1)} %get-tuple-element.8, f32[8,16,15,128]{3,2,1,0:T(8,128)} %get-tuple-element.7, f32[8,16,15,128]{3,2,1,0:T(8,128)} %get-tuple-element.6, f32[8,15,16,128]{3,2,1,0:T(8,128)} %get-tuple-element.11, ...), kind=kLoop, calls=%fused_computation.99 | loop fusion | flops 1835008 | bytes 8241152 | tf_op jit(solution)/shard_map/sub | solution.py:96
  59.8 3.0 %convolution_bitcast_fusion.4 = f32[8,8]{1,0:T(8,128)S(1)} fusion(f32[8,16,16,128]{3,2,1,0:T(8,128)S(1)} %add_subtract_fusion, f32[8,16,16,128]{3,2,1,0:T(8,128)S(1)} %copy-done.1), kind=kOutput, calls=%fused_computation.12 | convolution fusion | flops 25165824 | bytes 2097408 | tf_op jit(solution)/shard_map/aijz,bijz->ab/dot_general | solution.py:97
  66.6 0.8 copy-done.10
  70.3 3.6 %collective-permute-start.9 = (f32[1,1,8]{2,1,0:T(1,128)S(1)}, f32[1,1,8]{2,1,0:T(1,128)S(1)}, u32[]{:S(2)}, u32[]{:S(2)}) collective-permute-start(f32[1,1,8]{2,1,0:T(1,128)S(1)} %bitcast.479), channel_id=1, source_target_pairs={{16,0},{32,16},{48,32},{64,48},{80,64},{96,80},{112,96},{128,112},... | collective-permute-start | bytes 104 | tf_op jit(solution)/shard_map/ppermute | solution.py:23
  73.9 1.9 %collective-permute-start.8 = (f32[1,1,8]{2,1,0:T(1,128)S(1)}, f32[1,1,8]{2,1,0:T(1,128)S(1)}, u32[]{:S(2)}, u32[]{:S(2)}) collective-permute-start(f32[1,1,8]{2,1,0:T(1,128)S(1)} %bitcast.480), channel_id=1, source_target_pairs={{0,16},{16,32},{32,48},{48,64},{64,80},{80,96},{96,112},{112,128},... | collective-permute-start | bytes 104 | tf_op jit(solution)/shard_map/ppermute | solution.py:22
  77.2 4.3 %collective-permute-done.8 = f32[1,1,8]{2,1,0:T(1,128)S(1)} collective-permute-done((f32[1,1,8]{2,1,0:T(1,128)S(1)}, f32[1,1,8]{2,1,0:T(1,128)S(1)}, u32[]{:S(2)}, u32[]{:S(2)}) %collective-permute-start.8) | collective-permute-done | bytes 64 | tf_op jit(solution)/shard_map/ppermute | solution.py:22
  81.6 1.9 %collective-permute-start.11 = (f32[3,1,8]{2,1,0:T(1,128)S(1)}, f32[3,1,8]{2,1,0:T(1,128)S(1)}, u32[]{:S(2)}, u32[]{:S(2)}) collective-permute-start(f32[3,1,8]{2,1,0:T(1,128)S(1)} %pad_maximum_fusion.12), channel_id=1, source_target_pairs={{1,0},{2,1},{3,2},{4,3},{5,4},{6,5},{7,6},{8,7},{9,8},{10,9},{11,1... | collective-permute-start | bytes 296 | tf_op jit(solution)/shard_map/ppermute | solution.py:23
  83.5 4.9 %collective-permute-start.10 = (f32[3,1,8]{2,1,0:T(1,128)S(1)}, f32[3,1,8]{2,1,0:T(1,128)S(1)}, u32[]{:S(2)}, u32[]{:S(2)}) collective-permute-start(f32[3,1,8]{2,1,0:T(1,128)S(1)} %pad_maximum_fusion.12), channel_id=1, source_target_pairs={{0,1},{1,2},{2,3},{3,4},{4,5},{5,6},{6,7},{7,8},{8,9},{9,10},{10,1... | collective-permute-start | bytes 296 | tf_op jit(solution)/shard_map/ppermute | solution.py:22
  89.6 2.4 %collective-permute-start.13 = (f32[1,1,8]{2,1,0:T(1,128)S(1)}, f32[1,1,8]{2,1,0:T(1,128)S(1)}, u32[]{:S(2)}, u32[]{:S(2)}) collective-permute-start(f32[1,1,8]{2,1,0:T(1,128)S(1)} %bitcast.486), channel_id=1, source_target_pairs={{16,0},{32,16},{48,32},{64,48},{80,64},{96,80},{112,96},{128,112},... | collective-permute-start | bytes 104 | tf_op jit(solution)/shard_map/ppermute | solution.py:23
  92.0 2.9 %collective-permute-start.12 = (f32[1,1,8]{2,1,0:T(1,128)S(1)}, f32[1,1,8]{2,1,0:T(1,128)S(1)}, u32[]{:S(2)}, u32[]{:S(2)}) collective-permute-start(f32[1,1,8]{2,1,0:T(1,128)S(1)} %bitcast.487), channel_id=1, source_target_pairs={{0,16},{16,32},{32,48},{48,64},{64,80},{80,96},{96,112},{112,128},... | collective-permute-start | bytes 104 | tf_op jit(solution)/shard_map/ppermute | solution.py:22
  94.9 4.7 %collective-permute-done.12 = f32[1,1,8]{2,1,0:T(1,128)S(1)} collective-permute-done((f32[1,1,8]{2,1,0:T(1,128)S(1)}, f32[1,1,8]{2,1,0:T(1,128)S(1)}, u32[]{:S(2)}, u32[]{:S(2)}) %collective-permute-start.12) | collective-permute-done | bytes 64 | tf_op jit(solution)/shard_map/ppermute | solution.py:22
  99.6 1.9 %collective-permute-start.15 = (f32[3,1,8]{2,1,0:T(1,128)S(1)}, f32[3,1,8]{2,1,0:T(1,128)S(1)}, u32[]{:S(2)}, u32[]{:S(2)}) collective-permute-start(f32[3,1,8]{2,1,0:T(1,128)S(1)} %pad_maximum_fusion.13), channel_id=1, source_target_pairs={{1,0},{2,1},{3,2},{4,3},{5,4},{6,5},{7,6},{8,7},{9,8},{10,9},{11,1... | collective-permute-start | bytes 296 | tf_op jit(solution)/shard_map/ppermute | solution.py:23
  101.5 6.8 %collective-permute-start.14 = (f32[3,1,8]{2,1,0:T(1,128)S(1)}, f32[3,1,8]{2,1,0:T(1,128)S(1)}, u32[]{:S(2)}, u32[]{:S(2)}) collective-permute-start(f32[3,1,8]{2,1,0:T(1,128)S(1)} %pad_maximum_fusion.13), channel_id=1, source_target_pairs={{0,1},{1,2},{2,3},{3,4},{4,5},{5,6},{6,7},{7,8},{8,9},{9,10},{10,1... | collective-permute-start | bytes 296 | tf_op jit(solution)/shard_map/ppermute | solution.py:22
  109.6 1.9 %collective-permute-start.17 = (f32[1,1,8]{2,1,0:T(1,128)S(1)}, f32[1,1,8]{2,1,0:T(1,128)S(1)}, u32[]{:S(2)}, u32[]{:S(2)}) collective-permute-start(f32[1,1,8]{2,1,0:T(1,128)S(1)} %bitcast.489), channel_id=1, source_target_pairs={{16,0},{32,16},{48,32},{64,48},{80,64},{96,80},{112,96},{128,112},... | collective-permute-start | bytes 104 | tf_op jit(solution)/shard_map/ppermute | solution.py:23
  111.5 3.4 %collective-permute-start.16 = (f32[1,1,8]{2,1,0:T(1,128)S(1)}, f32[1,1,8]{2,1,0:T(1,128)S(1)}, u32[]{:S(2)}, u32[]{:S(2)}) collective-permute-start(f32[1,1,8]{2,1,0:T(1,128)S(1)} %bitcast.490), channel_id=1, source_target_pairs={{0,16},{16,32},{32,48},{48,64},{64,80},{80,96},{96,112},{112,128},... | collective-permute-start | bytes 104 | tf_op jit(solution)/shard_map/ppermute | solution.py:22
  114.9 4.2 %collective-permute-done.16 = f32[1,1,8]{2,1,0:T(1,128)S(1)} collective-permute-done((f32[1,1,8]{2,1,0:T(1,128)S(1)}, f32[1,1,8]{2,1,0:T(1,128)S(1)}, u32[]{:S(2)}, u32[]{:S(2)}) %collective-permute-start.16) | collective-permute-done | bytes 64 | tf_op jit(solution)/shard_map/ppermute | solution.py:22
  119.2 1.9 %collective-permute-start.19 = (f32[3,1,8]{2,1,0:T(1,128)S(1)}, f32[3,1,8]{2,1,0:T(1,128)S(1)}, u32[]{:S(2)}, u32[]{:S(2)}) collective-permute-start(f32[3,1,8]{2,1,0:T(1,128)S(1)} %pad_maximum_fusion.14), channel_id=1, source_target_pairs={{1,0},{2,1},{3,2},{4,3},{5,4},{6,5},{7,6},{8,7},{9,8},{10,9},{11,1... | collective-permute-start | bytes 296 | tf_op jit(solution)/shard_map/ppermute | solution.py:23
  121.1 6.5 %collective-permute-start.18 = (f32[3,1,8]{2,1,0:T(1,128)S(1)}, f32[3,1,8]{2,1,0:T(1,128)S(1)}, u32[]{:S(2)}, u32[]{:S(2)}) collective-permute-start(f32[3,1,8]{2,1,0:T(1,128)S(1)} %pad_maximum_fusion.14), channel_id=1, source_target_pairs={{0,1},{1,2},{2,3},{3,4},{4,5},{5,6},{6,7},{7,8},{8,9},{9,10},{10,1... | collective-permute-start | bytes 296 | tf_op jit(solution)/shard_map/ppermute | solution.py:22
  128.9 1.9 %collective-permute-start.21 = (f32[1,1,8]{2,1,0:T(1,128)S(1)}, f32[1,1,8]{2,1,0:T(1,128)S(1)}, u32[]{:S(2)}, u32[]{:S(2)}) collective-permute-start(f32[1,1,8]{2,1,0:T(1,128)S(1)} %bitcast.492), channel_id=1, source_target_pairs={{16,0},{32,16},{48,32},{64,48},{80,64},{96,80},{112,96},{128,112},... | collective-permute-start | bytes 104 | tf_op jit(solution)/shard_map/ppermute | solution.py:23
  130.8 3.4 %collective-permute-start.20 = (f32[1,1,8]{2,1,0:T(1,128)S(1)}, f32[1,1,8]{2,1,0:T(1,128)S(1)}, u32[]{:S(2)}, u32[]{:S(2)}) collective-permute-start(f32[1,1,8]{2,1,0:T(1,128)S(1)} %bitcast.493), channel_id=1, source_target_pairs={{0,16},{16,32},{32,48},{48,64},{64,80},{80,96},{96,112},{112,128},... | collective-permute-start | bytes 104 | tf_op jit(solution)/shard_map/ppermute | solution.py:22
  134.2 4.2 %collective-permute-done.20 = f32[1,1,8]{2,1,0:T(1,128)S(1)} collective-permute-done((f32[1,1,8]{2,1,0:T(1,128)S(1)}, f32[1,1,8]{2,1,0:T(1,128)S(1)}, u32[]{:S(2)}, u32[]{:S(2)}) %collective-permute-start.20) | collective-permute-done | bytes 64 | tf_op jit(solution)/shard_map/ppermute | solution.py:22
  138.4 1.9 %collective-permute-start.23 = (f32[3,1,8]{2,1,0:T(1,128)S(1)}, f32[3,1,8]{2,1,0:T(1,128)S(1)}, u32[]{:S(2)}, u32[]{:S(2)}) collective-permute-start(f32[3,1,8]{2,1,0:T(1,128)S(1)} %pad_maximum_fusion.15), channel_id=1, source_target_pairs={{1,0},{2,1},{3,2},{4,3},{5,4},{6,5},{7,6},{8,7},{9,8},{10,9},{11,1... | collective-permute-start | bytes 296 | tf_op jit(solution)/shard_map/ppermute | solution.py:23
  140.3 6.5 %collective-permute-start.22 = (f32[3,1,8]{2,1,0:T(1,128)S(1)}, f32[3,1,8]{2,1,0:T(1,128)S(1)}, u32[]{:S(2)}, u32[]{:S(2)}) collective-permute-start(f32[3,1,8]{2,1,0:T(1,128)S(1)} %pad_maximum_fusion.15), channel_id=1, source_target_pairs={{0,1},{1,2},{2,3},{3,4},{4,5},{5,6},{6,7},{7,8},{8,9},{9,10},{10,1... | collective-permute-start | bytes 296 | tf_op jit(solution)/shard_map/ppermute | solution.py:22
  148.1 1.9 %collective-permute-start.25 = (f32[1,1,8]{2,1,0:T(1,128)S(1)}, f32[1,1,8]{2,1,0:T(1,128)S(1)}, u32[]{:S(2)}, u32[]{:S(2)}) collective-permute-start(f32[1,1,8]{2,1,0:T(1,128)S(1)} %bitcast.483), channel_id=1, source_target_pairs={{16,0},{32,16},{48,32},{64,48},{80,64},{96,80},{112,96},{128,112},... | collective-permute-start | bytes 104 | tf_op jit(solution)/shard_map/ppermute | solution.py:23
  150.1 3.4 %collective-permute-start.24 = (f32[1,1,8]{2,1,0:T(1,128)S(1)}, f32[1,1,8]{2,1,0:T(1,128)S(1)}, u32[]{:S(2)}, u32[]{:S(2)}) collective-permute-start(f32[1,1,8]{2,1,0:T(1,128)S(1)} %bitcast.484), channel_id=1, source_target_pairs={{0,16},{16,32},{32,48},{48,64},{64,80},{80,96},{96,112},{112,128},... | collective-permute-start | bytes 104 | tf_op jit(solution)/shard_map/ppermute | solution.py:22
  153.4 4.2 %collective-permute-done.24 = f32[1,1,8]{2,1,0:T(1,128)S(1)} collective-permute-done((f32[1,1,8]{2,1,0:T(1,128)S(1)}, f32[1,1,8]{2,1,0:T(1,128)S(1)}, u32[]{:S(2)}, u32[]{:S(2)}) %collective-permute-start.24) | collective-permute-done | bytes 64 | tf_op jit(solution)/shard_map/ppermute | solution.py:22
  157.7 1.9 %collective-permute-start.27 = (f32[3,1,8]{2,1,0:T(1,128)S(1)}, f32[3,1,8]{2,1,0:T(1,128)S(1)}, u32[]{:S(2)}, u32[]{:S(2)}) collective-permute-start(f32[3,1,8]{2,1,0:T(1,128)S(1)} %pad_maximum_fusion.16), channel_id=1, source_target_pairs={{1,0},{2,1},{3,2},{4,3},{5,4},{6,5},{7,6},{8,7},{9,8},{10,9},{11,1... | collective-permute-start | bytes 296 | tf_op jit(solution)/shard_map/ppermute | solution.py:23
  159.6 6.5 %collective-permute-start.26 = (f32[3,1,8]{2,1,0:T(1,128)S(1)}, f32[3,1,8]{2,1,0:T(1,128)S(1)}, u32[]{:S(2)}, u32[]{:S(2)}) collective-permute-start(f32[3,1,8]{2,1,0:T(1,128)S(1)} %pad_maximum_fusion.16), channel_id=1, source_target_pairs={{0,1},{1,2},{2,3},{3,4},{4,5},{5,6},{6,7},{7,8},{8,9},{9,10},{10,1... | collective-permute-start | bytes 296 | tf_op jit(solution)/shard_map/ppermute | solution.py:22
  (148 shorter events, 22.7 us)
Async XLA Ops:
  0.6 22.7 %copy-start = (f32[16,16,128]{2,1,0:T(8,128)S(1)}, f32[16,16,128]{2,1,0:T(8,128)}, u32[]{:S(2)}) copy-start(f32[16,16,128]{2,1,0:T(8,128)} %param.5) | copy-start | bytes 393220
  0.6 17.5 %copy-start.1 = (f32[8,16,16,128]{3,2,1,0:T(8,128)S(1)}, f32[8,16,16,128]{3,2,1,0:T(8,128)}, u32[]{:S(2)}) copy-start(f32[8,16,16,128]{3,2,1,0:T(8,128)} %param.4) | copy-start | bytes 3145732
  0.7 37.7 %collective-permute-start.5 = (f32[1,1,8]{2,1,0:T(1,128)S(1)}, f32[1,1,8]{2,1,0:T(1,128)S(1)}, u32[]{:S(2)}, u32[]{:S(2)}) collective-permute-start(f32[1,1,8]{2,1,0:T(1,128)S(1)} %broadcast.95), channel_id=1, source_target_pairs={{16,0},{32,16},{48,32},{64,48},{80,64},{96,80},{112,96},{128,112},... | collective-permute-start | bytes 104 | tf_op jit(solution)/shard_map/ppermute | solution.py:23
  5.1 33.3 %collective-permute-start.4 = (f32[1,1,8]{2,1,0:T(1,128)S(1)}, f32[1,1,8]{2,1,0:T(1,128)S(1)}, u32[]{:S(2)}, u32[]{:S(2)}) collective-permute-start(f32[1,1,8]{2,1,0:T(1,128)S(1)} %broadcast.95), channel_id=1, source_target_pairs={{0,16},{16,32},{32,48},{48,64},{64,80},{80,96},{96,112},{112,128},... | collective-permute-start | bytes 104 | tf_op jit(solution)/shard_map/ppermute | solution.py:22
  9.5 18.4 %collective-permute-start = (f32[9,1,16,128]{3,2,1,0:T(8,128)}, f32[9,1,16,128]{3,2,1,0:T(8,128)}, u32[]{:S(2)}, u32[]{:S(2)}) collective-permute-start(f32[9,1,16,128]{3,2,1,0:T(8,128)} %get-tuple-element.4), channel_id=1, source_target_pairs={{0,16},{16,32},{32,48},{48,64},{64,80},{80,96},{96,112},{112,128},... | collective-permute-start | bytes 221192 | tf_op jit(solution)/shard_map/ppermute | solution.py:22
  11.7 16.2 %collective-permute-start.1 = (f32[9,1,16,128]{3,2,1,0:T(8,128)}, f32[9,1,16,128]{3,2,1,0:T(8,128)}, u32[]{:S(2)}, u32[]{:S(2)}) collective-permute-start(f32[9,1,16,128]{3,2,1,0:T(8,128)} %get-tuple-element.5), channel_id=1, source_target_pairs={{16,0},{32,16},{48,32},{64,48},{80,64},{96,80},{112,96},{128,112},... | collective-permute-start | bytes 221192 | tf_op jit(solution)/shard_map/ppermute | solution.py:23
  18.9 0.9 copy-start.6
  19.0 2.3 %copy-start.2 = (f32[16,16,127]{2,1,0:T(8,128)}, f32[16,16,127]{2,1,0:T(8,128)S(1)}, u32[]{:S(2)}) copy-start(f32[16,16,127]{2,1,0:T(8,128)S(1)} %fusion.58) | copy-start | bytes 390148
  19.1 2.6 %copy-start.4 = (f32[16,15,128]{2,1,0:T(8,128)}, f32[16,15,128]{2,1,0:T(8,128)S(1)}, u32[]{:S(2)}) copy-start(f32[16,15,128]{2,1,0:T(8,128)S(1)} %fusion.59) | copy-start | bytes 368644
  28.9 16.9 %collective-permute-start.3 = (f32[9,18,1,128]{3,1,2,0:T(8,128)S(1)}, f32[9,18,1,128]{3,1,2,0:T(8,128)S(1)}, u32[]{:S(2)}, u32[]{:S(2)}) collective-permute-start(f32[9,18,1,128]{3,1,2,0:T(8,128)S(1)} %copy.46), channel_id=1, source_target_pairs={{1,0},{2,1},{3,2},{4,3},{5,4},{6,5},{7,6},{8,7},{9,8},{10,9},{11,1... | collective-permute-start | bytes 248840 | tf_op jit(solution)/shard_map/ppermute | solution.py:23
  32.4 14.1 %collective-permute-start.2 = (f32[9,18,1,128]{3,1,2,0:T(8,128)S(1)}, f32[9,18,1,128]{3,1,2,0:T(8,128)S(1)}, u32[]{:S(2)}, u32[]{:S(2)}) collective-permute-start(f32[9,18,1,128]{3,1,2,0:T(8,128)S(1)} %copy.45), channel_id=1, source_target_pairs={{0,1},{1,2},{2,3},{3,4},{4,5},{5,6},{6,7},{7,8},{8,9},{9,10},{10,1... | collective-permute-start | bytes 248840 | tf_op jit(solution)/shard_map/ppermute | solution.py:22
  39.0 29.2 %collective-permute-start.7 = (f32[3,1,8]{2,1,0:T(1,128)}, f32[3,1,8]{2,1,0:T(1,128)}, u32[]{:S(2)}, u32[]{:S(2)}) collective-permute-start(f32[3,1,8]{2,1,0:T(1,128)} %pad_maximum_fusion.11), channel_id=1, source_target_pairs={{1,0},{2,1},{3,2},{4,3},{5,4},{6,5},{7,6},{8,7},{9,8},{10,9},{11,1... | collective-permute-start | bytes 296 | tf_op jit(solution)/shard_map/ppermute | solution.py:23
  41.0 28.1 %collective-permute-start.6 = (f32[3,1,8]{2,1,0:T(1,128)}, f32[3,1,8]{2,1,0:T(1,128)}, u32[]{:S(2)}, u32[]{:S(2)}) collective-permute-start(f32[3,1,8]{2,1,0:T(1,128)} %pad_maximum_fusion.11), channel_id=1, source_target_pairs={{0,1},{1,2},{2,3},{3,4},{4,5},{5,6},{6,7},{7,8},{8,9},{9,10},{10,1... | collective-permute-start | bytes 296 | tf_op jit(solution)/shard_map/ppermute | solution.py:22
  45.8 0.6 copy-start.8
  47.3 0.7 copy-start.7
  48.1 0.8 copy-start.11
  50.6 0.9 copy-start.13
  50.6 1.9 %copy-start.14 = (f32[1,16,128]{2,1,0:T(8,128)}, f32[1,16,128]{2,1,0:T(8,128)S(1)}, u32[]{:S(2)}) copy-start(f32[1,16,128]{2,1,0:T(8,128)S(1)} %get-tuple-element.17) | copy-start | bytes 24580
  52.5 3.3 %copy-start.3 = (f32[16,16,127]{2,1,0:T(8,128)S(1)}, f32[16,16,127]{2,1,0:T(8,128)}, u32[]{:S(2)}) copy-start(f32[16,16,127]{2,1,0:T(8,128)} %copy-done.2) | copy-start | bytes 390148
  52.5 3.3 %copy-start.5 = (f32[16,15,128]{2,1,0:T(8,128)S(1)}, f32[16,15,128]{2,1,0:T(8,128)}, u32[]{:S(2)}) copy-start(f32[16,15,128]{2,1,0:T(8,128)} %copy-done.4) | copy-start | bytes 368644
  59.8 6.7 %copy-start.9 = (f32[9,18,1,128]{3,1,2,0:T(8,128)S(1)}, f32[9,18,1,128]{3,1,2,0:T(8,128)}, u32[]{:S(2)}) copy-start(f32[9,18,1,128]{3,1,2,0:T(8,128)} %copy-done.8) | copy-start | bytes 248836
  65.8 0.6 copy-start.18
  66.6 0.8 copy-start.10
  68.2 0.8 copy-start.15
  69.1 0.8 copy-start.23
  70.3 7.0 %collective-permute-start.9 = (f32[1,1,8]{2,1,0:T(1,128)S(1)}, f32[1,1,8]{2,1,0:T(1,128)S(1)}, u32[]{:S(2)}, u32[]{:S(2)}) collective-permute-start(f32[1,1,8]{2,1,0:T(1,128)S(1)} %bitcast.479), channel_id=1, source_target_pairs={{16,0},{32,16},{48,32},{64,48},{80,64},{96,80},{112,96},{128,112},... | collective-permute-start | bytes 104 | tf_op jit(solution)/shard_map/ppermute | solution.py:23
  73.9 7.6 %collective-permute-start.8 = (f32[1,1,8]{2,1,0:T(1,128)S(1)}, f32[1,1,8]{2,1,0:T(1,128)S(1)}, u32[]{:S(2)}, u32[]{:S(2)}) collective-permute-start(f32[1,1,8]{2,1,0:T(1,128)S(1)} %bitcast.480), channel_id=1, source_target_pairs={{0,16},{16,32},{32,48},{48,64},{64,80},{80,96},{96,112},{112,128},... | collective-permute-start | bytes 104 | tf_op jit(solution)/shard_map/ppermute | solution.py:22
  75.9 0.7 copy-start.17
  76.6 0.7 copy-start.16
  77.2 12.3 %copy-start.21 = (f32[5,8,8]{2,1,0:T(8,128)}, f32[5,8,8]{2,1,0:T(8,128)S(1)}, u32[]{:S(2)}) copy-start(f32[5,8,8]{2,1,0:T(8,128)S(1)} %constant_dynamic-update-slice_fusion) | copy-start | bytes 3844
  81.6 6.9 %collective-permute-start.11 = (f32[3,1,8]{2,1,0:T(1,128)S(1)}, f32[3,1,8]{2,1,0:T(1,128)S(1)}, u32[]{:S(2)}, u32[]{:S(2)}) collective-permute-start(f32[3,1,8]{2,1,0:T(1,128)S(1)} %pad_maximum_fusion.12), channel_id=1, source_target_pairs={{1,0},{2,1},{3,2},{4,3},{5,4},{6,5},{7,6},{8,7},{9,8},{10,9},{11,1... | collective-permute-start | bytes 296 | tf_op jit(solution)/shard_map/ppermute | solution.py:23
  83.5 5.6 %collective-permute-start.10 = (f32[3,1,8]{2,1,0:T(1,128)S(1)}, f32[3,1,8]{2,1,0:T(1,128)S(1)}, u32[]{:S(2)}, u32[]{:S(2)}) collective-permute-start(f32[3,1,8]{2,1,0:T(1,128)S(1)} %pad_maximum_fusion.12), channel_id=1, source_target_pairs={{0,1},{1,2},{2,3},{3,4},{4,5},{5,6},{6,7},{7,8},{8,9},{9,10},{10,1... | collective-permute-start | bytes 296 | tf_op jit(solution)/shard_map/ppermute | solution.py:22
  89.6 5.3 %collective-permute-start.13 = (f32[1,1,8]{2,1,0:T(1,128)S(1)}, f32[1,1,8]{2,1,0:T(1,128)S(1)}, u32[]{:S(2)}, u32[]{:S(2)}) collective-permute-start(f32[1,1,8]{2,1,0:T(1,128)S(1)} %bitcast.486), channel_id=1, source_target_pairs={{16,0},{32,16},{48,32},{64,48},{80,64},{96,80},{112,96},{128,112},... | collective-permute-start | bytes 104 | tf_op jit(solution)/shard_map/ppermute | solution.py:23
  92.0 7.6 %collective-permute-start.12 = (f32[1,1,8]{2,1,0:T(1,128)S(1)}, f32[1,1,8]{2,1,0:T(1,128)S(1)}, u32[]{:S(2)}, u32[]{:S(2)}) collective-permute-start(f32[1,1,8]{2,1,0:T(1,128)S(1)} %bitcast.487), channel_id=1, source_target_pairs={{0,16},{16,32},{32,48},{48,64},{64,80},{80,96},{96,112},{112,128},... | collective-permute-start | bytes 104 | tf_op jit(solution)/shard_map/ppermute | solution.py:22
  99.6 8.9 %collective-permute-start.15 = (f32[3,1,8]{2,1,0:T(1,128)S(1)}, f32[3,1,8]{2,1,0:T(1,128)S(1)}, u32[]{:S(2)}, u32[]{:S(2)}) collective-permute-start(f32[3,1,8]{2,1,0:T(1,128)S(1)} %pad_maximum_fusion.13), channel_id=1, source_target_pairs={{1,0},{2,1},{3,2},{4,3},{5,4},{6,5},{7,6},{8,7},{9,8},{10,9},{11,1... | collective-permute-start | bytes 296 | tf_op jit(solution)/shard_map/ppermute | solution.py:23
  101.5 7.5 %collective-permute-start.14 = (f32[3,1,8]{2,1,0:T(1,128)S(1)}, f32[3,1,8]{2,1,0:T(1,128)S(1)}, u32[]{:S(2)}, u32[]{:S(2)}) collective-permute-start(f32[3,1,8]{2,1,0:T(1,128)S(1)} %pad_maximum_fusion.13), channel_id=1, source_target_pairs={{0,1},{1,2},{2,3},{3,4},{4,5},{5,6},{6,7},{7,8},{8,9},{9,10},{10,1... | collective-permute-start | bytes 296 | tf_op jit(solution)/shard_map/ppermute | solution.py:22
  109.6 5.3 %collective-permute-start.17 = (f32[1,1,8]{2,1,0:T(1,128)S(1)}, f32[1,1,8]{2,1,0:T(1,128)S(1)}, u32[]{:S(2)}, u32[]{:S(2)}) collective-permute-start(f32[1,1,8]{2,1,0:T(1,128)S(1)} %bitcast.489), channel_id=1, source_target_pairs={{16,0},{32,16},{48,32},{64,48},{80,64},{96,80},{112,96},{128,112},... | collective-permute-start | bytes 104 | tf_op jit(solution)/shard_map/ppermute | solution.py:23
  111.5 7.6 %collective-permute-start.16 = (f32[1,1,8]{2,1,0:T(1,128)S(1)}, f32[1,1,8]{2,1,0:T(1,128)S(1)}, u32[]{:S(2)}, u32[]{:S(2)}) collective-permute-start(f32[1,1,8]{2,1,0:T(1,128)S(1)} %bitcast.490), channel_id=1, source_target_pairs={{0,16},{16,32},{32,48},{48,64},{64,80},{80,96},{96,112},{112,128},... | collective-permute-start | bytes 104 | tf_op jit(solution)/shard_map/ppermute | solution.py:22
  119.2 8.6 %collective-permute-start.19 = (f32[3,1,8]{2,1,0:T(1,128)S(1)}, f32[3,1,8]{2,1,0:T(1,128)S(1)}, u32[]{:S(2)}, u32[]{:S(2)}) collective-permute-start(f32[3,1,8]{2,1,0:T(1,128)S(1)} %pad_maximum_fusion.14), channel_id=1, source_target_pairs={{1,0},{2,1},{3,2},{4,3},{5,4},{6,5},{7,6},{8,7},{9,8},{10,9},{11,1... | collective-permute-start | bytes 296 | tf_op jit(solution)/shard_map/ppermute | solution.py:23
  121.1 7.3 %collective-permute-start.18 = (f32[3,1,8]{2,1,0:T(1,128)S(1)}, f32[3,1,8]{2,1,0:T(1,128)S(1)}, u32[]{:S(2)}, u32[]{:S(2)}) collective-permute-start(f32[3,1,8]{2,1,0:T(1,128)S(1)} %pad_maximum_fusion.14), channel_id=1, source_target_pairs={{0,1},{1,2},{2,3},{3,4},{4,5},{5,6},{6,7},{7,8},{8,9},{9,10},{10,1... | collective-permute-start | bytes 296 | tf_op jit(solution)/shard_map/ppermute | solution.py:22
  128.9 5.3 %collective-permute-start.21 = (f32[1,1,8]{2,1,0:T(1,128)S(1)}, f32[1,1,8]{2,1,0:T(1,128)S(1)}, u32[]{:S(2)}, u32[]{:S(2)}) collective-permute-start(f32[1,1,8]{2,1,0:T(1,128)S(1)} %bitcast.492), channel_id=1, source_target_pairs={{16,0},{32,16},{48,32},{64,48},{80,64},{96,80},{112,96},{128,112},... | collective-permute-start | bytes 104 | tf_op jit(solution)/shard_map/ppermute | solution.py:23
  130.8 7.6 %collective-permute-start.20 = (f32[1,1,8]{2,1,0:T(1,128)S(1)}, f32[1,1,8]{2,1,0:T(1,128)S(1)}, u32[]{:S(2)}, u32[]{:S(2)}) collective-permute-start(f32[1,1,8]{2,1,0:T(1,128)S(1)} %bitcast.493), channel_id=1, source_target_pairs={{0,16},{16,32},{32,48},{48,64},{64,80},{80,96},{96,112},{112,128},... | collective-permute-start | bytes 104 | tf_op jit(solution)/shard_map/ppermute | solution.py:22
  138.4 8.6 %collective-permute-start.23 = (f32[3,1,8]{2,1,0:T(1,128)S(1)}, f32[3,1,8]{2,1,0:T(1,128)S(1)}, u32[]{:S(2)}, u32[]{:S(2)}) collective-permute-start(f32[3,1,8]{2,1,0:T(1,128)S(1)} %pad_maximum_fusion.15), channel_id=1, source_target_pairs={{1,0},{2,1},{3,2},{4,3},{5,4},{6,5},{7,6},{8,7},{9,8},{10,9},{11,1... | collective-permute-start | bytes 296 | tf_op jit(solution)/shard_map/ppermute | solution.py:23
  140.3 7.3 %collective-permute-start.22 = (f32[3,1,8]{2,1,0:T(1,128)S(1)}, f32[3,1,8]{2,1,0:T(1,128)S(1)}, u32[]{:S(2)}, u32[]{:S(2)}) collective-permute-start(f32[3,1,8]{2,1,0:T(1,128)S(1)} %pad_maximum_fusion.15), channel_id=1, source_target_pairs={{0,1},{1,2},{2,3},{3,4},{4,5},{5,6},{6,7},{7,8},{8,9},{9,10},{10,1... | collective-permute-start | bytes 296 | tf_op jit(solution)/shard_map/ppermute | solution.py:22
  148.1 5.3 %collective-permute-start.25 = (f32[1,1,8]{2,1,0:T(1,128)S(1)}, f32[1,1,8]{2,1,0:T(1,128)S(1)}, u32[]{:S(2)}, u32[]{:S(2)}) collective-permute-start(f32[1,1,8]{2,1,0:T(1,128)S(1)} %bitcast.483), channel_id=1, source_target_pairs={{16,0},{32,16},{48,32},{64,48},{80,64},{96,80},{112,96},{128,112},... | collective-permute-start | bytes 104 | tf_op jit(solution)/shard_map/ppermute | solution.py:23
  150.1 7.6 %collective-permute-start.24 = (f32[1,1,8]{2,1,0:T(1,128)S(1)}, f32[1,1,8]{2,1,0:T(1,128)S(1)}, u32[]{:S(2)}, u32[]{:S(2)}) collective-permute-start(f32[1,1,8]{2,1,0:T(1,128)S(1)} %bitcast.484), channel_id=1, source_target_pairs={{0,16},{16,32},{32,48},{48,64},{64,80},{80,96},{96,112},{112,128},... | collective-permute-start | bytes 104 | tf_op jit(solution)/shard_map/ppermute | solution.py:22
  157.7 8.6 %collective-permute-start.27 = (f32[3,1,8]{2,1,0:T(1,128)S(1)}, f32[3,1,8]{2,1,0:T(1,128)S(1)}, u32[]{:S(2)}, u32[]{:S(2)}) collective-permute-start(f32[3,1,8]{2,1,0:T(1,128)S(1)} %pad_maximum_fusion.16), channel_id=1, source_target_pairs={{1,0},{2,1},{3,2},{4,3},{5,4},{6,5},{7,6},{8,7},{9,8},{10,9},{11,1... | collective-permute-start | bytes 296 | tf_op jit(solution)/shard_map/ppermute | solution.py:23
  159.6 7.3 %collective-permute-start.26 = (f32[3,1,8]{2,1,0:T(1,128)S(1)}, f32[3,1,8]{2,1,0:T(1,128)S(1)}, u32[]{:S(2)}, u32[]{:S(2)}) collective-permute-start(f32[3,1,8]{2,1,0:T(1,128)S(1)} %pad_maximum_fusion.16), channel_id=1, source_target_pairs={{0,1},{1,2},{2,3},{3,4},{4,5},{5,6},{6,7},{7,8},{8,9},{9,10},{10,1... | collective-permute-start | bytes 296 | tf_op jit(solution)/shard_map/ppermute | solution.py:22
  (4 other events, 2.4 us)
where the time goes:
time: 169 us; the launch traced here: 168 us
  starting transfers between devices  98.7 us (58%)
  waiting for transfers between devices  24 us (14%)
  other arithmetic  17.6 us (10%)
  matrix products  16.2 us (10%)
  local copies, waits for them, and re-layouts  10 us (6%)
    ppermute x14, starting transfers between devices, extended(): before = lax.ppermute(last, axis, up)  61.2 us
    ppermute x14, starting transfers between devices, extended(): after = lax.ppermute(first, axis, down)  37.5 us
    ppermute x14, waiting for transfers between devices, extended(): before = lax.ppermute(last, axis, up)  24 us
    unnamed x53, local copies, waits for them, and re-layouts  6.74 us
    dot_general x30, matrix products, product_of(): jnp.einsum('...ab,...b->...a', blocks[..., index, :, :], vector, precisio...  5.19 us
  transfers between devices with their start and end apart: 28, of which 10 were waited for; matrix products, arithmetic and copies ran while one was open for 20% of the time, Pallas kernels for 0%

commit v1 on v0

v1 whole, which is shorter than its diff:
```python
import jax
import jax.numpy as jnp
from jax import lax
from jax.experimental import pallas as pl
from jax.experimental.pallas import tpu as pltpu
from jax.sharding import PartitionSpec as P

NVEC = 8
ITERS = 6
SIGMA = 0.05
OMEGA = 0.6
HIGH = lax.Precision.HIGHEST

SELF, XLO, XLO_T, YLO, YLO_T, X_BELOW, Y_BELOW, RHS, WORDS = (0, 64, 128, 192, 256, 320, 384, 448, 512)
WINDOW = 16
PARAMS = pltpu.CompilerParams(vmem_limit_bytes=32 * 1024 * 1024)


def viscosity(rate):
    return lax.rsqrt(rate) + 0.5 * (1.0 - jnp.exp(-10.0 * rate)) / rate


def fold(tiles):
    row = lax.broadcasted_iota(jnp.int32, tiles[0].shape, 0)
    for half in (4, 2, 1):
        low = (row & half) == 0
        count = len(tiles) // 2
        tiles = [
            jnp.where(
                low,
                tiles[i] + pltpu.roll(tiles[i], 8 - half, 0),
                tiles[i + count] + pltpu.roll(tiles[i + count], half, 0),
            )
            for i in range(count)
        ]
    return tiles[0]


def halves(x):
    return x[:8] + x[8:]


def self_kernel(rate_ref, vec_ref, res_ref, out_ref, visc_ref, acc_ref, rhs_ref):
    at_top_x = lax.axis_index("sx") == lax.axis_size("sx") - 1
    at_top_y = lax.axis_index("sy") == lax.axis_size("sy") - 1
    visc_ref[...] = viscosity(rate_ref[...])
    acc_ref[...] = jnp.zeros_like(acc_ref)
    rhs_ref[...] = jnp.zeros_like(rhs_ref)
    cx, cy, cz = rate_ref.shape
    row = lax.broadcasted_iota(jnp.int32, (cy, cz), 0)
    lane = lax.broadcasted_iota(jnp.int32, (cy, cz), 1)
    top_x = jnp.where(at_top_x, 1.0, 0.5)
    top_y = jnp.where(at_top_y, 1.0, 0.5)

    @pl.loop(0, cx)
    def _(i):
        visc = visc_ref[i]
        after = visc_ref[jnp.minimum(i + 1, cx - 1)]
        before = visc_ref[jnp.maximum(i - 1, 0)]
        inner = i < cx - 1
        face_x = jnp.where(inner, 0.5 * (visc + after), 0.0)
        high_x = jnp.where(inner, face_x, top_x * visc)
        low_x = jnp.where(i > 0, 0.5 * (visc + before), 0.5 * visc)
        mean_y = 0.5 * (visc + pltpu.roll(visc, cy - 1, 0))
        face_y = jnp.where(row < cy - 1, mean_y, 0.0)
        high_y = jnp.where(row < cy - 1, mean_y, top_y * visc)
        low_y = jnp.where(row > 0, pltpu.roll(mean_y, 1, 0), 0.5 * visc)
        mean_z = 0.5 * (visc + pltpu.roll(visc, cz - 1, 1))
        face_z = jnp.where(lane < cz - 1, mean_z, 0.0)
        high_z = jnp.where(lane < cz - 1, mean_z, visc)
        low_z = jnp.where(lane > 0, pltpu.roll(mean_z, 1, 1), visc)
        weight = 0.5 * (SIGMA + (low_x + high_x) + (low_y + high_y) + (low_z + high_z))
        res = res_ref[i]
        following = jnp.minimum(i + 1, cx - 1)
        vectors = [vec_ref[a, i] for a in range(NVEC)]
        for a in range(NVEC):
            rhs_ref[a] += halves(vectors[a] * res)
        for b in range(NVEC):
            v = vectors[b]
            image = (
                weight * v
                - face_x * vec_ref[b, following]
                - face_y * pltpu.roll(v, cy - 1, 0)
                - face_z * pltpu.roll(v, cz - 1, 1)
            )
            for a in range(NVEC):
                acc_ref[b * NVEC + a] += halves(vectors[a] * image)

    for b in range(NVEC):
        out_ref[pl.ds(b * NVEC, NVEC), :] = fold(
            [acc_ref[b * NVEC + a] + acc_ref[a * NVEC + b] for a in range(NVEC)]
        )
    out_ref[pl.ds(NVEC * NVEC, NVEC), :] = fold([rhs_ref[a] for a in range(NVEC)])


def face_rows(axis, own, own_rate, below, rows_ref, lo, lo_t, beneath):
    inner = lax.axis_index(axis) > 0
    visc = viscosity(own_rate)
    visc_below = viscosity(jnp.where(inner, below[NVEC], 1.0))
    coupling = jnp.where(inner, -0.5 * (visc + visc_below), 0.0)
    beside = 0.5 * jnp.where(inner, visc_below, visc)
    shared = jnp.where(inner, 0.5 * visc, 0.0)
    first = [own[a] for a in range(NVEC)]
    last = [below[a] for a in range(NVEC)]
    coupled = [coupling * last[b] for b in range(NVEC)]
    cross = [[halves(first[a] * coupled[b]) for a in range(NVEC)] for b in range(NVEC)]
    for b in range(NVEC):
        rows_ref[pl.ds(lo + b * NVEC, NVEC), :] = fold(cross[b])
        rows_ref[pl.ds(lo_t + b * NVEC, NVEC), :] = fold([cross[a][b] for a in range(NVEC)])
    for b in range(NVEC):
        mine = beside * first[b]
        rows_ref[pl.ds(SELF + b * NVEC, NVEC), :] += fold([halves(first[a] * mine) for a in range(NVEC)])
        theirs = shared * last[b]
        rows_ref[pl.ds(beneath + b * NVEC, NVEC), :] = fold([halves(last[a] * theirs) for a in range(NVEC)])


def face_kernel(self_ref, first_x_ref, first_y_ref, below_x_ref, below_y_ref, out_ref, rows_ref):
    rows_ref[pl.ds(SELF, 64), :] = self_ref[pl.ds(0, 64), :]
    rows_ref[pl.ds(RHS, NVEC), :] = self_ref[pl.ds(64, NVEC), :]
    rows_ref[pl.ds(RHS + NVEC, WORDS - RHS - NVEC), :] = jnp.zeros((WORDS - RHS - NVEC, 128), jnp.float32)
    face_rows("sx", first_x_ref, first_x_ref[NVEC], below_x_ref, rows_ref, XLO, XLO_T, X_BELOW)
    face_rows("sy", first_y_ref, first_y_ref[NVEC], below_y_ref, rows_ref, YLO, YLO_T, Y_BELOW)
    message = jnp.sum(rows_ref[...].T, axis=0, keepdims=True)
    out_ref[...] = jnp.broadcast_to(message[None], out_ref.shape)


def solve_kernel(got_ref, blocks_ref, coarse_ref, table_ref):
    count_y, window, words = got_ref.shape
    lanes = count_y * window
    index_x, index_y = lax.axis_index("sx"), lax.axis_index("sy")
    count_x = lax.axis_size("sx")
    place = index_x - window_start(index_x, count_x, window)
    table_ref[...] = got_ref[...].reshape(lanes, words).T
    lane = lax.broadcasted_iota(jnp.int32, (1, lanes), 1)
    has_x = lane % window < window - 1
    has_y = lane < lanes - window

    def columns(base):
        return [table_ref[pl.ds(base + b * NVEC, NVEC), :] for b in range(NVEC)]

    def from_x(value):
        return jnp.where(has_x, pltpu.roll(value, lanes - 1, 1), 0.0)

    def from_y(value):
        return jnp.where(has_y, pltpu.roll(value, lanes - window, 1), 0.0)

    def product(matrix, vector):
        terms = [matrix[b] * vector[b : b + 1] for b in range(NVEC)]
        while len(terms) > 1:
            terms = [terms[i] + terms[i + 1] for i in range(0, len(terms), 2)]
        return terms[0]

    own = [
        s + from_x(x) + from_y(y)
        for s, x, y in zip(columns(SELF), columns(X_BELOW), columns(Y_BELOW))
    ]
    row = lax.broadcasted_iota(jnp.int32, (NVEC, lanes), 0)
    inverse = list(own)
    for k in range(NVEC):
        pivot = 1.0 / inverse[k][k : k + 1]
        at_k = row == k
        column = inverse[k]
        for j in range(NVEC):
            if j != k:
                scaled = inverse[j][k : k + 1] * pivot
                inverse[j] = jnp.where(at_k, scaled, inverse[j] - column * scaled)
        inverse[k] = jnp.where(at_k, pivot, -column * pivot)

    right = table_ref[pl.ds(RHS, NVEC), :]
    xlo, xlo_t, ylo, ylo_t = (columns(base) for base in (XLO, XLO_T, YLO, YLO_T))
    coarse = OMEGA * product(inverse, right)
    for _ in range(ITERS - 1):
        remainder = right - product(own, coarse)
        remainder = remainder - product(xlo, pltpu.roll(coarse, 1, 1)) - from_x(product(xlo_t, coarse))
        remainder = remainder - product(ylo, pltpu.roll(coarse, window, 1)) - from_y(product(ylo_t, coarse))
        coarse = coarse + OMEGA * product(inverse, remainder)
    here = (lane == index_y * window + place).astype(jnp.float32)
    picked = lax.dot_general(
        here, coarse, (((1,), (1,)), ((), ())), precision=HIGH, preferred_element_type=jnp.float32
    )
    coarse_ref[...] = picked

    more_x, more_y = index_x < count_x - 1, index_y < count_y - 1
    mine = got_ref[index_y, pl.ds(place, 1), :]
    next_x = jnp.where(more_x, got_ref[index_y, pl.ds(jnp.minimum(place + 1, window - 1), 1), :], 0.0)
    next_y = jnp.where(more_y, got_ref[jnp.minimum(index_y + 1, count_y - 1), pl.ds(place, 1), :], 0.0)
    flat = [
        mine[:, SELF : SELF + 64] + next_x[:, X_BELOW : X_BELOW + 64] + next_y[:, Y_BELOW : Y_BELOW + 64],
        mine[:, XLO : XLO + 64],
        next_x[:, XLO_T : XLO_T + 64],
        mine[:, YLO : YLO + 64],
        next_y[:, YLO_T : YLO_T + 64],
    ]
    entry = lax.broadcasted_iota(jnp.int32, (NVEC, 64), 1)
    matches = entry % NVEC == lax.broadcasted_iota(jnp.int32, (NVEC, 64), 0)
    spread = jnp.concatenate([jnp.where(matches, f, 0.0) for f in flat], axis=0)
    select = (
        lax.broadcasted_iota(jnp.int32, (64, NVEC), 0) // NVEC == lax.broadcasted_iota(jnp.int32, (64, NVEC), 1)
    ).astype(jnp.float32)
    blocks_ref[...] = jnp.dot(spread, select, precision=HIGH, preferred_element_type=jnp.float32).reshape(5, 8, 8)


def window_start(index, count, window):
    return jnp.clip(index - window // 2, 0, count - window)


def shape(*dims):
    return jax.ShapeDtypeStruct(dims, jnp.float32)


def per_device(strain_rate, deflation, residual):
    count_x, count_y = lax.axis_size("sx"), lax.axis_size("sy")
    index_x = lax.axis_index("sx")
    window = min(WINDOW, count_x)
    last_x = jnp.concatenate([deflation[:, -1], strain_rate[None, -1]], 0)
    last_y = jnp.concatenate([deflation[:, :, -1], strain_rate[None, :, -1]], 0)
    below_x = lax.ppermute(last_x, "sx", [(i, i + 1) for i in range(count_x - 1)])
    below_y = lax.ppermute(last_y, "sy", [(i, i + 1) for i in range(count_y - 1)])
    first_x = jnp.concatenate([deflation[:, 0], strain_rate[None, 0]], 0)
    first_y = jnp.concatenate([deflation[:, :, 0], strain_rate[None, :, 0]], 0)
    cz = strain_rate.shape[-1]
    own_rows = pl.pallas_call(
        self_kernel,
        out_shape=shape(72, cz),
        scratch_shapes=[
            pltpu.VMEM(strain_rate.shape, jnp.float32),
            pltpu.VMEM((64, 8, cz), jnp.float32),
            pltpu.VMEM((NVEC, 8, cz), jnp.float32),
        ],
        compiler_params=PARAMS,
        cost_estimate=pl.CostEstimate(flops=10000000, bytes_accessed=1400000, transcendentals=0),
        name="own_block",
    )(strain_rate, deflation, residual)
    messages = pl.pallas_call(
        face_kernel,
        out_shape=shape(count_x, 1, WORDS),
        scratch_shapes=[pltpu.VMEM((WORDS, cz), jnp.float32)],
        compiler_params=PARAMS,
        name="face_blocks",
    )(own_rows, first_x, first_y, below_x, below_y)
    line = lax.all_to_all(messages, "sx", 0, 0)
    start = window_start(index_x, count_x, window)
    near = lax.dynamic_slice_in_dim(line, start, window, 0).reshape(window, WORDS)
    got = lax.all_to_all(jnp.broadcast_to(near, (count_y, window, WORDS)), "sy", 0, 0)
    blocks, coarse = pl.pallas_call(
        solve_kernel,
        out_shape=(shape(5, NVEC, NVEC), shape(1, NVEC)),
        scratch_shapes=[pltpu.VMEM((WORDS, count_y * window), jnp.float32)],
        compiler_params=PARAMS,
        name="coarse_sweeps",
    )(got)
    return (blocks.reshape(1, 1, 5, NVEC, NVEC), coarse.reshape(1, 1, NVEC))


def solution(mesh):
    placed = (P("sx", "sy", None), P(None, "sx", "sy", None), P("sx", "sy", None))
    return jax.shard_map(
        per_device,
        mesh=mesh,
        in_specs=placed,
        out_specs=(P("sx", "sy", None, None, None), P("sx", "sy", None)),
        check_vma=False,
    )
```

time: 169 us -> 77.7 us (0.46)
  the two profiles are of different devices: /device:TPU:449 before, /device:TPU:1 now
where the time goes in v1:
time: 77.7 us; the launch traced here: 77.3 us
  blocking collectives  31.6 us (41%)
  starting transfers between devices  19 us (24%)
  waiting for transfers between devices  15.6 us (20%)
  Pallas kernels  6.08 us (8%)
  local copies, waits for them, and re-layouts  4.21 us (5%)
    all_to_all x1, blocking collectives, per_device(): lax.all_to_all(jnp.broadcast_to(near, (count_y, window, WORDS)), 'sy', 0, 0)  31.6 us
    all_to_all x1, waiting for transfers between devices, per_device(): line = lax.all_to_all(messages, 'sx', 0, 0)  12.4 us
    all_to_all x1, starting transfers between devices, per_device(): line = lax.all_to_all(messages, 'sx', 0, 0)  9.07 us
    ppermute x1, starting transfers between devices, per_device(): lax.ppermute(last_y, 'sy', [(i, i + 1) for i in range(count_y - 1)])  5.88 us
    ppermute x1, starting transfers between devices, per_device(): lax.ppermute(last_x, 'sx', [(i, i + 1) for i in range(count_x - 1)])  4.08 us
    ppermute x1, waiting for transfers between devices, per_device(): lax.ppermute(last_y, 'sy', [(i, i + 1) for i in range(count_y - 1)])  3.26 us
    pallas_call x1, Pallas kernels, per_device(): pl.pallas_call(self_kernel, out_shape=shape(72, cz), scratch_shapes=[pltp...  3.24 us
    pallas_call x1, Pallas kernels, per_device(): pl.pallas_call(solve_kernel, out_shape=(shape(5, NVEC, NVEC), shape(1, NV...  1.63 us
  transfers between devices with their start and end apart: 3, of which 2 were waited for; matrix products, arithmetic and copies ran while one was open for 2% of the time, Pallas kernels for 4%

profile of v1, /device:TPU:1, one launch (start us, length us, event | category | flops | bytes accessed | tf_op | source)
XLA Modules:
  0.0 77.3 jit_solution(13486914248870081056)
XLA Ops:
  0.6 0.7 fusion.2
  1.3 0.9 %slice_bitcast_fusion = (f32[8,16,128]{2,1,0:T(8,128)S(1)}, f32[8,16,128]{2,1,0:T(8,128)S(1)}) fusion(f32[8,16,16,128]{3,2,1,0:T(8,128)} %vec_ref.1), kind=kLoop, calls=%fused_computation.4 | loop fusion | bytes 262144 | tf_op jit(solution)/shard_map/squeeze | solution.py:215
  2.2 0.0 copy-start.1
  2.3 4.1 %collective-permute-start = (f32[9,16,128]{2,1,0:T(8,128)S(1)}, f32[9,16,128]{2,1,0:T(8,128)S(1)}, u32[]{:S(2)}, u32[]{:S(2)}) collective-permute-start(f32[9,16,128]{2,1,0:T(8,128)S(1)} %pad_maximum_fusion.2), channel_id=1, source_target_pairs={{0,16},{16,32},{32,48},{48,64},{64,80},{80,96},{96,112},{112,128},... | collective-permute-start | bytes 221192 | tf_op jit(solution)/shard_map/ppermute | solution.py:217
  6.3 0.0 copy-done.1
  6.4 1.3 %fusion = (f32[8,16,1,128]{3,2,1,0:T(1,128)S(1)}, f32[8,16,1,128]{3,2,1,0:T(1,128)S(1)}) fusion(f32[8,16,16,128]{3,2,1,0:T(8,128)} %vec_ref.1), kind=kLoop, calls=%fused_computation.8 | loop fusion | bytes 262144 | tf_op jit(solution)/shard_map/slice | solution.py:216
  7.7 0.0 copy-start.2
  7.7 5.9 %collective-permute-start.1 = (f32[9,16,128]{2,1,0:T(8,128)S(1)}, f32[9,16,128]{2,1,0:T(8,128)S(1)}, u32[]{:S(2)}, u32[]{:S(2)}) collective-permute-start(f32[9,16,128]{2,1,0:T(8,128)S(1)} %pad_maximum_fusion.3), channel_id=1, source_target_pairs={{0,1},{1,2},{2,3},{3,4},{4,5},{5,6},{6,7},{7,8},{8,9},{9,10},{10,1... | collective-permute-start | bytes 221192 | tf_op jit(solution)/shard_map/ppermute | solution.py:218
  13.6 0.0 copy-done.2
  13.6 0.0 copy-start
  13.6 1.2 %copy-done = f32[8,16,16,128]{3,2,1,0:T(8,128)S(1)} copy-done((f32[8,16,16,128]{3,2,1,0:T(8,128)S(1)}, f32[8,16,16,128]{3,2,1,0:T(8,128)}, u32[]{:S(2)}) %copy-start) | copy-done | bytes 1048600
  14.8 3.2 %own_block.1.self_ref = f32[72,128]{1,0:T(8,128)S(1)} custom-call(f32[16,16,128]{2,1,0:T(8,128)S(1)} %copy-done.1, f32[8,16,16,128]{3,2,1,0:T(8,128)S(1)} %copy-done, f32[16,16,128]{2,1,0:T(8,128)S(1)} %copy-done.2), custom_call_target="tpu_custom_call" | custom-call | flops 10000000 | bytes 1400000 | tf_op jit(solution)/shard_map/own_block/pallas_call | solution.py:222
  18.1 0.0 collective-permute-done.below_x_ref
  18.1 3.3 %collective-permute-done.1.below_y_ref = f32[9,16,128]{2,1,0:T(8,128)S(1)} collective-permute-done((f32[9,16,128]{2,1,0:T(8,128)S(1)}, f32[9,16,128]{2,1,0:T(8,128)S(1)}, u32[]{:S(2)}, u32[]{:S(2)}) %collective-permute-start.1) | collective-permute-done | bytes 73760 | tf_op jit(solution)/shard_map/ppermute | solution.py:218
  21.4 1.2 %face_blocks.1 = f32[64,1,512]{2,1,0:T(1,128)} custom-call(f32[72,128]{1,0:T(8,128)S(1)} %own_block.1.self_ref, f32[9,16,128]{2,1,0:T(8,128)S(1)} %get-tuple-element.14.first_x_ref, f32[9,16,128]{2,1,0:T(8,128)S(1)} %get-tuple-element.15.first_y_ref, f32[9,16,128]{2,1,0:T(8,128)S(1)} %collective-permute-done.below_x_ref, ...), custom_call_target="tpu_custom_call" | custom-call | tf_op jit(solution)/shard_map/face_blocks/pallas_call | solution.py:234
  22.6 9.1 %all-to-all-start = ((f32[64,1,512]{2,1,0:T(1,128)}), f32[64,1,512]{2,1,0:T(1,128)S(1)}, u32[]{:S(2)}, u32[]{:S(2)}) async-start(f32[64,1,512]{2,1,0:T(1,128)} %face_blocks.1), calls=%async_computation | async-start | bytes 262144 | tf_op jit(solution)/shard_map/all_to_all | solution.py:241
  31.7 12.4 %all-to-all-done = f32[64,1,512]{2,1,0:T(1,128)S(1)} async-done(((f32[64,1,512]{2,1,0:T(1,128)}), f32[64,1,512]{2,1,0:T(1,128)S(1)}, u32[]{:S(2)}, u32[]{:S(2)}) %all-to-all-start) | async-done | bytes 131104 | tf_op jit(solution)/shard_map/all_to_all | solution.py:241
  44.1 0.1 broadcast_in_dim.3
  44.1 31.6 %all_to_all.10.got_ref = f32[16,16,512]{2,1,0:T(8,128)S(1)} all-to-all(f32[16,16,512]{2,1,0:T(8,128)S(1)} %broadcast_in_dim.3), channel_id=1, replica_groups=mesh['sx'=64,'sy'=16] {'sy'}, dimensions={0} | all-to-all | bytes 1048576 | tf_op jit(solution)/shard_map/all_to_all | solution.py:244
  75.7 1.6 %coarse_sweeps.1 = (f32[5,8,8]{2,1,0:T(8,128)}, f32[1,8]{1,0:T(1,128)}) custom-call(f32[16,16,512]{2,1,0:T(8,128)S(1)} %all_to_all.10.got_ref), custom_call_target="tpu_custom_call" | custom-call | tf_op jit(solution)/shard_map/coarse_sweeps/pallas_call | solution.py:245
  (6 shorter events, 0.1 us)
Async XLA Ops:
  2.2 4.1 %copy-start.1 = (f32[16,16,128]{2,1,0:T(8,128)S(1)}, f32[16,16,128]{2,1,0:T(8,128)}, u32[]{:S(2)}) copy-start(f32[16,16,128]{2,1,0:T(8,128)} %rate_ref.1) | copy-start | bytes 393220
  2.3 15.8 %collective-permute-start = (f32[9,16,128]{2,1,0:T(8,128)S(1)}, f32[9,16,128]{2,1,0:T(8,128)S(1)}, u32[]{:S(2)}, u32[]{:S(2)}) collective-permute-start(f32[9,16,128]{2,1,0:T(8,128)S(1)} %pad_maximum_fusion.2), channel_id=1, source_target_pairs={{0,16},{16,32},{32,48},{48,64},{64,80},{80,96},{96,112},{112,128},... | collective-permute-start | bytes 221192 | tf_op jit(solution)/shard_map/ppermute | solution.py:217
  7.7 5.9 %copy-start.2 = (f32[16,16,128]{2,1,0:T(8,128)S(1)}, f32[16,16,128]{2,1,0:T(8,128)}, u32[]{:S(2)}) copy-start(f32[16,16,128]{2,1,0:T(8,128)} %res_ref.1) | copy-start | bytes 393220
  7.7 13.7 %collective-permute-start.1 = (f32[9,16,128]{2,1,0:T(8,128)S(1)}, f32[9,16,128]{2,1,0:T(8,128)S(1)}, u32[]{:S(2)}, u32[]{:S(2)}) collective-permute-start(f32[9,16,128]{2,1,0:T(8,128)S(1)} %pad_maximum_fusion.3), channel_id=1, source_target_pairs={{0,1},{1,2},{2,3},{3,4},{4,5},{5,6},{6,7},{7,8},{8,9},{9,10},{10,1... | collective-permute-start | bytes 221192 | tf_op jit(solution)/shard_map/ppermute | solution.py:218
  13.6 1.2 %copy-start = (f32[8,16,16,128]{3,2,1,0:T(8,128)S(1)}, f32[8,16,16,128]{3,2,1,0:T(8,128)}, u32[]{:S(2)}) copy-start(f32[8,16,16,128]{3,2,1,0:T(8,128)} %vec_ref.1) | copy-start | bytes 3145732
  22.6 21.5 %all-to-all-start = ((f32[64,1,512]{2,1,0:T(1,128)}), f32[64,1,512]{2,1,0:T(1,128)S(1)}, u32[]{:S(2)}, u32[]{:S(2)}) async-start(f32[64,1,512]{2,1,0:T(1,128)} %face_blocks.1), calls=%async_computation | async-start | bytes 262144 | tf_op jit(solution)/shard_map/all_to_all | solution.py:241

commit v2 on v1

--- a/solution.py
+++ b/solution.py
@@ -11,7 +11,7 @@
 OMEGA = 0.6
 HIGH = lax.Precision.HIGHEST
 
-SELF, XLO, XLO_T, YLO, YLO_T, X_BELOW, Y_BELOW, RHS, WORDS = (0, 64, 128, 192, 256, 320, 384, 448, 512)
+PACKED, TRIANGLE, X_DIAG, Y_DIAG, XLO, YLO, RHS, WORDS = (0, 64, 96, 104, 112, 176, 240, 256)
 WINDOW = 16
 PARAMS = pltpu.CompilerParams(vmem_limit_bytes=32 * 1024 * 1024)
 
@@ -93,33 +93,66 @@
     out_ref[pl.ds(NVEC * NVEC, NVEC), :] = fold([rhs_ref[a] for a in range(NVEC)])
 
 
-def face_rows(axis, own, own_rate, below, rows_ref, lo, lo_t, beneath):
+def transposed(tiles):
+    row = lax.broadcasted_iota(jnp.int32, tiles[0].shape, 0)
+    tiles = list(tiles)
+    for half in (4, 2, 1):
+        low = (row & half) == 0
+        for i in range(NVEC):
+            if not i & half:
+                p, q = tiles[i], tiles[i + half]
+                tiles[i] = jnp.where(low, p, pltpu.roll(q, half, 0))
+                tiles[i + half] = jnp.where(low, pltpu.roll(p, NVEC - half, 0), q)
+    return tiles
+
+
+def face_columns(axis, own, below):
     inner = lax.axis_index(axis) > 0
-    visc = viscosity(own_rate)
+    visc = viscosity(own[NVEC])
     visc_below = viscosity(jnp.where(inner, below[NVEC], 1.0))
     coupling = jnp.where(inner, -0.5 * (visc + visc_below), 0.0)
     beside = 0.5 * jnp.where(inner, visc_below, visc)
     shared = jnp.where(inner, 0.5 * visc, 0.0)
     first = [own[a] for a in range(NVEC)]
     last = [below[a] for a in range(NVEC)]
-    coupled = [coupling * last[b] for b in range(NVEC)]
-    cross = [[halves(first[a] * coupled[b]) for a in range(NVEC)] for b in range(NVEC)]
+
+    def gram(left, right, weight):
+        columns = []
+        for b in range(NVEC):
+            scaled = weight * right[b]
+            columns.append(fold([halves(left[a] * scaled) for a in range(NVEC)]))
+        return columns
+
+    return gram(first, last, coupling), gram(first, first, beside), gram(last, last, shared)
+
+
+def diagonal_of(columns, row):
+    result = columns[0]
+    for b in range(1, NVEC):
+        result = jnp.where(row == b, columns[b], result)
+    return result
+
+
+def face_kernel(self_ref, first_x_ref, first_y_ref, below_x_ref, below_y_ref, out_ref, rows_ref):
+    lo_x, beside_x, beneath_x = face_columns("sx", first_x_ref, below_x_ref)
+    lo_y, beside_y, beneath_y = face_columns("sy", first_y_ref, below_y_ref)
+    row = lax.broadcasted_iota(jnp.int32, lo_x[0].shape, 0)
+
+    def put(base, value):
+        rows_ref[pl.ds(base, NVEC), :] = value
+
     for b in range(NVEC):
-        rows_ref[pl.ds(lo + b * NVEC, NVEC), :] = fold(cross[b])
-        rows_ref[pl.ds(lo_t + b * NVEC, NVEC), :] = fold([cross[a][b] for a in range(NVEC)])
-    for b in range(NVEC):
-        mine = beside * first[b]
-        rows_ref[pl.ds(SELF + b * NVEC, NVEC), :] += fold([halves(first[a] * mine) for a in range(NVEC)])
-        theirs = shared * last[b]
-        rows_ref[pl.ds(beneath + b * NVEC, NVEC), :] = fold([halves(last[a] * theirs) for a in range(NVEC)])
-
-
-def face_kernel(self_ref, first_x_ref, first_y_ref, below_x_ref, below_y_ref, out_ref, rows_ref):
-    rows_ref[pl.ds(SELF, 64), :] = self_ref[pl.ds(0, 64), :]
-    rows_ref[pl.ds(RHS, NVEC), :] = self_ref[pl.ds(64, NVEC), :]
-    rows_ref[pl.ds(RHS + NVEC, WORDS - RHS - NVEC), :] = jnp.zeros((WORDS - RHS - NVEC, 128), jnp.float32)
-    face_rows("sx", first_x_ref, first_x_ref[NVEC], below_x_ref, rows_ref, XLO, XLO_T, X_BELOW)
-    face_rows("sy", first_y_ref, first_y_ref[NVEC], below_y_ref, rows_ref, YLO, YLO_T, Y_BELOW)
+        own = self_ref[pl.ds(b * NVEC, NVEC), :] + beside_x[b] + beside_y[b]
+        put(PACKED + b * NVEC, jnp.where(row <= b, own, beneath_x[b]))
+        put(XLO + b * NVEC, lo_x[b])
+        put(YLO + b * NVEC, lo_y[b])
+    for b in range(NVEC // 2):
+        far = beneath_y[NVEC - 1 - b]
+        put(TRIANGLE + b * NVEC, jnp.where(row > b, beneath_y[b], pltpu.roll(far, b, 0) if b else far))
+    put(X_DIAG, diagonal_of(beneath_x, row))
+    put(Y_DIAG, diagonal_of(beneath_y, row))
+    put(RHS, self_ref[pl.ds(64, NVEC), :])
+    put(RHS + NVEC, jnp.zeros_like(lo_x[0]))
     message = jnp.sum(rows_ref[...].T, axis=0, keepdims=True)
     out_ref[...] = jnp.broadcast_to(message[None], out_ref.shape)
 
@@ -132,11 +165,12 @@
     place = index_x - window_start(index_x, count_x, window)
     table_ref[...] = got_ref[...].reshape(lanes, words).T
     lane = lax.broadcasted_iota(jnp.int32, (1, lanes), 1)
+    row = lax.broadcasted_iota(jnp.int32, (NVEC, lanes), 0)
     has_x = lane % window < window - 1
     has_y = lane < lanes - window
 
-    def columns(base):
-        return [table_ref[pl.ds(base + b * NVEC, NVEC), :] for b in range(NVEC)]
+    def columns(base, count=NVEC):
+        return [table_ref[pl.ds(base + b * NVEC, NVEC), :] for b in range(count)]
 
     def from_x(value):
         return jnp.where(has_x, pltpu.roll(value, lanes - 1, 1), 0.0)
@@ -150,11 +184,22 @@
             terms = [terms[i] + terms[i + 1] for i in range(0, len(terms), 2)]
         return terms[0]
 
+    def mirrored(lower, upper, diagonal):
+        return [
+            jnp.where(row > b, lower[b], jnp.where(row < b, upper[b], diagonal)) for b in range(NVEC)
+        ]
+
+    packed = columns(PACKED)
+    packed_t = transposed(packed)
+    x_diag, y_diag = columns(X_DIAG, 2)
+    beneath_x = mirrored(packed, packed_t, x_diag)
+    lower = columns(TRIANGLE, NVEC // 2)
+    lower = lower + [pltpu.roll(lower[c], NVEC - c, 0) if c else lower[c] for c in (3, 2, 1, 0)]
+    beneath_y = mirrored(lower, transposed(lower), y_diag)
     own = [
-        s + from_x(x) + from_y(y)
-        for s, x, y in zip(columns(SELF), columns(X_BELOW), columns(Y_BELOW))
+        jnp.where(row <= b, packed[b], packed_t[b]) + from_x(beneath_x[b]) + from_y(beneath_y[b])
+        for b in range(NVEC)
     ]
-    row = lax.broadcasted_iota(jnp.int32, (NVEC, lanes), 0)
     inverse = list(own)
     for k in range(NVEC):
         pivot = 1.0 / inverse[k][k : k + 1]
@@ -167,33 +212,32 @@
         inverse[k] = jnp.where(at_k, pivot, -column * pivot)
 
     right = table_ref[pl.ds(RHS, NVEC), :]
-    xlo, xlo_t, ylo, ylo_t = (columns(base) for base in (XLO, XLO_T, YLO, YLO_T))
+    xlo, ylo = columns(XLO), columns(YLO)
+    xlo_t, ylo_t = transposed(xlo), transposed(ylo)
     coarse = OMEGA * product(inverse, right)
     for _ in range(ITERS - 1):
         remainder = right - product(own, coarse)
         remainder = remainder - product(xlo, pltpu.roll(coarse, 1, 1)) - from_x(product(xlo_t, coarse))
         remainder = remainder - product(ylo, pltpu.roll(coarse, window, 1)) - from_y(product(ylo_t, coarse))
         coarse = coarse + OMEGA * product(inverse, remainder)
+
     here = (lane == index_y * window + place).astype(jnp.float32)
-    picked = lax.dot_general(
-        here, coarse, (((1,), (1,)), ((), ())), precision=HIGH, preferred_element_type=jnp.float32
+    results = jnp.concatenate(
+        own + xlo + [from_x(m) for m in xlo_t] + ylo + [from_y(m) for m in ylo_t] + [coarse], axis=0
     )
-    coarse_ref[...] = picked
-
-    more_x, more_y = index_x < count_x - 1, index_y < count_y - 1
-    mine = got_ref[index_y, pl.ds(place, 1), :]
-    next_x = jnp.where(more_x, got_ref[index_y, pl.ds(jnp.minimum(place + 1, window - 1), 1), :], 0.0)
-    next_y = jnp.where(more_y, got_ref[jnp.minimum(index_y + 1, count_y - 1), pl.ds(place, 1), :], 0.0)
-    flat = [
-        mine[:, SELF : SELF + 64] + next_x[:, X_BELOW : X_BELOW + 64] + next_y[:, Y_BELOW : Y_BELOW + 64],
-        mine[:, XLO : XLO + 64],
-        next_x[:, XLO_T : XLO_T + 64],
-        mine[:, YLO : YLO + 64],
-        next_y[:, YLO_T : YLO_T + 64],
-    ]
+    flat = lax.dot_general(
+        jnp.broadcast_to(here, (NVEC, lanes)),
+        results,
+        (((1,), (1,)), ((), ())),
+        precision=HIGH,
+        preferred_element_type=jnp.float32,
+    )
+    coarse_ref[...] = flat[:1, 320:328]
     entry = lax.broadcasted_iota(jnp.int32, (NVEC, 64), 1)
     matches = entry % NVEC == lax.broadcasted_iota(jnp.int32, (NVEC, 64), 0)
-    spread = jnp.concatenate([jnp.where(matches, f, 0.0) for f in flat], axis=0)
+    spread = jnp.concatenate(
+        [jnp.where(matches, flat[:, s * 64 : s * 64 + 64], 0.0) for s in range(5)], axis=0
+    )
     select = (
         lax.broadcasted_iota(jnp.int32, (64, NVEC), 0) // NVEC == lax.broadcasted_iota(jnp.int32, (64, NVEC), 1)
     ).astype(jnp.float32)

time: 77.7 us -> 71.7 us (0.923)
  blocking collectives: 31.6 us -> 26.4 us
  waiting for transfers between devices: 15.6 us -> 14.7 us
    all_to_all x1, blocking collectives: 31.6 us -> 26.4 us  [per_device(): lax.all_to_all(jnp.broadcast_to(near, (count_y, window, WORDS)), 'sy', 0, 0)]
    all_to_all x1, waiting for transfers between devices: 12.4 us -> 11.5 us  [per_device(): line = lax.all_to_all(messages, 'sx', 0, 0)]
  transfers between devices with their start and end apart: 3 -> 3, of which waited for: 2 -> 2; matrix products, arithmetic and copies ran while one was open for 2% -> 2% of each run, Pallas kernels for 4% -> 5%
where the time goes in v2:
time: 71.7 us; the launch traced here: 71.3 us
  blocking collectives  26.4 us (37%)
  starting transfers between devices  19 us (26%)
  waiting for transfers between devices  14.7 us (21%)
  Pallas kernels  6.17 us (9%)
  local copies, waits for them, and re-layouts  4.17 us (6%)
  between operations  0.76 us (1%)
    all_to_all x1, blocking collectives, per_device(): lax.all_to_all(jnp.broadcast_to(near, (count_y, window, WORDS)), 'sy', 0, 0)  26.4 us
    all_to_all x1, waiting for transfers between devices, per_device(): line = lax.all_to_all(messages, 'sx', 0, 0)  11.5 us
    all_to_all x1, starting transfers between devices, per_device(): line = lax.all_to_all(messages, 'sx', 0, 0)  9.06 us
    ppermute x1, starting transfers between devices, per_device(): lax.ppermute(last_y, 'sy', [(i, i + 1) for i in range(count_y - 1)])  5.88 us
    ppermute x1, starting transfers between devices, per_device(): lax.ppermute(last_x, 'sx', [(i, i + 1) for i in range(count_x - 1)])  4.08 us
    ppermute x1, waiting for transfers between devices, per_device(): lax.ppermute(last_y, 'sy', [(i, i + 1) for i in range(count_y - 1)])  3.26 us
    pallas_call x1, Pallas kernels, per_device(): pl.pallas_call(self_kernel, out_shape=shape(72, cz), scratch_shapes=[pltp...  3.24 us
    pallas_call x1, Pallas kernels, per_device(): pl.pallas_call(solve_kernel, out_shape=(shape(5, NVEC, NVEC), shape(1, NV...  1.78 us
  transfers between devices with their start and end apart: 3, of which 2 were waited for; matrix products, arithmetic and copies ran while one was open for 2% of the time, Pallas kernels for 5%

profile of v2, /device:TPU:1, one launch (start us, length us, event | category | flops | bytes accessed | tf_op | source)
XLA Modules:
  0.0 71.3 jit_solution(801489208511922297)
XLA Ops:
  0.6 0.7 %fusion.2 = (f32[1,16,128]{2,1,0:T(8,128)S(1)}, f32[1,16,128]{2,1,0:T(8,128)S(1)}) fusion(f32[16,16,128]{2,1,0:T(8,128)} %rate_ref.1), kind=kLoop, calls=%fused_computation.10 | loop fusion | bytes 32768 | tf_op jit(solution)/shard_map/slice | solution.py:259
  1.3 0.9 %slice_bitcast_fusion = (f32[8,16,128]{2,1,0:T(8,128)S(1)}, f32[8,16,128]{2,1,0:T(8,128)S(1)}) fusion(f32[8,16,16,128]{3,2,1,0:T(8,128)} %vec_ref.1), kind=kLoop, calls=%fused_computation.4 | loop fusion | bytes 262144 | tf_op jit(solution)/shard_map/squeeze | solution.py:259
  2.2 0.0 copy-start.1
  2.3 4.1 %collective-permute-start = (f32[9,16,128]{2,1,0:T(8,128)S(1)}, f32[9,16,128]{2,1,0:T(8,128)S(1)}, u32[]{:S(2)}, u32[]{:S(2)}) collective-permute-start(f32[9,16,128]{2,1,0:T(8,128)S(1)} %pad_maximum_fusion.2), channel_id=1, source_target_pairs={{0,16},{16,32},{32,48},{48,64},{64,80},{80,96},{96,112},{112,128},... | collective-permute-start | bytes 221192 | tf_op jit(solution)/shard_map/ppermute | solution.py:261
  6.3 0.0 copy-done.1
  6.4 1.3 %fusion = (f32[8,16,1,128]{3,2,1,0:T(1,128)S(1)}, f32[8,16,1,128]{3,2,1,0:T(1,128)S(1)}) fusion(f32[8,16,16,128]{3,2,1,0:T(8,128)} %vec_ref.1), kind=kLoop, calls=%fused_computation.8 | loop fusion | bytes 262144 | tf_op jit(solution)/shard_map/slice | solution.py:260
  7.7 0.0 copy-start.2
  7.7 5.9 %collective-permute-start.1 = (f32[9,16,128]{2,1,0:T(8,128)S(1)}, f32[9,16,128]{2,1,0:T(8,128)S(1)}, u32[]{:S(2)}, u32[]{:S(2)}) collective-permute-start(f32[9,16,128]{2,1,0:T(8,128)S(1)} %pad_maximum_fusion.3), channel_id=1, source_target_pairs={{0,1},{1,2},{2,3},{3,4},{4,5},{5,6},{6,7},{7,8},{8,9},{9,10},{10,1... | collective-permute-start | bytes 221192 | tf_op jit(solution)/shard_map/ppermute | solution.py:262
  13.6 0.0 copy-done.2
  13.6 0.0 copy-start
  13.6 1.2 %copy-done = f32[8,16,16,128]{3,2,1,0:T(8,128)S(1)} copy-done((f32[8,16,16,128]{3,2,1,0:T(8,128)S(1)}, f32[8,16,16,128]{3,2,1,0:T(8,128)}, u32[]{:S(2)}) %copy-start) | copy-done | bytes 1048600
  14.8 3.2 %own_block.1.self_ref = f32[72,128]{1,0:T(8,128)S(1)} custom-call(f32[16,16,128]{2,1,0:T(8,128)S(1)} %copy-done.1, f32[8,16,16,128]{3,2,1,0:T(8,128)S(1)} %copy-done, f32[16,16,128]{2,1,0:T(8,128)S(1)} %copy-done.2), custom_call_target="tpu_custom_call" | custom-call | flops 10000000 | bytes 1400000 | tf_op jit(solution)/shard_map/own_block/pallas_call | solution.py:266
  18.1 0.0 collective-permute-done.below_x_ref
  18.1 3.3 %collective-permute-done.1.below_y_ref = f32[9,16,128]{2,1,0:T(8,128)S(1)} collective-permute-done((f32[9,16,128]{2,1,0:T(8,128)S(1)}, f32[9,16,128]{2,1,0:T(8,128)S(1)}, u32[]{:S(2)}, u32[]{:S(2)}) %collective-permute-start.1) | collective-permute-done | bytes 73760 | tf_op jit(solution)/shard_map/ppermute | solution.py:262
  21.4 1.1 %face_blocks.1 = f32[64,1,256]{2,1,0:T(1,128)} custom-call(f32[72,128]{1,0:T(8,128)S(1)} %own_block.1.self_ref, f32[9,16,128]{2,1,0:T(8,128)S(1)} %get-tuple-element.14.first_x_ref, f32[9,16,128]{2,1,0:T(8,128)S(1)} %get-tuple-element.15.first_y_ref, f32[9,16,128]{2,1,0:T(8,128)S(1)} %collective-permute-done.below_x_ref, ...), custom_call_target="tpu_custom_call" | custom-call | tf_op jit(solution)/shard_map/face_blocks/pallas_call | solution.py:278
  22.5 9.1 %all-to-all-start = ((f32[64,1,256]{2,1,0:T(1,128)}), f32[64,1,256]{2,1,0:T(1,128)S(1)}, u32[]{:S(2)}, u32[]{:S(2)}) async-start(f32[64,1,256]{2,1,0:T(1,128)} %face_blocks.1), calls=%async_computation | async-start | bytes 131072 | tf_op jit(solution)/shard_map/all_to_all | solution.py:285
  31.6 11.5 %all-to-all-done = f32[64,1,256]{2,1,0:T(1,128)S(1)} async-done(((f32[64,1,256]{2,1,0:T(1,128)}), f32[64,1,256]{2,1,0:T(1,128)S(1)}, u32[]{:S(2)}, u32[]{:S(2)}) %all-to-all-start) | async-done | bytes 65568 | tf_op jit(solution)/shard_map/all_to_all | solution.py:285
  43.1 26.4 %all_to_all.10.got_ref = f32[16,16,256]{2,1,0:T(8,128)S(1)} all-to-all(f32[16,16,256]{2,1,0:T(8,128)S(1)} %broadcast_in_dim.3), channel_id=1, replica_groups=mesh['sx'=64,'sy'=16] {'sy'}, dimensions={0} | all-to-all | bytes 524288 | tf_op jit(solution)/shard_map/all_to_all | solution.py:288
  69.5 1.8 %coarse_sweeps.1 = (f32[5,8,8]{2,1,0:T(8,128)}, f32[1,8]{1,0:T(1,128)}) custom-call(f32[16,16,256]{2,1,0:T(8,128)S(1)} %all_to_all.10.got_ref), custom_call_target="tpu_custom_call" | custom-call | tf_op jit(solution)/shard_map/coarse_sweeps/pallas_call | solution.py:289
  (7 shorter events, 0.1 us)
Async XLA Ops:
  2.2 4.1 %copy-start.1 = (f32[16,16,128]{2,1,0:T(8,128)S(1)}, f32[16,16,128]{2,1,0:T(8,128)}, u32[]{:S(2)}) copy-start(f32[16,16,128]{2,1,0:T(8,128)} %rate_ref.1) | copy-start | bytes 393220
  2.3 15.8 %collective-permute-start = (f32[9,16,128]{2,1,0:T(8,128)S(1)}, f32[9,16,128]{2,1,0:T(8,128)S(1)}, u32[]{:S(2)}, u32[]{:S(2)}) collective-permute-start(f32[9,16,128]{2,1,0:T(8,128)S(1)} %pad_maximum_fusion.2), channel_id=1, source_target_pairs={{0,16},{16,32},{32,48},{48,64},{64,80},{80,96},{96,112},{112,128},... | collective-permute-start | bytes 221192 | tf_op jit(solution)/shard_map/ppermute | solution.py:261
  7.7 5.9 %copy-start.2 = (f32[16,16,128]{2,1,0:T(8,128)S(1)}, f32[16,16,128]{2,1,0:T(8,128)}, u32[]{:S(2)}) copy-start(f32[16,16,128]{2,1,0:T(8,128)} %res_ref.1) | copy-start | bytes 393220
  7.7 13.7 %collective-permute-start.1 = (f32[9,16,128]{2,1,0:T(8,128)S(1)}, f32[9,16,128]{2,1,0:T(8,128)S(1)}, u32[]{:S(2)}, u32[]{:S(2)}) collective-permute-start(f32[9,16,128]{2,1,0:T(8,128)S(1)} %pad_maximum_fusion.3), channel_id=1, source_target_pairs={{0,1},{1,2},{2,3},{3,4},{4,5},{5,6},{6,7},{7,8},{8,9},{9,10},{10,1... | collective-permute-start | bytes 221192 | tf_op jit(solution)/shard_map/ppermute | solution.py:262
  13.6 1.2 %copy-start = (f32[8,16,16,128]{3,2,1,0:T(8,128)S(1)}, f32[8,16,16,128]{3,2,1,0:T(8,128)}, u32[]{:S(2)}) copy-start(f32[8,16,16,128]{3,2,1,0:T(8,128)} %vec_ref.1) | copy-start | bytes 3145732
  22.5 20.5 %all-to-all-start = ((f32[64,1,256]{2,1,0:T(1,128)}), f32[64,1,256]{2,1,0:T(1,128)S(1)}, u32[]{:S(2)}, u32[]{:S(2)}) async-start(f32[64,1,256]{2,1,0:T(1,128)} %face_blocks.1), calls=%async_computation | async-start | bytes 131072 | tf_op jit(solution)/shard_map/all_to_all | solution.py:285

commit v3 on v2

--- a/solution.py
+++ b/solution.py
@@ -13,6 +13,7 @@
 
 PACKED, TRIANGLE, X_DIAG, Y_DIAG, XLO, YLO, RHS, WORDS = (0, 64, 96, 104, 112, 176, 240, 256)
 WINDOW = 16
+ROW = 8
 PARAMS = pltpu.CompilerParams(vmem_limit_bytes=32 * 1024 * 1024)
 
 
@@ -161,8 +162,7 @@
     count_y, window, words = got_ref.shape
     lanes = count_y * window
     index_x, index_y = lax.axis_index("sx"), lax.axis_index("sy")
-    count_x = lax.axis_size("sx")
-    place = index_x - window_start(index_x, count_x, window)
+    place = ROW + index_x % ROW - window_start(index_x, lax.axis_size("sx"))
     table_ref[...] = got_ref[...].reshape(lanes, words).T
     lane = lax.broadcasted_iota(jnp.int32, (1, lanes), 1)
     row = lax.broadcasted_iota(jnp.int32, (NVEC, lanes), 0)
@@ -244,8 +244,21 @@
     blocks_ref[...] = jnp.dot(spread, select, precision=HIGH, preferred_element_type=jnp.float32).reshape(5, 8, 8)
 
 
-def window_start(index, count, window):
-    return jnp.clip(index - window // 2, 0, count - window)
+def window_start(index, count):
+    chip_row = index // ROW
+    low = jnp.where(chip_row > 0, 0, ROW)
+    high = jnp.where(chip_row < count // ROW - 1, 3 * ROW, 2 * ROW) - WINDOW
+    return jnp.clip(ROW + index % ROW - WINDOW // 2, low, high)
+
+
+def window_kernel(lower_ref, line_ref, upper_ref, out_ref, rows_ref, near_ref):
+    start = window_start(lax.axis_index("sx"), lax.axis_size("sx"))
+    for part, ref in enumerate((lower_ref, line_ref, upper_ref)):
+        for i in range(ROW):
+            rows_ref[pl.ds(part * ROW + i, 1), :] = ref[i]
+    for i in range(WINDOW):
+        near_ref[pl.ds(i, 1), :] = rows_ref[pl.ds(start + i, 1), :]
+    out_ref[...] = jnp.broadcast_to(near_ref[...][None], out_ref.shape)
 
 
 def shape(*dims):
@@ -254,8 +267,6 @@
 
 def per_device(strain_rate, deflation, residual):
     count_x, count_y = lax.axis_size("sx"), lax.axis_size("sy")
-    index_x = lax.axis_index("sx")
-    window = min(WINDOW, count_x)
     last_x = jnp.concatenate([deflation[:, -1], strain_rate[None, -1]], 0)
     last_y = jnp.concatenate([deflation[:, :, -1], strain_rate[None, :, -1]], 0)
     below_x = lax.ppermute(last_x, "sx", [(i, i + 1) for i in range(count_x - 1)])
@@ -277,19 +288,27 @@
     )(strain_rate, deflation, residual)
     messages = pl.pallas_call(
         face_kernel,
-        out_shape=shape(count_x, 1, WORDS),
+        out_shape=shape(ROW, 1, WORDS),
         scratch_shapes=[pltpu.VMEM((WORDS, cz), jnp.float32)],
         compiler_params=PARAMS,
         name="face_blocks",
     )(own_rows, first_x, first_y, below_x, below_y)
-    line = lax.all_to_all(messages, "sx", 0, 0)
-    start = window_start(index_x, count_x, window)
-    near = lax.dynamic_slice_in_dim(line, start, window, 0).reshape(window, WORDS)
-    got = lax.all_to_all(jnp.broadcast_to(near, (count_y, window, WORDS)), "sy", 0, 0)
+    rows = [[ROW * g + i for i in range(ROW)] for g in range(count_x // ROW)]
+    line = lax.all_to_all(messages, "sx", 0, 0, axis_index_groups=rows)
+    lower = lax.ppermute(line, "sx", [(i, i + ROW) for i in range(count_x - ROW)])
+    upper = lax.ppermute(line, "sx", [(i + ROW, i) for i in range(count_x - ROW)])
+    near = pl.pallas_call(
+        window_kernel,
+        out_shape=shape(count_y, WINDOW, WORDS),
+        scratch_shapes=[pltpu.VMEM((3 * ROW, WORDS), jnp.float32), pltpu.VMEM((WINDOW, WORDS), jnp.float32)],
+        compiler_params=PARAMS,
+        name="window",
+    )(lower, line, upper)
+    got = lax.all_to_all(near, "sy", 0, 0)
     blocks, coarse = pl.pallas_call(
         solve_kernel,
         out_shape=(shape(5, NVEC, NVEC), shape(1, NVEC)),
-        scratch_shapes=[pltpu.VMEM((WORDS, count_y * window), jnp.float32)],
+        scratch_shapes=[pltpu.VMEM((WORDS, count_y * WINDOW), jnp.float32)],
         compiler_params=PARAMS,
         name="coarse_sweeps",
     )(got)

time: 71.7 us -> 67.8 us (0.946)
  the two profiles are of different devices: /device:TPU:1 before, /device:TPU:65 now
where the time goes in v3:
time: 67.8 us; the launch traced here: 67.4 us
  blocking collectives  40.1 us (59%)
  starting transfers between devices  14.4 us (21%)
  Pallas kernels  5.6 us (8%)
  local copies, waits for them, and re-layouts  4.15 us (6%)
  waiting for transfers between devices  2.28 us (3%)
  between operations  0.77 us (1%)
    all_to_all x1, blocking collectives, per_device(): got = lax.all_to_all(near, 'sy', 0, 0)  28.2 us
    all_to_all x1, blocking collectives, per_device(): line = lax.all_to_all(messages, 'sx', 0, 0, axis_index_groups=rows)  12 us
    ppermute x1, starting transfers between devices, per_device(): lax.ppermute(last_y, 'sy', [(i, i + 1) for i in range(count_y - 1)])  5.88 us
    ppermute x1, starting transfers between devices, per_device(): lax.ppermute(line, 'sx', [(i, i + ROW) for i in range(count_x - ROW)])  3.32 us
    ppermute x1, starting transfers between devices, per_device(): lax.ppermute(last_x, 'sx', [(i, i + 1) for i in range(count_x - 1)])  3.25 us
    pallas_call x1, Pallas kernels, per_device(): pl.pallas_call(self_kernel, out_shape=shape(72, cz), scratch_shapes=[pltp...  3.24 us
    ppermute x1, waiting for transfers between devices, per_device(): lax.ppermute(line, 'sx', [(i, i + ROW) for i in range(count_x - ROW)])  2.27 us
    ppermute x1, starting transfers between devices, per_device(): lax.ppermute(line, 'sx', [(i + ROW, i) for i in range(count_x - ROW)])  1.95 us
  transfers between devices with their start and end apart: 4, of which 1 were waited for; matrix products, arithmetic and copies ran while one was open for 2% of the time, Pallas kernels for 5%

profile of v3, /device:TPU:65, one launch (start us, length us, event | category | flops | bytes accessed | tf_op | source)
XLA Modules:
  0.0 67.4 jit_solution(16022565037748812418)
XLA Ops:
  0.6 0.7 %fusion.2 = (f32[1,16,128]{2,1,0:T(8,128)S(1)}, f32[1,16,128]{2,1,0:T(8,128)S(1)}) fusion(f32[16,16,128]{2,1,0:T(8,128)} %rate_ref.1), kind=kLoop, calls=%fused_computation.8 | loop fusion | bytes 32768 | tf_op jit(solution)/shard_map/slice | solution.py:270
  1.3 0.9 %slice_bitcast_fusion = (f32[8,16,128]{2,1,0:T(8,128)S(1)}, f32[8,16,128]{2,1,0:T(8,128)S(1)}) fusion(f32[8,16,16,128]{3,2,1,0:T(8,128)} %vec_ref.1), kind=kLoop, calls=%fused_computation.4 | loop fusion | bytes 262144 | tf_op jit(solution)/shard_map/squeeze | solution.py:270
  2.2 0.0 copy-start.1
  2.3 3.3 %collective-permute-start = (f32[9,16,128]{2,1,0:T(8,128)S(1)}, f32[9,16,128]{2,1,0:T(8,128)S(1)}, u32[]{:S(2)}, u32[]{:S(2)}) collective-permute-start(f32[9,16,128]{2,1,0:T(8,128)S(1)} %pad_maximum_fusion.2), channel_id=1, source_target_pairs={{0,16},{16,32},{32,48},{48,64},{64,80},{80,96},{96,112},{112,128},... | collective-permute-start | bytes 221192 | tf_op jit(solution)/shard_map/ppermute | solution.py:272
  5.5 0.0 copy-done.1
  5.6 1.3 %fusion = (f32[8,16,1,128]{3,2,1,0:T(1,128)S(1)}, f32[8,16,1,128]{3,2,1,0:T(1,128)S(1)}) fusion(f32[8,16,16,128]{3,2,1,0:T(8,128)} %vec_ref.1), kind=kLoop, calls=%fused_computation.6 | loop fusion | bytes 262144 | tf_op jit(solution)/shard_map/slice | solution.py:271
  6.9 0.0 copy-start.2
  6.9 5.9 %collective-permute-start.1 = (f32[9,16,128]{2,1,0:T(8,128)S(1)}, f32[9,16,128]{2,1,0:T(8,128)S(1)}, u32[]{:S(2)}, u32[]{:S(2)}) collective-permute-start(f32[9,16,128]{2,1,0:T(8,128)S(1)} %pad_maximum_fusion.3), channel_id=1, source_target_pairs={{0,1},{1,2},{2,3},{3,4},{4,5},{5,6},{6,7},{7,8},{8,9},{9,10},{10,1... | collective-permute-start | bytes 221192 | tf_op jit(solution)/shard_map/ppermute | solution.py:273
  12.8 0.0 copy-done.2
  12.8 0.0 copy-start
  12.8 1.2 %copy-done = f32[8,16,16,128]{3,2,1,0:T(8,128)S(1)} copy-done((f32[8,16,16,128]{3,2,1,0:T(8,128)S(1)}, f32[8,16,16,128]{3,2,1,0:T(8,128)}, u32[]{:S(2)}) %copy-start) | copy-done | bytes 1048600
  14.0 3.2 %own_block.1.self_ref = f32[72,128]{1,0:T(8,128)S(1)} custom-call(f32[16,16,128]{2,1,0:T(8,128)S(1)} %copy-done.1, f32[8,16,16,128]{3,2,1,0:T(8,128)S(1)} %copy-done, f32[16,16,128]{2,1,0:T(8,128)S(1)} %copy-done.2), custom_call_target="tpu_custom_call" | custom-call | flops 10000000 | bytes 1400000 | tf_op jit(solution)/shard_map/own_block/pallas_call | solution.py:277
  17.3 0.0 collective-permute-done.below_x_ref
  17.3 0.0 collective-permute-done.1.below_y_ref
  17.3 0.5 face_blocks.1
  17.8 12.0 %all_to_all.10.line_ref = f32[8,1,256]{2,1,0:T(1,128)S(1)} all-to-all(f32[8,1,256]{2,1,0:T(1,128)S(1)} %face_blocks.1), channel_id=1, replica_groups={{0,16,32,48,64,80,96,112},{128,144,160,176,192,208,224,240},{256,272,28..., dimensions={0} | all-to-all | bytes 16384 | tf_op jit(solution)/shard_map/all_to_all | solution.py:297
  29.8 2.0 %collective-permute-start.3 = (f32[8,1,256]{2,1,0:T(1,128)S(1)}, f32[8,1,256]{2,1,0:T(1,128)S(1)}, u32[]{:S(2)}, u32[]{:S(2)}) collective-permute-start(f32[8,1,256]{2,1,0:T(1,128)S(1)} %all_to_all.10.line_ref), channel_id=1, source_target_pairs={{128,0},{144,16},{160,32},{176,48},{192,64},{208,80},{224,96},{240... | collective-permute-start | bytes 24584 | tf_op jit(solution)/shard_map/ppermute | solution.py:299
  31.7 3.3 %collective-permute-start.2 = (f32[8,1,256]{2,1,0:T(1,128)S(1)}, f32[8,1,256]{2,1,0:T(1,128)S(1)}, u32[]{:S(2)}, u32[]{:S(2)}) collective-permute-start(f32[8,1,256]{2,1,0:T(1,128)S(1)} %all_to_all.10.line_ref), channel_id=1, source_target_pairs={{0,128},{16,144},{32,160},{48,176},{64,192},{80,208},{96,224},{112... | collective-permute-start | bytes 24584 | tf_op jit(solution)/shard_map/ppermute | solution.py:298
  35.0 0.0 collective-permute-done.3.upper_ref
  35.1 2.3 %collective-permute-done.2.lower_ref = f32[8,1,256]{2,1,0:T(1,128)S(1)} collective-permute-done((f32[8,1,256]{2,1,0:T(1,128)S(1)}, f32[8,1,256]{2,1,0:T(1,128)S(1)}, u32[]{:S(2)}, u32[]{:S(2)}) %collective-permute-start.2) | collective-permute-done | bytes 8224 | tf_op jit(solution)/shard_map/ppermute | solution.py:298
  37.3 0.1 window.1
  37.4 28.2 %all_to_all.11.got_ref = f32[16,16,256]{2,1,0:T(8,128)S(1)} all-to-all(f32[16,16,256]{2,1,0:T(8,128)S(1)} %window.1), channel_id=1, replica_groups=mesh['sx'=64,'sy'=16] {'sy'}, dimensions={0} | all-to-all | bytes 524288 | tf_op jit(solution)/shard_map/all_to_all | solution.py:307
  65.6 1.8 %coarse_sweeps.1 = (f32[5,8,8]{2,1,0:T(8,128)}, f32[1,8]{1,0:T(1,128)}) custom-call(f32[16,16,256]{2,1,0:T(8,128)S(1)} %all_to_all.11.got_ref), custom_call_target="tpu_custom_call" | custom-call | tf_op jit(solution)/shard_map/coarse_sweeps/pallas_call | solution.py:308
  (4 shorter events, 0.0 us)
Async XLA Ops:
  2.2 3.3 %copy-start.1 = (f32[16,16,128]{2,1,0:T(8,128)S(1)}, f32[16,16,128]{2,1,0:T(8,128)}, u32[]{:S(2)}) copy-start(f32[16,16,128]{2,1,0:T(8,128)} %rate_ref.1) | copy-start | bytes 393220
  2.3 15.0 %collective-permute-start = (f32[9,16,128]{2,1,0:T(8,128)S(1)}, f32[9,16,128]{2,1,0:T(8,128)S(1)}, u32[]{:S(2)}, u32[]{:S(2)}) collective-permute-start(f32[9,16,128]{2,1,0:T(8,128)S(1)} %pad_maximum_fusion.2), channel_id=1, source_target_pairs={{0,16},{16,32},{32,48},{48,64},{64,80},{80,96},{96,112},{112,128},... | collective-permute-start | bytes 221192 | tf_op jit(solution)/shard_map/ppermute | solution.py:272
  6.9 5.9 %copy-start.2 = (f32[16,16,128]{2,1,0:T(8,128)S(1)}, f32[16,16,128]{2,1,0:T(8,128)}, u32[]{:S(2)}) copy-start(f32[16,16,128]{2,1,0:T(8,128)} %res_ref.1) | copy-start | bytes 393220
  6.9 10.4 %collective-permute-start.1 = (f32[9,16,128]{2,1,0:T(8,128)S(1)}, f32[9,16,128]{2,1,0:T(8,128)S(1)}, u32[]{:S(2)}, u32[]{:S(2)}) collective-permute-start(f32[9,16,128]{2,1,0:T(8,128)S(1)} %pad_maximum_fusion.3), channel_id=1, source_target_pairs={{0,1},{1,2},{2,3},{3,4},{4,5},{5,6},{6,7},{7,8},{8,9},{9,10},{10,1... | collective-permute-start | bytes 221192 | tf_op jit(solution)/shard_map/ppermute | solution.py:273
  12.8 1.2 %copy-start = (f32[8,16,16,128]{3,2,1,0:T(8,128)S(1)}, f32[8,16,16,128]{3,2,1,0:T(8,128)}, u32[]{:S(2)}) copy-start(f32[8,16,16,128]{3,2,1,0:T(8,128)} %vec_ref.1) | copy-start | bytes 3145732
  29.8 5.3 %collective-permute-start.3 = (f32[8,1,256]{2,1,0:T(1,128)S(1)}, f32[8,1,256]{2,1,0:T(1,128)S(1)}, u32[]{:S(2)}, u32[]{:S(2)}) collective-permute-start(f32[8,1,256]{2,1,0:T(1,128)S(1)} %all_to_all.10.line_ref), channel_id=1, source_target_pairs={{128,0},{144,16},{160,32},{176,48},{192,64},{208,80},{224,96},{240... | collective-permute-start | bytes 24584 | tf_op jit(solution)/shard_map/ppermute | solution.py:299
  31.7 5.6 %collective-permute-start.2 = (f32[8,1,256]{2,1,0:T(1,128)S(1)}, f32[8,1,256]{2,1,0:T(1,128)S(1)}, u32[]{:S(2)}, u32[]{:S(2)}) collective-permute-start(f32[8,1,256]{2,1,0:T(1,128)S(1)} %all_to_all.10.line_ref), channel_id=1, source_target_pairs={{0,128},{16,144},{32,160},{48,176},{64,192},{80,208},{96,224},{112... | collective-permute-start | bytes 24584 | tf_op jit(solution)/shard_map/ppermute | solution.py:298

commit v4 on v3

--- a/solution.py
+++ b/solution.py
@@ -14,6 +14,9 @@
 PACKED, TRIANGLE, X_DIAG, Y_DIAG, XLO, YLO, RHS, WORDS = (0, 64, 96, 104, 112, 176, 240, 256)
 WINDOW = 16
 ROW = 8
+CORES = 2
+REACH = 3
+LINES = 2 * CORES * (REACH + 1)
 PARAMS = pltpu.CompilerParams(vmem_limit_bytes=32 * 1024 * 1024)
 
 
@@ -158,14 +161,25 @@
     out_ref[...] = jnp.broadcast_to(message[None], out_ref.shape)
 
 
-def solve_kernel(got_ref, blocks_ref, coarse_ref, table_ref):
-    count_y, window, words = got_ref.shape
-    lanes = count_y * window
+def solve_kernel(near_ref, mine_ref, other_ref, blocks_ref, coarse_ref, table_ref):
+    window, words = near_ref.shape[1:]
+    lanes = LINES * window
     index_x, index_y = lax.axis_index("sx"), lax.axis_index("sy")
+    core, chip = index_y % CORES, index_y // CORES
     place = ROW + index_x % ROW - window_start(index_x, lax.axis_size("sx"))
-    table_ref[...] = got_ref[...].reshape(lanes, words).T
+    below = [jnp.where(core == 0, mine_ref[i], other_ref[i]) for i in range(CORES * REACH)]
+    above = [jnp.where(core == 0, other_ref[i], mine_ref[i]) for i in range(CORES * REACH)]
+    parts = [jnp.zeros((CORES * window, words), jnp.float32)]
+    for step in range(REACH, 0, -1):
+        parts += below[CORES * (step - 1) : CORES * step]
+    parts += [near_ref[i] for i in range(CORES)] + above
+    table_ref[...] = jnp.concatenate(parts, axis=0).T
     lane = lax.broadcasted_iota(jnp.int32, (1, lanes), 1)
     row = lax.broadcasted_iota(jnp.int32, (NVEC, lanes), 0)
+    away = lane // (CORES * window) - (REACH + 1)
+    count_chips = lax.axis_size("sy") // CORES
+    filled = (away >= -REACH) & (chip + away >= 0) & (chip + away < count_chips)
+    unit = jnp.where(filled, 0.0, 1.0)
     has_x = lane % window < window - 1
     has_y = lane < lanes - window
 
@@ -197,7 +211,10 @@
     lower = lower + [pltpu.roll(lower[c], NVEC - c, 0) if c else lower[c] for c in (3, 2, 1, 0)]
     beneath_y = mirrored(lower, transposed(lower), y_diag)
     own = [
-        jnp.where(row <= b, packed[b], packed_t[b]) + from_x(beneath_x[b]) + from_y(beneath_y[b])
+        jnp.where(row <= b, packed[b], packed_t[b])
+        + from_x(beneath_x[b])
+        + from_y(beneath_y[b])
+        + jnp.where(row == b, unit, 0.0)
         for b in range(NVEC)
     ]
     inverse = list(own)
@@ -221,7 +238,7 @@
         remainder = remainder - product(ylo, pltpu.roll(coarse, window, 1)) - from_y(product(ylo_t, coarse))
         coarse = coarse + OMEGA * product(inverse, remainder)
 
-    here = (lane == index_y * window + place).astype(jnp.float32)
+    here = (lane == (CORES * (REACH + 1) + core) * window + place).astype(jnp.float32)
     results = jnp.concatenate(
         own + xlo + [from_x(m) for m in xlo_t] + ylo + [from_y(m) for m in ylo_t] + [coarse], axis=0
     )
@@ -251,14 +268,15 @@
     return jnp.clip(ROW + index % ROW - WINDOW // 2, low, high)
 
 
-def window_kernel(lower_ref, line_ref, upper_ref, out_ref, rows_ref, near_ref):
+def window_kernel(lower_ref, line_ref, upper_ref, out_ref, rows_ref):
     start = window_start(lax.axis_index("sx"), lax.axis_size("sx"))
+    count = CORES * ROW
     for part, ref in enumerate((lower_ref, line_ref, upper_ref)):
-        for i in range(ROW):
-            rows_ref[pl.ds(part * ROW + i, 1), :] = ref[i]
-    for i in range(WINDOW):
-        near_ref[pl.ds(i, 1), :] = rows_ref[pl.ds(start + i, 1), :]
-    out_ref[...] = jnp.broadcast_to(near_ref[...][None], out_ref.shape)
+        for i in range(count):
+            rows_ref[pl.ds(part * count + i, 1), :] = ref[i]
+    for core in range(CORES):
+        for i in range(WINDOW):
+            out_ref[core, pl.ds(i, 1), :] = rows_ref[pl.ds(CORES * (start + i) + core, 1), :]
 
 
 def shape(*dims):
@@ -288,30 +306,42 @@
     )(strain_rate, deflation, residual)
     messages = pl.pallas_call(
         face_kernel,
-        out_shape=shape(ROW, 1, WORDS),
+        out_shape=shape(CORES * ROW, 1, WORDS),
         scratch_shapes=[pltpu.VMEM((WORDS, cz), jnp.float32)],
         compiler_params=PARAMS,
         name="face_blocks",
     )(own_rows, first_x, first_y, below_x, below_y)
-    rows = [[ROW * g + i for i in range(ROW)] for g in range(count_x // ROW)]
-    line = lax.all_to_all(messages, "sx", 0, 0, axis_index_groups=rows)
+    chips = range(count_y // CORES)
+    rows = [
+        [(ROW * g + i) * count_y + CORES * z + c for i in range(ROW) for c in range(CORES)]
+        for g in range(count_x // ROW)
+        for z in chips
+    ]
+    line = lax.all_to_all(messages, ("sx", "sy"), 0, 0, axis_index_groups=rows)
     lower = lax.ppermute(line, "sx", [(i, i + ROW) for i in range(count_x - ROW)])
     upper = lax.ppermute(line, "sx", [(i + ROW, i) for i in range(count_x - ROW)])
     near = pl.pallas_call(
         window_kernel,
-        out_shape=shape(count_y, WINDOW, WORDS),
-        scratch_shapes=[pltpu.VMEM((3 * ROW, WORDS), jnp.float32), pltpu.VMEM((WINDOW, WORDS), jnp.float32)],
+        out_shape=shape(CORES, WINDOW, WORDS),
+        scratch_shapes=[pltpu.VMEM((3 * CORES * ROW, WORDS), jnp.float32)],
         compiler_params=PARAMS,
         name="window",
     )(lower, line, upper)
-    got = lax.all_to_all(near, "sy", 0, 0)
+    received = []
+    for step in range(1, REACH + 1):
+        up = [(CORES * z, CORES * (z + step)) for z in chips if z + step in chips]
+        down = [(CORES * z + 1, CORES * (z - step) + 1) for z in chips if z - step in chips]
+        received.append(lax.ppermute(near, "sy", up + down))
+    mine = jnp.concatenate(received, axis=0)
+    swap = [(CORES * z + c, CORES * z + 1 - c) for z in chips for c in range(CORES)]
+    other = lax.ppermute(mine, "sy", swap)
     blocks, coarse = pl.pallas_call(
         solve_kernel,
         out_shape=(shape(5, NVEC, NVEC), shape(1, NVEC)),
-        scratch_shapes=[pltpu.VMEM((WORDS, count_y * WINDOW), jnp.float32)],
+        scratch_shapes=[pltpu.VMEM((WORDS, LINES * WINDOW), jnp.float32)],
         compiler_params=PARAMS,
         name="coarse_sweeps",
-    )(got)
+    )(near, mine, other)
     return (blocks.reshape(1, 1, 5, NVEC, NVEC), coarse.reshape(1, 1, NVEC))
 
 

time: 67.8 us -> 71.1 us (1.049)
  the two profiles are of different devices: /device:TPU:65 before, /device:TPU:49 now
where the time goes in v4:
time: 71.1 us; the launch traced here: 70.7 us
  starting transfers between devices  30.2 us (42%)
  waiting for transfers between devices  17.5 us (25%)
  blocking collectives  13.1 us (18%)
  Pallas kernels  5.62 us (8%)
  local copies, waits for them, and re-layouts  3.51 us (5%)
  between operations  0.8 us (1%)
    all_to_all x1, blocking collectives, per_device(): line = lax.all_to_all(messages, ('sx', 'sy'), 0, 0, axis_index_groups=rows)  13.1 us
    ppermute x3, waiting for transfers between devices, per_device(): received.append(lax.ppermute(near, 'sy', up + down))  12.8 us
    ppermute x1, starting transfers between devices, per_device(): other = lax.ppermute(mine, 'sy', swap)  10.8 us
    ppermute x1, starting transfers between devices, per_device(): lax.ppermute(last_y, 'sy', [(i, i + 1) for i in range(count_y - 1)])  5.88 us
    ppermute x1, starting transfers between devices, per_device(): lax.ppermute(line, 'sx', [(i, i + ROW) for i in range(count_x - ROW)])  4.52 us
    ppermute x3, starting transfers between devices, per_device(): received.append(lax.ppermute(near, 'sy', up + down))  3.88 us
    ppermute x1, waiting for transfers between devices, per_device(): lax.ppermute(line, 'sx', [(i + ROW, i) for i in range(count_x - ROW)])  3.75 us
    pallas_call x1, Pallas kernels, per_device(): pl.pallas_call(self_kernel, out_shape=shape(72, cz), scratch_shapes=[pltp...  3.24 us
  transfers between devices with their start and end apart: 8, of which 5 were waited for; matrix products, arithmetic and copies ran while one was open for 2% of the time, Pallas kernels for 5%

profile of v4, /device:TPU:49, one launch (start us, length us, event | category | flops | bytes accessed | tf_op | source)
XLA Modules:
  0.0 70.7 jit_solution(11225395774260333127)
XLA Ops:
  0.6 0.0 copy-start.1
  0.6 0.9 %slice_bitcast_fusion = (f32[8,16,128]{2,1,0:T(8,128)S(1)}, f32[8,16,128]{2,1,0:T(8,128)S(1)}) fusion(f32[8,16,16,128]{3,2,1,0:T(8,128)} %vec_ref.1), kind=kLoop, calls=%fused_computation.4 | loop fusion | bytes 262144 | tf_op jit(solution)/shard_map/squeeze | solution.py:288
  1.6 0.0 copy-done.1
  1.6 3.1 %collective-permute-start = (f32[9,16,128]{2,1,0:T(8,128)S(1)}, f32[9,16,128]{2,1,0:T(8,128)S(1)}, u32[]{:S(2)}, u32[]{:S(2)}) collective-permute-start(f32[9,16,128]{2,1,0:T(8,128)S(1)} %pad_maximum_fusion.2), channel_id=1, source_target_pairs={{0,16},{16,32},{32,48},{48,64},{64,80},{80,96},{96,112},{112,128},... | collective-permute-start | bytes 221192 | tf_op jit(solution)/shard_map/ppermute | solution.py:290
  4.7 1.3 %fusion = (f32[8,16,1,128]{3,2,1,0:T(1,128)S(1)}, f32[8,16,1,128]{3,2,1,0:T(1,128)S(1)}) fusion(f32[8,16,16,128]{3,2,1,0:T(8,128)} %vec_ref.1), kind=kLoop, calls=%fused_computation.9 | loop fusion | bytes 262144 | tf_op jit(solution)/shard_map/slice | solution.py:289
  6.0 0.0 copy-start.2
  6.1 5.9 %collective-permute-start.1 = (f32[9,16,128]{2,1,0:T(8,128)S(1)}, f32[9,16,128]{2,1,0:T(8,128)S(1)}, u32[]{:S(2)}, u32[]{:S(2)}) collective-permute-start(f32[9,16,128]{2,1,0:T(8,128)S(1)} %pad_maximum_fusion.3), channel_id=1, source_target_pairs={{0,1},{1,2},{2,3},{3,4},{4,5},{5,6},{6,7},{7,8},{8,9},{9,10},{10,1... | collective-permute-start | bytes 221192 | tf_op jit(solution)/shard_map/ppermute | solution.py:291
  12.0 0.0 copy-done.2
  12.0 0.0 copy-start
  12.0 1.2 %copy-done = f32[8,16,16,128]{3,2,1,0:T(8,128)S(1)} copy-done((f32[8,16,16,128]{3,2,1,0:T(8,128)S(1)}, f32[8,16,16,128]{3,2,1,0:T(8,128)}, u32[]{:S(2)}) %copy-start) | copy-done | bytes 1048600
  13.2 3.2 %own_block.1.self_ref = f32[72,128]{1,0:T(8,128)S(1)} custom-call(f32[16,16,128]{2,1,0:T(8,128)S(1)} %copy-done.1, f32[8,16,16,128]{3,2,1,0:T(8,128)S(1)} %copy-done, f32[16,16,128]{2,1,0:T(8,128)S(1)} %copy-done.2), custom_call_target="tpu_custom_call" | custom-call | flops 10000000 | bytes 1400000 | tf_op jit(solution)/shard_map/own_block/pallas_call | solution.py:295
  16.5 0.0 collective-permute-done.below_x_ref
  16.5 0.0 collective-permute-done.1.below_y_ref
  16.5 0.5 face_blocks.1
  17.0 13.1 %all_to_all.5.line_ref = f32[16,1,256]{2,1,0:T(1,128)S(1)} all-to-all(f32[16,1,256]{2,1,0:T(1,128)S(1)} %face_blocks.1), channel_id=1, replica_groups={{0,1,16,17,32,33,48,49,64,65,80,81,96,97,112,113},{2,3,18,19,34,35,50,5..., dimensions={0} | all-to-all | bytes 32768 | tf_op jit(solution)/shard_map/all_to_all | solution.py:320
  30.1 4.5 %collective-permute-start.2 = (f32[16,1,256]{2,1,0:T(1,128)S(1)}, f32[16,1,256]{2,1,0:T(1,128)S(1)}, u32[]{:S(2)}, u32[]{:S(2)}) collective-permute-start(f32[16,1,256]{2,1,0:T(1,128)S(1)} %all_to_all.5.line_ref), channel_id=1, source_target_pairs={{0,128},{16,144},{32,160},{48,176},{64,192},{80,208},{96,224},{112... | collective-permute-start | bytes 49160 | tf_op jit(solution)/shard_map/ppermute | solution.py:321
  34.7 1.9 %collective-permute-start.3 = (f32[16,1,256]{2,1,0:T(1,128)S(1)}, f32[16,1,256]{2,1,0:T(1,128)S(1)}, u32[]{:S(2)}, u32[]{:S(2)}) collective-permute-start(f32[16,1,256]{2,1,0:T(1,128)S(1)} %all_to_all.5.line_ref), channel_id=1, source_target_pairs={{128,0},{144,16},{160,32},{176,48},{192,64},{208,80},{224,96},{240... | collective-permute-start | bytes 49160 | tf_op jit(solution)/shard_map/ppermute | solution.py:322
  36.6 0.0 collective-permute-done.2.lower_ref
  36.6 3.8 %collective-permute-done.3.upper_ref = f32[16,1,256]{2,1,0:T(1,128)S(1)} collective-permute-done((f32[16,1,256]{2,1,0:T(1,128)S(1)}, f32[16,1,256]{2,1,0:T(1,128)S(1)}, u32[]{:S(2)}, u32[]{:S(2)}) %collective-permute-start.3) | collective-permute-done | bytes 16416 | tf_op jit(solution)/shard_map/ppermute | solution.py:322
  40.3 0.1 window.1.near_ref
  40.4 1.3 %collective-permute-start.4 = (f32[2,16,256]{2,1,0:T(8,128)S(1)}, f32[2,16,256]{2,1,0:T(8,128)S(1)}, u32[]{:S(2)}, u32[]{:S(2)}) collective-permute-start(f32[2,16,256]{2,1,0:T(8,128)S(1)} %window.1.near_ref), channel_id=1, source_target_pairs={{0,2},{2,4},{4,6},{6,8},{8,10},{10,12},{12,14},{3,1},{5,3},{7,5},{... | collective-permute-start | bytes 98312 | tf_op jit(solution)/shard_map/ppermute | solution.py:334
  41.7 1.3 %collective-permute-start.5 = (f32[2,16,256]{2,1,0:T(8,128)S(1)}, f32[2,16,256]{2,1,0:T(8,128)S(1)}, u32[]{:S(2)}, u32[]{:S(2)}) collective-permute-start(f32[2,16,256]{2,1,0:T(8,128)S(1)} %window.1.near_ref), channel_id=1, source_target_pairs={{0,4},{2,6},{4,8},{6,10},{8,12},{10,14},{5,1},{7,3},{9,5},{11,7},{... | collective-permute-start | bytes 98312 | tf_op jit(solution)/shard_map/ppermute | solution.py:334
  43.0 1.3 %collective-permute-start.6 = (f32[2,16,256]{2,1,0:T(8,128)S(1)}, f32[2,16,256]{2,1,0:T(8,128)S(1)}, u32[]{:S(2)}, u32[]{:S(2)}) collective-permute-start(f32[2,16,256]{2,1,0:T(8,128)S(1)} %window.1.near_ref), channel_id=1, source_target_pairs={{0,6},{2,8},{4,10},{6,12},{8,14},{7,1},{9,3},{11,5},{13,7},{15,9},... | collective-permute-start | bytes 98312 | tf_op jit(solution)/shard_map/ppermute | solution.py:334
  44.3 2.3 %collective-permute-done.4 = f32[2,16,256]{2,1,0:T(8,128)S(1)} collective-permute-done((f32[2,16,256]{2,1,0:T(8,128)S(1)}, f32[2,16,256]{2,1,0:T(8,128)S(1)}, u32[]{:S(2)}, u32[]{:S(2)}) %collective-permute-start.4) | collective-permute-done | bytes 32800 | tf_op jit(solution)/shard_map/ppermute | solution.py:334
  46.6 4.6 %collective-permute-done.5 = f32[2,16,256]{2,1,0:T(8,128)S(1)} collective-permute-done((f32[2,16,256]{2,1,0:T(8,128)S(1)}, f32[2,16,256]{2,1,0:T(8,128)S(1)}, u32[]{:S(2)}, u32[]{:S(2)}) %collective-permute-start.5) | collective-permute-done | bytes 32800 | tf_op jit(solution)/shard_map/ppermute | solution.py:334
  51.3 5.9 %collective-permute-done.6 = f32[2,16,256]{2,1,0:T(8,128)S(1)} collective-permute-done((f32[2,16,256]{2,1,0:T(8,128)S(1)}, f32[2,16,256]{2,1,0:T(8,128)S(1)}, u32[]{:S(2)}, u32[]{:S(2)}) %collective-permute-start.6) | collective-permute-done | bytes 32800 | tf_op jit(solution)/shard_map/ppermute | solution.py:334
  57.2 10.8 %collective-permute-start.7 = (f32[6,16,256]{2,1,0:T(8,128)S(1)}, f32[6,16,256]{2,1,0:T(8,128)S(1)}, u32[]{:S(2)}, u32[]{:S(2)}) collective-permute-start(f32[6,16,256]{2,1,0:T(8,128)S(1)} %constant_dynamic-update-slice_fusion.mine_ref), channel_id=1, source_target_pairs={{0,1},{1,0},{2,3},{3,2},{4,5},{5,4},{6,7},{7,6},{8,9},{9,8},{10,11... | collective-permute-start | bytes 294920 | tf_op jit(solution)/shard_map/ppermute | solution.py:337
  68.0 0.9 %collective-permute-done.7.other_ref = f32[6,16,256]{2,1,0:T(8,128)S(1)} collective-permute-done((f32[6,16,256]{2,1,0:T(8,128)S(1)}, f32[6,16,256]{2,1,0:T(8,128)S(1)}, u32[]{:S(2)}, u32[]{:S(2)}) %collective-permute-start.7) | collective-permute-done | bytes 98336 | tf_op jit(solution)/shard_map/ppermute | solution.py:337
  68.9 1.8 %coarse_sweeps.1 = (f32[5,8,8]{2,1,0:T(8,128)}, f32[1,8]{1,0:T(1,128)}) custom-call(f32[2,16,256]{2,1,0:T(8,128)S(1)} %window.1.near_ref, f32[6,16,256]{2,1,0:T(8,128)S(1)} %constant_dynamic-update-slice_fusion.mine_ref, f32[6,16,256]{2,1,0:T(8,128)S(1)} %collective-permute-done.7.other_ref), custom_call_target="tpu_custom_call" | custom-call | tf_op jit(solution)/shard_map/coarse_sweeps/pallas_call | solution.py:338
  (8 shorter events, 0.1 us)
Async XLA Ops:
  0.6 1.0 %copy-start.1 = (f32[16,16,128]{2,1,0:T(8,128)S(1)}, f32[16,16,128]{2,1,0:T(8,128)}, u32[]{:S(2)}) copy-start(f32[16,16,128]{2,1,0:T(8,128)} %rate_ref.1) | copy-start | bytes 393220
  1.6 14.9 %collective-permute-start = (f32[9,16,128]{2,1,0:T(8,128)S(1)}, f32[9,16,128]{2,1,0:T(8,128)S(1)}, u32[]{:S(2)}, u32[]{:S(2)}) collective-permute-start(f32[9,16,128]{2,1,0:T(8,128)S(1)} %pad_maximum_fusion.2), channel_id=1, source_target_pairs={{0,16},{16,32},{32,48},{48,64},{64,80},{80,96},{96,112},{112,128},... | collective-permute-start | bytes 221192 | tf_op jit(solution)/shard_map/ppermute | solution.py:290
  6.0 5.9 %copy-start.2 = (f32[16,16,128]{2,1,0:T(8,128)S(1)}, f32[16,16,128]{2,1,0:T(8,128)}, u32[]{:S(2)}) copy-start(f32[16,16,128]{2,1,0:T(8,128)} %res_ref.1) | copy-start | bytes 393220
  6.1 10.4 %collective-permute-start.1 = (f32[9,16,128]{2,1,0:T(8,128)S(1)}, f32[9,16,128]{2,1,0:T(8,128)S(1)}, u32[]{:S(2)}, u32[]{:S(2)}) collective-permute-start(f32[9,16,128]{2,1,0:T(8,128)S(1)} %pad_maximum_fusion.3), channel_id=1, source_target_pairs={{0,1},{1,2},{2,3},{3,4},{4,5},{5,6},{6,7},{7,8},{8,9},{9,10},{10,1... | collective-permute-start | bytes 221192 | tf_op jit(solution)/shard_map/ppermute | solution.py:291
  12.0 1.2 %copy-start = (f32[8,16,16,128]{3,2,1,0:T(8,128)S(1)}, f32[8,16,16,128]{3,2,1,0:T(8,128)}, u32[]{:S(2)}) copy-start(f32[8,16,16,128]{3,2,1,0:T(8,128)} %vec_ref.1) | copy-start | bytes 3145732
  30.1 6.5 %collective-permute-start.2 = (f32[16,1,256]{2,1,0:T(1,128)S(1)}, f32[16,1,256]{2,1,0:T(1,128)S(1)}, u32[]{:S(2)}, u32[]{:S(2)}) collective-permute-start(f32[16,1,256]{2,1,0:T(1,128)S(1)} %all_to_all.5.line_ref), channel_id=1, source_target_pairs={{0,128},{16,144},{32,160},{48,176},{64,192},{80,208},{96,224},{112... | collective-permute-start | bytes 49160 | tf_op jit(solution)/shard_map/ppermute | solution.py:321
  34.7 5.7 %collective-permute-start.3 = (f32[16,1,256]{2,1,0:T(1,128)S(1)}, f32[16,1,256]{2,1,0:T(1,128)S(1)}, u32[]{:S(2)}, u32[]{:S(2)}) collective-permute-start(f32[16,1,256]{2,1,0:T(1,128)S(1)} %all_to_all.5.line_ref), channel_id=1, source_target_pairs={{128,0},{144,16},{160,32},{176,48},{192,64},{208,80},{224,96},{240... | collective-permute-start | bytes 49160 | tf_op jit(solution)/shard_map/ppermute | solution.py:322
  40.4 6.2 %collective-permute-start.4 = (f32[2,16,256]{2,1,0:T(8,128)S(1)}, f32[2,16,256]{2,1,0:T(8,128)S(1)}, u32[]{:S(2)}, u32[]{:S(2)}) collective-permute-start(f32[2,16,256]{2,1,0:T(8,128)S(1)} %window.1.near_ref), channel_id=1, source_target_pairs={{0,2},{2,4},{4,6},{6,8},{8,10},{10,12},{12,14},{3,1},{5,3},{7,5},{... | collective-permute-start | bytes 98312 | tf_op jit(solution)/shard_map/ppermute | solution.py:334
  41.7 9.6 %collective-permute-start.5 = (f32[2,16,256]{2,1,0:T(8,128)S(1)}, f32[2,16,256]{2,1,0:T(8,128)S(1)}, u32[]{:S(2)}, u32[]{:S(2)}) collective-permute-start(f32[2,16,256]{2,1,0:T(8,128)S(1)} %window.1.near_ref), channel_id=1, source_target_pairs={{0,4},{2,6},{4,8},{6,10},{8,12},{10,14},{5,1},{7,3},{9,5},{11,7},{... | collective-permute-start | bytes 98312 | tf_op jit(solution)/shard_map/ppermute | solution.py:334
  43.0 14.1 %collective-permute-start.6 = (f32[2,16,256]{2,1,0:T(8,128)S(1)}, f32[2,16,256]{2,1,0:T(8,128)S(1)}, u32[]{:S(2)}, u32[]{:S(2)}) collective-permute-start(f32[2,16,256]{2,1,0:T(8,128)S(1)} %window.1.near_ref), channel_id=1, source_target_pairs={{0,6},{2,8},{4,10},{6,12},{8,14},{7,1},{9,3},{11,5},{13,7},{15,9},... | collective-permute-start | bytes 98312 | tf_op jit(solution)/shard_map/ppermute | solution.py:334
  57.2 11.8 %collective-permute-start.7 = (f32[6,16,256]{2,1,0:T(8,128)S(1)}, f32[6,16,256]{2,1,0:T(8,128)S(1)}, u32[]{:S(2)}, u32[]{:S(2)}) collective-permute-start(f32[6,16,256]{2,1,0:T(8,128)S(1)} %constant_dynamic-update-slice_fusion.mine_ref), channel_id=1, source_target_pairs={{0,1},{1,0},{2,3},{3,2},{4,5},{5,4},{6,7},{7,6},{8,9},{9,8},{10,11... | collective-permute-start | bytes 294920 | tf_op jit(solution)/shard_map/ppermute | solution.py:337

commit v5 on v3

--- a/solution.py
+++ b/solution.py
@@ -158,25 +158,28 @@
     out_ref[...] = jnp.broadcast_to(message[None], out_ref.shape)
 
 
-def solve_kernel(got_ref, blocks_ref, coarse_ref, table_ref):
-    count_y, window, words = got_ref.shape
-    lanes = count_y * window
+def solve_kernel(lower_ref, line_ref, upper_ref, blocks_ref, coarse_ref, rows_ref, table_ref):
+    count_y, words = line_ref.shape[1:]
+    lanes = WINDOW * count_y
     index_x, index_y = lax.axis_index("sx"), lax.axis_index("sy")
-    place = ROW + index_x % ROW - window_start(index_x, lax.axis_size("sx"))
-    table_ref[...] = got_ref[...].reshape(lanes, words).T
+    start = window_start(index_x, lax.axis_size("sx"))
+    place = ROW + index_x % ROW - start
+    for part, ref in enumerate((lower_ref, line_ref, upper_ref)):
+        rows_ref[pl.ds(part * ROW, ROW)] = ref[...]
+    table_ref[...] = rows_ref[pl.ds(start, WINDOW)].reshape(lanes, words).T
     lane = lax.broadcasted_iota(jnp.int32, (1, lanes), 1)
     row = lax.broadcasted_iota(jnp.int32, (NVEC, lanes), 0)
-    has_x = lane % window < window - 1
-    has_y = lane < lanes - window
+    has_x = lane < lanes - count_y
+    has_y = lane % count_y < count_y - 1
 
     def columns(base, count=NVEC):
         return [table_ref[pl.ds(base + b * NVEC, NVEC), :] for b in range(count)]
 
     def from_x(value):
-        return jnp.where(has_x, pltpu.roll(value, lanes - 1, 1), 0.0)
+        return jnp.where(has_x, pltpu.roll(value, lanes - count_y, 1), 0.0)
 
     def from_y(value):
-        return jnp.where(has_y, pltpu.roll(value, lanes - window, 1), 0.0)
+        return jnp.where(has_y, pltpu.roll(value, lanes - 1, 1), 0.0)
 
     def product(matrix, vector):
         terms = [matrix[b] * vector[b : b + 1] for b in range(NVEC)]
@@ -217,11 +220,11 @@
     coarse = OMEGA * product(inverse, right)
     for _ in range(ITERS - 1):
         remainder = right - product(own, coarse)
-        remainder = remainder - product(xlo, pltpu.roll(coarse, 1, 1)) - from_x(product(xlo_t, coarse))
-        remainder = remainder - product(ylo, pltpu.roll(coarse, window, 1)) - from_y(product(ylo_t, coarse))
+        remainder = remainder - product(xlo, pltpu.roll(coarse, count_y, 1)) - from_x(product(xlo_t, coarse))
+        remainder = remainder - product(ylo, pltpu.roll(coarse, 1, 1)) - from_y(product(ylo_t, coarse))
         coarse = coarse + OMEGA * product(inverse, remainder)
 
-    here = (lane == index_y * window + place).astype(jnp.float32)
+    here = (lane == place * count_y + index_y).astype(jnp.float32)
     results = jnp.concatenate(
         own + xlo + [from_x(m) for m in xlo_t] + ylo + [from_y(m) for m in ylo_t] + [coarse], axis=0
     )
@@ -249,16 +252,6 @@
     low = jnp.where(chip_row > 0, 0, ROW)
     high = jnp.where(chip_row < count // ROW - 1, 3 * ROW, 2 * ROW) - WINDOW
     return jnp.clip(ROW + index % ROW - WINDOW // 2, low, high)
-
-
-def window_kernel(lower_ref, line_ref, upper_ref, out_ref, rows_ref, near_ref):
-    start = window_start(lax.axis_index("sx"), lax.axis_size("sx"))
-    for part, ref in enumerate((lower_ref, line_ref, upper_ref)):
-        for i in range(ROW):
-            rows_ref[pl.ds(part * ROW + i, 1), :] = ref[i]
-    for i in range(WINDOW):
-        near_ref[pl.ds(i, 1), :] = rows_ref[pl.ds(start + i, 1), :]
-    out_ref[...] = jnp.broadcast_to(near_ref[...][None], out_ref.shape)
 
 
 def shape(*dims):
@@ -288,30 +281,28 @@
     )(strain_rate, deflation, residual)
     messages = pl.pallas_call(
         face_kernel,
-        out_shape=shape(ROW, 1, WORDS),
+        out_shape=shape(count_y, 1, WORDS),
         scratch_shapes=[pltpu.VMEM((WORDS, cz), jnp.float32)],
         compiler_params=PARAMS,
         name="face_blocks",
     )(own_rows, first_x, first_y, below_x, below_y)
+    across = lax.all_to_all(messages, "sy", 0, 0).reshape(count_y, WORDS)
     rows = [[ROW * g + i for i in range(ROW)] for g in range(count_x // ROW)]
-    line = lax.all_to_all(messages, "sx", 0, 0, axis_index_groups=rows)
+    line = lax.all_to_all(
+        jnp.broadcast_to(across, (ROW, count_y, WORDS)), "sx", 0, 0, axis_index_groups=rows
+    )
     lower = lax.ppermute(line, "sx", [(i, i + ROW) for i in range(count_x - ROW)])
     upper = lax.ppermute(line, "sx", [(i + ROW, i) for i in range(count_x - ROW)])
-    near = pl.pallas_call(
-        window_kernel,
-        out_shape=shape(count_y, WINDOW, WORDS),
-        scratch_shapes=[pltpu.VMEM((3 * ROW, WORDS), jnp.float32), pltpu.VMEM((WINDOW, WORDS), jnp.float32)],
-        compiler_params=PARAMS,
-        name="window",
-    )(lower, line, upper)
-    got = lax.all_to_all(near, "sy", 0, 0)
     blocks, coarse = pl.pallas_call(
         solve_kernel,
         out_shape=(shape(5, NVEC, NVEC), shape(1, NVEC)),
-        scratch_shapes=[pltpu.VMEM((WORDS, count_y * WINDOW), jnp.float32)],
+        scratch_shapes=[
+            pltpu.VMEM((3 * ROW, count_y, WORDS), jnp.float32),
+            pltpu.VMEM((WORDS, count_y * WINDOW), jnp.float32),
+        ],
         compiler_params=PARAMS,
         name="coarse_sweeps",
-    )(got)
+    )(lower, line, upper)
     return (blocks.reshape(1, 1, 5, NVEC, NVEC), coarse.reshape(1, 1, NVEC))
 
 

time: 67.8 us -> 68.9 us (1.016)
  the two profiles are of different devices: /device:TPU:65 before, /device:TPU:48 now
where the time goes in v5:
time: 68.9 us; the launch traced here: 68.6 us
  blocking collectives  40.8 us (59%)
  starting transfers between devices  11.7 us (17%)
  waiting for transfers between devices  6.15 us (9%)
  Pallas kernels  5.56 us (8%)
  local copies, waits for them, and re-layouts  3.51 us (5%)
  between operations  0.75 us (1%)
    all_to_all x1, blocking collectives, per_device(): across = lax.all_to_all(messages, 'sy', 0, 0).reshape(count_y, WORDS)  25.8 us
    all_to_all x1, blocking collectives, per_device(): lax.all_to_all(jnp.broadcast_to(across, (ROW, count_y, WORDS)), 'sx', 0,...  15 us
    ppermute x1, waiting for transfers between devices, per_device(): lax.ppermute(line, 'sx', [(i + ROW, i) for i in range(count_x - ROW)])  5.57 us
    ppermute x1, starting transfers between devices, per_device(): lax.ppermute(line, 'sx', [(i, i + ROW) for i in range(count_x - ROW)])  4.8 us
    ppermute x1, starting transfers between devices, per_device(): lax.ppermute(last_x, 'sx', [(i, i + 1) for i in range(count_x - 1)])  3.4 us
    pallas_call x1, Pallas kernels, per_device(): pl.pallas_call(self_kernel, out_shape=shape(72, cz), scratch_shapes=[pltp...  3.24 us
    ppermute x1, starting transfers between devices, per_device(): lax.ppermute(line, 'sx', [(i + ROW, i) for i in range(count_x - ROW)])  1.92 us
    pallas_call x1, Pallas kernels, per_device(): pl.pallas_call(solve_kernel, out_shape=(shape(5, NVEC, NVEC), shape(1, NV...  1.81 us
  transfers between devices with their start and end apart: 4, of which 2 were waited for; matrix products, arithmetic and copies ran while one was open for 2% of the time, Pallas kernels for 5%

profile of v5, /device:TPU:48, one launch (start us, length us, event | category | flops | bytes accessed | tf_op | source)
XLA Modules:
  0.0 68.6 jit_solution(10982922621494714047)
XLA Ops:
  0.6 0.0 copy-start.1
  0.6 0.9 %slice_bitcast_fusion = (f32[8,16,128]{2,1,0:T(8,128)S(1)}, f32[8,16,128]{2,1,0:T(8,128)S(1)}) fusion(f32[8,16,16,128]{3,2,1,0:T(8,128)} %vec_ref.1), kind=kLoop, calls=%fused_computation.4 | loop fusion | bytes 262144 | tf_op jit(solution)/shard_map/squeeze | solution.py:263
  1.6 0.0 copy-done.1
  1.6 3.4 %collective-permute-start = (f32[9,16,128]{2,1,0:T(8,128)S(1)}, f32[9,16,128]{2,1,0:T(8,128)S(1)}, u32[]{:S(2)}, u32[]{:S(2)}) collective-permute-start(f32[9,16,128]{2,1,0:T(8,128)S(1)} %pad_maximum_fusion.2), channel_id=1, source_target_pairs={{0,16},{16,32},{32,48},{48,64},{64,80},{80,96},{96,112},{112,128},... | collective-permute-start | bytes 221192 | tf_op jit(solution)/shard_map/ppermute | solution.py:265
  5.0 1.3 %fusion = (f32[8,16,1,128]{3,2,1,0:T(1,128)S(1)}, f32[8,16,1,128]{3,2,1,0:T(1,128)S(1)}) fusion(f32[8,16,16,128]{3,2,1,0:T(8,128)} %vec_ref.1), kind=kLoop, calls=%fused_computation.7 | loop fusion | bytes 262144 | tf_op jit(solution)/shard_map/slice | solution.py:264
  6.3 0.0 copy-start.2
  6.4 1.6 %collective-permute-start.1 = (f32[9,16,128]{2,1,0:T(8,128)S(1)}, f32[9,16,128]{2,1,0:T(8,128)S(1)}, u32[]{:S(2)}, u32[]{:S(2)}) collective-permute-start(f32[9,16,128]{2,1,0:T(8,128)S(1)} %pad_maximum_fusion.3), channel_id=1, source_target_pairs={{0,1},{1,2},{2,3},{3,4},{4,5},{5,6},{6,7},{7,8},{8,9},{9,10},{10,1... | collective-permute-start | bytes 221192 | tf_op jit(solution)/shard_map/ppermute | solution.py:266
  8.0 0.0 copy-done.2
  8.0 0.0 copy-start
  8.0 1.2 %copy-done = f32[8,16,16,128]{3,2,1,0:T(8,128)S(1)} copy-done((f32[8,16,16,128]{3,2,1,0:T(8,128)S(1)}, f32[8,16,16,128]{3,2,1,0:T(8,128)}, u32[]{:S(2)}) %copy-start) | copy-done | bytes 1048600
  9.2 3.2 %own_block.1.self_ref = f32[72,128]{1,0:T(8,128)S(1)} custom-call(f32[16,16,128]{2,1,0:T(8,128)S(1)} %copy-done.1, f32[8,16,16,128]{3,2,1,0:T(8,128)S(1)} %copy-done, f32[16,16,128]{2,1,0:T(8,128)S(1)} %copy-done.2), custom_call_target="tpu_custom_call" | custom-call | flops 10000000 | bytes 1400000 | tf_op jit(solution)/shard_map/own_block/pallas_call | solution.py:270
  12.5 0.0 collective-permute-done.below_x_ref
  12.5 0.0 collective-permute-done.1.below_y_ref
  12.5 0.5 face_blocks.1
  13.0 25.8 %all_to_all.10 = f32[16,1,256]{2,1,0:T(1,128)S(1)} all-to-all(f32[16,1,256]{2,1,0:T(1,128)S(1)} %face_blocks.1), channel_id=1, replica_groups=mesh['sx'=64,'sy'=16] {'sy'}, dimensions={0} | all-to-all | bytes 32768 | tf_op jit(solution)/shard_map/all_to_all | solution.py:289
  38.9 15.0 %all_to_all.11.line_ref = f32[8,16,256]{2,1,0:T(8,128)S(1)} all-to-all(f32[8,16,256]{2,1,0:T(8,128)S(1)} %broadcast_in_dim.3), channel_id=1, replica_groups={{0,16,32,48,64,80,96,112},{128,144,160,176,192,208,224,240},{256,272,28..., dimensions={0} | all-to-all | bytes 262144 | tf_op jit(solution)/shard_map/all_to_all | solution.py:291
  53.9 4.8 %collective-permute-start.2 = (f32[8,16,256]{2,1,0:T(8,128)S(1)}, f32[8,16,256]{2,1,0:T(8,128)S(1)}, u32[]{:S(2)}, u32[]{:S(2)}) collective-permute-start(f32[8,16,256]{2,1,0:T(8,128)S(1)} %all_to_all.11.line_ref), channel_id=1, source_target_pairs={{0,128},{16,144},{32,160},{48,176},{64,192},{80,208},{96,224},{112... | collective-permute-start | bytes 393224 | tf_op jit(solution)/shard_map/ppermute | solution.py:294
  58.7 1.9 %collective-permute-start.3 = (f32[8,16,256]{2,1,0:T(8,128)S(1)}, f32[8,16,256]{2,1,0:T(8,128)S(1)}, u32[]{:S(2)}, u32[]{:S(2)}) collective-permute-start(f32[8,16,256]{2,1,0:T(8,128)S(1)} %all_to_all.11.line_ref), channel_id=1, source_target_pairs={{128,0},{144,16},{160,32},{176,48},{192,64},{208,80},{224,96},{240... | collective-permute-start | bytes 393224 | tf_op jit(solution)/shard_map/ppermute | solution.py:295
  60.6 0.6 collective-permute-done.2.lower_ref
  61.2 5.6 %collective-permute-done.3.upper_ref = f32[8,16,256]{2,1,0:T(8,128)S(1)} collective-permute-done((f32[8,16,256]{2,1,0:T(8,128)S(1)}, f32[8,16,256]{2,1,0:T(8,128)S(1)}, u32[]{:S(2)}, u32[]{:S(2)}) %collective-permute-start.3) | collective-permute-done | bytes 131104 | tf_op jit(solution)/shard_map/ppermute | solution.py:295
  66.7 1.8 %coarse_sweeps.1 = (f32[5,8,8]{2,1,0:T(8,128)}, f32[1,8]{1,0:T(1,128)}) custom-call(f32[8,16,256]{2,1,0:T(8,128)S(1)} %collective-permute-done.2.lower_ref, f32[8,16,256]{2,1,0:T(8,128)S(1)} %all_to_all.11.line_ref, f32[8,16,256]{2,1,0:T(8,128)S(1)} %collective-permute-done.3.upper_ref), custom_call_target="tpu_custom_call" | custom-call | tf_op jit(solution)/shard_map/coarse_sweeps/pallas_call | solution.py:296
  (7 shorter events, 0.1 us)
Async XLA Ops:
  0.6 1.0 %copy-start.1 = (f32[16,16,128]{2,1,0:T(8,128)S(1)}, f32[16,16,128]{2,1,0:T(8,128)}, u32[]{:S(2)}) copy-start(f32[16,16,128]{2,1,0:T(8,128)} %rate_ref.1) | copy-start | bytes 393220
  1.6 10.9 %collective-permute-start = (f32[9,16,128]{2,1,0:T(8,128)S(1)}, f32[9,16,128]{2,1,0:T(8,128)S(1)}, u32[]{:S(2)}, u32[]{:S(2)}) collective-permute-start(f32[9,16,128]{2,1,0:T(8,128)S(1)} %pad_maximum_fusion.2), channel_id=1, source_target_pairs={{0,16},{16,32},{32,48},{48,64},{64,80},{80,96},{96,112},{112,128},... | collective-permute-start | bytes 221192 | tf_op jit(solution)/shard_map/ppermute | solution.py:265
  6.3 1.7 %copy-start.2 = (f32[16,16,128]{2,1,0:T(8,128)S(1)}, f32[16,16,128]{2,1,0:T(8,128)}, u32[]{:S(2)}) copy-start(f32[16,16,128]{2,1,0:T(8,128)} %res_ref.1) | copy-start | bytes 393220
  6.4 6.1 %collective-permute-start.1 = (f32[9,16,128]{2,1,0:T(8,128)S(1)}, f32[9,16,128]{2,1,0:T(8,128)S(1)}, u32[]{:S(2)}, u32[]{:S(2)}) collective-permute-start(f32[9,16,128]{2,1,0:T(8,128)S(1)} %pad_maximum_fusion.3), channel_id=1, source_target_pairs={{0,1},{1,2},{2,3},{3,4},{4,5},{5,6},{6,7},{7,8},{8,9},{9,10},{10,1... | collective-permute-start | bytes 221192 | tf_op jit(solution)/shard_map/ppermute | solution.py:266
  8.0 1.2 %copy-start = (f32[8,16,16,128]{3,2,1,0:T(8,128)S(1)}, f32[8,16,16,128]{3,2,1,0:T(8,128)}, u32[]{:S(2)}) copy-start(f32[8,16,16,128]{3,2,1,0:T(8,128)} %vec_ref.1) | copy-start | bytes 3145732
  53.9 7.3 %collective-permute-start.2 = (f32[8,16,256]{2,1,0:T(8,128)S(1)}, f32[8,16,256]{2,1,0:T(8,128)S(1)}, u32[]{:S(2)}, u32[]{:S(2)}) collective-permute-start(f32[8,16,256]{2,1,0:T(8,128)S(1)} %all_to_all.11.line_ref), channel_id=1, source_target_pairs={{0,128},{16,144},{32,160},{48,176},{64,192},{80,208},{96,224},{112... | collective-permute-start | bytes 393224 | tf_op jit(solution)/shard_map/ppermute | solution.py:294
  58.7 8.1 %collective-permute-start.3 = (f32[8,16,256]{2,1,0:T(8,128)S(1)}, f32[8,16,256]{2,1,0:T(8,128)S(1)}, u32[]{:S(2)}, u32[]{:S(2)}) collective-permute-start(f32[8,16,256]{2,1,0:T(8,128)S(1)} %all_to_all.11.line_ref), channel_id=1, source_target_pairs={{128,0},{144,16},{160,32},{176,48},{192,64},{208,80},{224,96},{240... | collective-permute-start | bytes 393224 | tf_op jit(solution)/shard_map/ppermute | solution.py:295

commit v6 on v3

--- a/solution.py
+++ b/solution.py
@@ -13,6 +13,8 @@
 
 PACKED, TRIANGLE, X_DIAG, Y_DIAG, XLO, YLO, RHS, WORDS = (0, 64, 96, 104, 112, 176, 240, 256)
 WINDOW = 16
+CHUNK = 4
+CHUNKS = 4
 ROW = 8
 PARAMS = pltpu.CompilerParams(vmem_limit_bytes=32 * 1024 * 1024)
 
@@ -41,7 +43,12 @@
     return x[:8] + x[8:]
 
 
-def self_kernel(rate_ref, vec_ref, res_ref, out_ref, visc_ref, acc_ref, rhs_ref):
+def self_kernel(rate_ref, far_ref, res_ref, out_ref, vec_ref, visc_ref, acc_ref, rhs_ref, sems):
+    copies = []
+    for k in range(CHUNKS):
+        part = (slice(None), pl.ds(k * CHUNK, CHUNK))
+        copies.append(pltpu.make_async_copy(far_ref.at[part], vec_ref.at[part], sems.at[k]))
+        copies[k].start()
     at_top_x = lax.axis_index("sx") == lax.axis_size("sx") - 1
     at_top_y = lax.axis_index("sy") == lax.axis_size("sy") - 1
     visc_ref[...] = viscosity(rate_ref[...])
@@ -53,8 +60,7 @@
     top_x = jnp.where(at_top_x, 1.0, 0.5)
     top_y = jnp.where(at_top_y, 1.0, 0.5)
 
-    @pl.loop(0, cx)
-    def _(i):
+    def layer(i):
         visc = visc_ref[i]
         after = visc_ref[jnp.minimum(i + 1, cx - 1)]
         before = visc_ref[jnp.maximum(i - 1, 0)]
@@ -87,6 +93,12 @@
             for a in range(NVEC):
                 acc_ref[b * NVEC + a] += halves(vectors[a] * image)
 
+    copies[0].wait()
+    for k in range(CHUNKS):
+        if k + 1 < CHUNKS:
+            copies[k + 1].wait()
+        pl.loop(k * CHUNK, (k + 1) * CHUNK, unroll=2)(layer)
+
     for b in range(NVEC):
         out_ref[pl.ds(b * NVEC, NVEC), :] = fold(
             [acc_ref[b * NVEC + a] + acc_ref[a * NVEC + b] for a in range(NVEC)]
@@ -277,12 +289,19 @@
     own_rows = pl.pallas_call(
         self_kernel,
         out_shape=shape(72, cz),
+        in_specs=[
+            pl.BlockSpec(memory_space=pltpu.VMEM),
+            pl.BlockSpec(memory_space=pltpu.HBM),
+            pl.BlockSpec(memory_space=pltpu.VMEM),
+        ],
         scratch_shapes=[
+            pltpu.VMEM(deflation.shape, jnp.float32),
             pltpu.VMEM(strain_rate.shape, jnp.float32),
             pltpu.VMEM((64, 8, cz), jnp.float32),
             pltpu.VMEM((NVEC, 8, cz), jnp.float32),
+            pltpu.SemaphoreType.DMA((CHUNKS,)),
         ],
-        compiler_params=PARAMS,
+        compiler_params=pltpu.CompilerParams(vmem_limit_bytes=60 * 1024 * 1024),
         cost_estimate=pl.CostEstimate(flops=10000000, bytes_accessed=1400000, transcendentals=0),
         name="own_block",
     )(strain_rate, deflation, residual)

time: 67.8 us -> 69.4 us (1.024)
  Pallas kernels: 5.6 us -> 7.04 us
    pallas_call x1, Pallas kernels: 3.24 us -> 4.68 us  [per_device(): pl.pallas_call(self_kernel, out_shape=shape(72, cz), in_specs=[pl.BlockSp...]
    slice x2, local copies, waits for them, and re-layouts: 1.31 us -> 2.19 us  [per_device(): last_y = jnp.concatenate([deflation[:, :, -1], strain_rate[None, :, -1]], 0)]
  transfers between devices with their start and end apart: 4 -> 4, of which waited for: 1 -> 1; matrix products, arithmetic and copies ran while one was open for 2% -> 3% of each run, Pallas kernels for 5% -> 7%
where the time goes in v6:
time: 69.4 us; the launch traced here: 68.9 us
  blocking collectives  40.1 us (58%)
  starting transfers between devices  14.1 us (20%)
  Pallas kernels  7.04 us (10%)
  local copies, waits for them, and re-layouts  4.51 us (6%)
  waiting for transfers between devices  2.28 us (3%)
  between operations  0.74 us (1%)
    all_to_all x1, blocking collectives, per_device(): got = lax.all_to_all(near, 'sy', 0, 0)  28.2 us
    all_to_all x1, blocking collectives, per_device(): line = lax.all_to_all(messages, 'sx', 0, 0, axis_index_groups=rows)  12 us
    ppermute x1, starting transfers between devices, per_device(): lax.ppermute(last_y, 'sy', [(i, i + 1) for i in range(count_y - 1)])  5.75 us
    pallas_call x1, Pallas kernels, per_device(): pl.pallas_call(self_kernel, out_shape=shape(72, cz), in_specs=[pl.BlockSp...  4.68 us
    ppermute x1, starting transfers between devices, per_device(): lax.ppermute(line, 'sx', [(i, i + ROW) for i in range(count_x - ROW)])  3.32 us
    ppermute x1, starting transfers between devices, per_device(): lax.ppermute(last_x, 'sx', [(i, i + 1) for i in range(count_x - 1)])  3.12 us
    ppermute x1, waiting for transfers between devices, per_device(): lax.ppermute(line, 'sx', [(i, i + ROW) for i in range(count_x - ROW)])  2.27 us
    slice x2, local copies, waits for them, and re-layouts, per_device(): last_y = jnp.concatenate([deflation[:, :, -1], strain_rate[None, :, -1]], 0)  2.19 us
  transfers between devices with their start and end apart: 4, of which 1 were waited for; matrix products, arithmetic and copies ran while one was open for 3% of the time, Pallas kernels for 7%

profile of v6, /device:TPU:65, one launch (start us, length us, event | category | flops | bytes accessed | tf_op | source)
XLA Modules:
  0.0 68.9 jit_solution(3859862819416791383)
XLA Ops:
  0.6 0.7 %fusion.2 = (f32[1,16,128]{2,1,0:T(8,128)S(1)}, f32[1,16,128]{2,1,0:T(8,128)S(1)}) fusion(f32[16,16,128]{2,1,0:T(8,128)} %rate_ref.1), kind=kLoop, calls=%fused_computation.8 | loop fusion | bytes 32768 | tf_op jit(solution)/shard_map/slice | solution.py:282
  1.3 0.9 %slice_bitcast_fusion = (f32[8,16,128]{2,1,0:T(8,128)S(1)}, f32[8,16,128]{2,1,0:T(8,128)S(1)}) fusion(f32[8,16,16,128]{3,2,1,0:T(8,128)} %far_ref.1), kind=kLoop, calls=%fused_computation.4 | loop fusion | bytes 262144 | tf_op jit(solution)/shard_map/squeeze | solution.py:282
  2.2 3.1 %collective-permute-start = (f32[9,16,128]{2,1,0:T(8,128)S(1)}, f32[9,16,128]{2,1,0:T(8,128)S(1)}, u32[]{:S(2)}, u32[]{:S(2)}) collective-permute-start(f32[9,16,128]{2,1,0:T(8,128)S(1)} %pad_maximum_fusion.2), channel_id=1, source_target_pairs={{0,16},{16,32},{32,48},{48,64},{64,80},{80,96},{96,112},{112,128},... | collective-permute-start | bytes 221192 | tf_op jit(solution)/shard_map/ppermute | solution.py:284
  5.4 0.9 %fusion.1 = (f32[16,1,128]{2,1,0:T(1,128)S(1)}, f32[16,1,128]{2,1,0:T(1,128)S(1)}) fusion(f32[16,16,128]{2,1,0:T(8,128)} %rate_ref.1), kind=kLoop, calls=%fused_computation.7 | loop fusion | bytes 32768 | tf_op jit(solution)/shard_map/slice | solution.py:283
  6.3 1.3 %fusion = (f32[8,16,1,128]{3,2,1,0:T(1,128)S(1)}, f32[8,16,1,128]{3,2,1,0:T(1,128)S(1)}) fusion(f32[8,16,16,128]{3,2,1,0:T(8,128)} %far_ref.1), kind=kLoop, calls=%fused_computation.6 | loop fusion | bytes 262144 | tf_op jit(solution)/shard_map/slice | solution.py:283
  7.6 5.8 %collective-permute-start.1 = (f32[9,16,128]{2,1,0:T(8,128)S(1)}, f32[9,16,128]{2,1,0:T(8,128)S(1)}, u32[]{:S(2)}, u32[]{:S(2)}) collective-permute-start(f32[9,16,128]{2,1,0:T(8,128)S(1)} %pad_maximum_fusion.3), channel_id=1, source_target_pairs={{0,1},{1,2},{2,3},{3,4},{4,5},{5,6},{6,7},{7,8},{8,9},{9,10},{10,1... | collective-permute-start | bytes 221192 | tf_op jit(solution)/shard_map/ppermute | solution.py:285
  13.3 4.7 %own_block.1.self_ref = f32[72,128]{1,0:T(8,128)} custom-call(f32[16,16,128]{2,1,0:T(8,128)} %rate_ref.1, f32[8,16,16,128]{3,2,1,0:T(8,128)} %far_ref.1, f32[16,16,128]{2,1,0:T(8,128)} %res_ref.1), custom_call_target="tpu_custom_call" | custom-call | flops 10000000 | bytes 1400000 | tf_op jit(solution)/shard_map/own_block/pallas_call | solution.py:289
  18.0 0.0 copy-start
  18.1 0.0 collective-permute-done.below_x_ref
  18.1 0.0 collective-permute-done.1.below_y_ref
  18.1 0.7 %copy-done = f32[72,128]{1,0:T(8,128)S(1)} copy-done((f32[72,128]{1,0:T(8,128)S(1)}, f32[72,128]{1,0:T(8,128)}, u32[]{:S(2)}) %copy-start) | copy-done | bytes 36888
  18.8 0.5 face_blocks.1
  19.3 12.0 %all_to_all.10.line_ref = f32[8,1,256]{2,1,0:T(1,128)S(1)} all-to-all(f32[8,1,256]{2,1,0:T(1,128)S(1)} %face_blocks.1), channel_id=1, replica_groups={{0,16,32,48,64,80,96,112},{128,144,160,176,192,208,224,240},{256,272,28..., dimensions={0} | all-to-all | bytes 16384 | tf_op jit(solution)/shard_map/all_to_all | solution.py:316
  31.3 2.0 %collective-permute-start.3 = (f32[8,1,256]{2,1,0:T(1,128)S(1)}, f32[8,1,256]{2,1,0:T(1,128)S(1)}, u32[]{:S(2)}, u32[]{:S(2)}) collective-permute-start(f32[8,1,256]{2,1,0:T(1,128)S(1)} %all_to_all.10.line_ref), channel_id=1, source_target_pairs={{128,0},{144,16},{160,32},{176,48},{192,64},{208,80},{224,96},{240... | collective-permute-start | bytes 24584 | tf_op jit(solution)/shard_map/ppermute | solution.py:318
  33.2 3.3 %collective-permute-start.2 = (f32[8,1,256]{2,1,0:T(1,128)S(1)}, f32[8,1,256]{2,1,0:T(1,128)S(1)}, u32[]{:S(2)}, u32[]{:S(2)}) collective-permute-start(f32[8,1,256]{2,1,0:T(1,128)S(1)} %all_to_all.10.line_ref), channel_id=1, source_target_pairs={{0,128},{16,144},{32,160},{48,176},{64,192},{80,208},{96,224},{112... | collective-permute-start | bytes 24584 | tf_op jit(solution)/shard_map/ppermute | solution.py:317
  36.5 0.0 collective-permute-done.3.upper_ref
  36.6 2.3 %collective-permute-done.2.lower_ref = f32[8,1,256]{2,1,0:T(1,128)S(1)} collective-permute-done((f32[8,1,256]{2,1,0:T(1,128)S(1)}, f32[8,1,256]{2,1,0:T(1,128)S(1)}, u32[]{:S(2)}, u32[]{:S(2)}) %collective-permute-start.2) | collective-permute-done | bytes 8224 | tf_op jit(solution)/shard_map/ppermute | solution.py:317
  38.8 0.1 window.1
  38.9 28.2 %all_to_all.11.got_ref = f32[16,16,256]{2,1,0:T(8,128)S(1)} all-to-all(f32[16,16,256]{2,1,0:T(8,128)S(1)} %window.1), channel_id=1, replica_groups=mesh['sx'=64,'sy'=16] {'sy'}, dimensions={0} | all-to-all | bytes 524288 | tf_op jit(solution)/shard_map/all_to_all | solution.py:326
  67.1 1.8 %coarse_sweeps.1 = (f32[5,8,8]{2,1,0:T(8,128)}, f32[1,8]{1,0:T(1,128)}) custom-call(f32[16,16,256]{2,1,0:T(8,128)S(1)} %all_to_all.11.got_ref), custom_call_target="tpu_custom_call" | custom-call | tf_op jit(solution)/shard_map/coarse_sweeps/pallas_call | solution.py:327
  (3 shorter events, 0.0 us)
Async XLA Ops:
  2.2 15.8 %collective-permute-start = (f32[9,16,128]{2,1,0:T(8,128)S(1)}, f32[9,16,128]{2,1,0:T(8,128)S(1)}, u32[]{:S(2)}, u32[]{:S(2)}) collective-permute-start(f32[9,16,128]{2,1,0:T(8,128)S(1)} %pad_maximum_fusion.2), channel_id=1, source_target_pairs={{0,16},{16,32},{32,48},{48,64},{64,80},{80,96},{96,112},{112,128},... | collective-permute-start | bytes 221192 | tf_op jit(solution)/shard_map/ppermute | solution.py:284
  7.6 10.5 %collective-permute-start.1 = (f32[9,16,128]{2,1,0:T(8,128)S(1)}, f32[9,16,128]{2,1,0:T(8,128)S(1)}, u32[]{:S(2)}, u32[]{:S(2)}) collective-permute-start(f32[9,16,128]{2,1,0:T(8,128)S(1)} %pad_maximum_fusion.3), channel_id=1, source_target_pairs={{0,1},{1,2},{2,3},{3,4},{4,5},{5,6},{6,7},{7,8},{8,9},{9,10},{10,1... | collective-permute-start | bytes 221192 | tf_op jit(solution)/shard_map/ppermute | solution.py:285
  18.0 0.8 %copy-start = (f32[72,128]{1,0:T(8,128)S(1)}, f32[72,128]{1,0:T(8,128)}, u32[]{:S(2)}) copy-start(f32[72,128]{1,0:T(8,128)} %own_block.1.self_ref) | copy-start | bytes 110596
  31.3 5.3 %collective-permute-start.3 = (f32[8,1,256]{2,1,0:T(1,128)S(1)}, f32[8,1,256]{2,1,0:T(1,128)S(1)}, u32[]{:S(2)}, u32[]{:S(2)}) collective-permute-start(f32[8,1,256]{2,1,0:T(1,128)S(1)} %all_to_all.10.line_ref), channel_id=1, source_target_pairs={{128,0},{144,16},{160,32},{176,48},{192,64},{208,80},{224,96},{240... | collective-permute-start | bytes 24584 | tf_op jit(solution)/shard_map/ppermute | solution.py:318
  33.2 5.6 %collective-permute-start.2 = (f32[8,1,256]{2,1,0:T(1,128)S(1)}, f32[8,1,256]{2,1,0:T(1,128)S(1)}, u32[]{:S(2)}, u32[]{:S(2)}) collective-permute-start(f32[8,1,256]{2,1,0:T(1,128)S(1)} %all_to_all.10.line_ref), channel_id=1, source_target_pairs={{0,128},{16,144},{32,160},{48,176},{64,192},{80,208},{96,224},{112... | collective-permute-start | bytes 24584 | tf_op jit(solution)/shard_map/ppermute | solution.py:317

commit v7 on v3

--- a/solution.py
+++ b/solution.py
@@ -39,6 +39,19 @@
 
 def halves(x):
     return x[:8] + x[8:]
+
+
+def pack_kernel(rate_ref, vec_ref, last_x_ref, last_y_ref, first_x_ref, first_y_ref):
+    cx, cy, _ = rate_ref.shape
+    for a in range(NVEC):
+        last_x_ref[a] = vec_ref[a, cx - 1]
+        first_x_ref[a] = vec_ref[a, 0]
+        last_y_ref[a] = vec_ref[a, :, cy - 1, :]
+        first_y_ref[a] = vec_ref[a, :, 0, :]
+    last_x_ref[NVEC] = rate_ref[cx - 1]
+    first_x_ref[NVEC] = rate_ref[0]
+    last_y_ref[NVEC] = rate_ref[:, cy - 1, :]
+    first_y_ref[NVEC] = rate_ref[:, 0, :]
 
 
 def self_kernel(rate_ref, vec_ref, res_ref, out_ref, visc_ref, acc_ref, rhs_ref):
@@ -267,13 +280,15 @@
 
 def per_device(strain_rate, deflation, residual):
     count_x, count_y = lax.axis_size("sx"), lax.axis_size("sy")
-    last_x = jnp.concatenate([deflation[:, -1], strain_rate[None, -1]], 0)
-    last_y = jnp.concatenate([deflation[:, :, -1], strain_rate[None, :, -1]], 0)
+    cz = strain_rate.shape[-1]
+    last_x, last_y, first_x, first_y = pl.pallas_call(
+        pack_kernel,
+        out_shape=(shape(NVEC + 1, *strain_rate.shape[1:]), shape(NVEC + 1, strain_rate.shape[0], cz)) * 2,
+        compiler_params=PARAMS,
+        name="faces",
+    )(strain_rate, deflation)
     below_x = lax.ppermute(last_x, "sx", [(i, i + 1) for i in range(count_x - 1)])
     below_y = lax.ppermute(last_y, "sy", [(i, i + 1) for i in range(count_y - 1)])
-    first_x = jnp.concatenate([deflation[:, 0], strain_rate[None, 0]], 0)
-    first_y = jnp.concatenate([deflation[:, :, 0], strain_rate[None, :, 0]], 0)
-    cz = strain_rate.shape[-1]
     own_rows = pl.pallas_call(
         self_kernel,
         out_shape=shape(72, cz),

time: 67.8 us -> 65.9 us (0.972)
  local copies, waits for them, and re-layouts: 4.15 us -> 2.13 us
    slice x3 -> x0, local copies, waits for them, and re-layouts: 2.03 us -> none  [the longest x2 1.31 us: per_device(): last_y = jnp.concatenate([deflation[:, :, -1], strain_rate[None, :, -1]], 0)]
    unnamed x6, local copies, waits for them, and re-layouts: 1.23 us -> 2.13 us
    squeeze x1 -> x0, local copies, waits for them, and re-layouts: 0.88 us -> none  [per_device(): last_x = jnp.concatenate([deflation[:, -1], strain_rate[None, -1]], 0)]
  transfers between devices with their start and end apart: 4 -> 4, of which waited for: 1 -> 1; matrix products, arithmetic and copies ran while one was open for 2% -> 0% of each run, Pallas kernels for 5% -> 5%
where the time goes in v7:
time: 65.9 us; the launch traced here: 65.5 us
  blocking collectives  40.6 us (62%)
  starting transfers between devices  14.1 us (21%)
  Pallas kernels  5.68 us (9%)
  waiting for transfers between devices  2.28 us (3%)
  local copies, waits for them, and re-layouts  2.13 us (3%)
  between operations  0.72 us (1%)
    all_to_all x1, blocking collectives, per_device(): got = lax.all_to_all(near, 'sy', 0, 0)  28.6 us
    all_to_all x1, blocking collectives, per_device(): line = lax.all_to_all(messages, 'sx', 0, 0, axis_index_groups=rows)  12 us
    ppermute x1, starting transfers between devices, per_device(): lax.ppermute(last_y, 'sy', [(i, i + 1) for i in range(count_y - 1)])  5.75 us
    ppermute x1, starting transfers between devices, per_device(): lax.ppermute(line, 'sx', [(i, i + ROW) for i in range(count_x - ROW)])  3.32 us
    pallas_call x1, Pallas kernels, per_device(): pl.pallas_call(self_kernel, out_shape=shape(72, cz), scratch_shapes=[pltp...  3.25 us
    ppermute x1, starting transfers between devices, per_device(): lax.ppermute(last_x, 'sx', [(i, i + 1) for i in range(count_x - 1)])  3.12 us
    ppermute x1, waiting for transfers between devices, per_device(): lax.ppermute(line, 'sx', [(i, i + ROW) for i in range(count_x - ROW)])  2.27 us
    unnamed x6, local copies, waits for them, and re-layouts  2.13 us
  transfers between devices with their start and end apart: 4, of which 1 were waited for; matrix products, arithmetic and copies ran while one was open for 0% of the time, Pallas kernels for 5%

profile of v7, /device:TPU:65, one launch (start us, length us, event | category | flops | bytes accessed | tf_op | source)
XLA Modules:
  0.0 65.5 jit_solution(3124448894522219696)
XLA Ops:
  0.6 0.0 copy-start
  0.6 1.2 %copy-done = f32[8,16,16,128]{3,2,1,0:T(8,128)S(1)} copy-done((f32[8,16,16,128]{3,2,1,0:T(8,128)S(1)}, f32[8,16,16,128]{3,2,1,0:T(8,128)}, u32[]{:S(2)}) %copy-start) | copy-done | bytes 1048600
  1.9 0.0 copy-start.1
  1.9 0.9 %copy-done.1 = f32[16,16,128]{2,1,0:T(8,128)S(1)} copy-done((f32[16,16,128]{2,1,0:T(8,128)S(1)}, f32[16,16,128]{2,1,0:T(8,128)}, u32[]{:S(2)}) %copy-start.1) | copy-done | bytes 131096
  2.8 0.0 copy-start.2
  2.8 0.1 faces.1
  2.9 3.1 %collective-permute-start = (f32[9,16,128]{2,1,0:T(8,128)S(1)}, f32[9,16,128]{2,1,0:T(8,128)S(1)}, u32[]{:S(2)}, u32[]{:S(2)}) collective-permute-start(f32[9,16,128]{2,1,0:T(8,128)S(1)} %get-tuple-element.10), channel_id=1, source_target_pairs={{0,16},{16,32},{32,48},{48,64},{64,80},{80,96},{96,112},{112,128},... | collective-permute-start | bytes 221192 | tf_op jit(solution)/shard_map/ppermute | solution.py:290
  6.0 5.8 %collective-permute-start.1 = (f32[9,16,128]{2,1,0:T(8,128)S(1)}, f32[9,16,128]{2,1,0:T(8,128)S(1)}, u32[]{:S(2)}, u32[]{:S(2)}) collective-permute-start(f32[9,16,128]{2,1,0:T(8,128)S(1)} %get-tuple-element.11), channel_id=1, source_target_pairs={{0,1},{1,2},{2,3},{3,4},{4,5},{5,6},{6,7},{7,8},{8,9},{9,10},{10,1... | collective-permute-start | bytes 221192 | tf_op jit(solution)/shard_map/ppermute | solution.py:291
  11.7 0.0 copy-done.2
  11.7 3.2 %own_block.1.self_ref = f32[72,128]{1,0:T(8,128)S(1)} custom-call(f32[16,16,128]{2,1,0:T(8,128)S(1)} %copy-done.1, f32[8,16,16,128]{3,2,1,0:T(8,128)S(1)} %copy-done, f32[16,16,128]{2,1,0:T(8,128)S(1)} %copy-done.2), custom_call_target="tpu_custom_call" | custom-call | flops 10000000 | bytes 1400000 | tf_op jit(solution)/shard_map/own_block/pallas_call | solution.py:292
  15.0 0.0 collective-permute-done.below_x_ref
  15.0 0.0 collective-permute-done.1.below_y_ref
  15.0 0.5 face_blocks.1
  15.5 12.0 %all_to_all.10.line_ref = f32[8,1,256]{2,1,0:T(1,128)S(1)} all-to-all(f32[8,1,256]{2,1,0:T(1,128)S(1)} %face_blocks.1), channel_id=1, replica_groups={{0,16,32,48,64,80,96,112},{128,144,160,176,192,208,224,240},{256,272,28..., dimensions={0} | all-to-all | bytes 16384 | tf_op jit(solution)/shard_map/all_to_all | solution.py:312
  27.5 2.0 %collective-permute-start.3 = (f32[8,1,256]{2,1,0:T(1,128)S(1)}, f32[8,1,256]{2,1,0:T(1,128)S(1)}, u32[]{:S(2)}, u32[]{:S(2)}) collective-permute-start(f32[8,1,256]{2,1,0:T(1,128)S(1)} %all_to_all.10.line_ref), channel_id=1, source_target_pairs={{128,0},{144,16},{160,32},{176,48},{192,64},{208,80},{224,96},{240... | collective-permute-start | bytes 24584 | tf_op jit(solution)/shard_map/ppermute | solution.py:314
  29.4 3.3 %collective-permute-start.2 = (f32[8,1,256]{2,1,0:T(1,128)S(1)}, f32[8,1,256]{2,1,0:T(1,128)S(1)}, u32[]{:S(2)}, u32[]{:S(2)}) collective-permute-start(f32[8,1,256]{2,1,0:T(1,128)S(1)} %all_to_all.10.line_ref), channel_id=1, source_target_pairs={{0,128},{16,144},{32,160},{48,176},{64,192},{80,208},{96,224},{112... | collective-permute-start | bytes 24584 | tf_op jit(solution)/shard_map/ppermute | solution.py:313
  32.8 0.0 collective-permute-done.3.upper_ref
  32.8 2.3 %collective-permute-done.2.lower_ref = f32[8,1,256]{2,1,0:T(1,128)S(1)} collective-permute-done((f32[8,1,256]{2,1,0:T(1,128)S(1)}, f32[8,1,256]{2,1,0:T(1,128)S(1)}, u32[]{:S(2)}, u32[]{:S(2)}) %collective-permute-start.2) | collective-permute-done | bytes 8224 | tf_op jit(solution)/shard_map/ppermute | solution.py:313
  35.0 0.1 window.1
  35.1 28.6 %all_to_all.11.got_ref = f32[16,16,256]{2,1,0:T(8,128)S(1)} all-to-all(f32[16,16,256]{2,1,0:T(8,128)S(1)} %window.1), channel_id=1, replica_groups=mesh['sx'=64,'sy'=16] {'sy'}, dimensions={0} | all-to-all | bytes 524288 | tf_op jit(solution)/shard_map/all_to_all | solution.py:322
  63.8 1.8 %coarse_sweeps.1 = (f32[5,8,8]{2,1,0:T(8,128)}, f32[1,8]{1,0:T(1,128)}) custom-call(f32[16,16,256]{2,1,0:T(8,128)S(1)} %all_to_all.11.got_ref), custom_call_target="tpu_custom_call" | custom-call | tf_op jit(solution)/shard_map/coarse_sweeps/pallas_call | solution.py:323
Async XLA Ops:
  0.6 1.2 %copy-start = (f32[8,16,16,128]{3,2,1,0:T(8,128)S(1)}, f32[8,16,16,128]{3,2,1,0:T(8,128)}, u32[]{:S(2)}) copy-start(f32[8,16,16,128]{3,2,1,0:T(8,128)} %vec_ref.3) | copy-start | bytes 3145732
  1.9 0.9 %copy-start.1 = (f32[16,16,128]{2,1,0:T(8,128)S(1)}, f32[16,16,128]{2,1,0:T(8,128)}, u32[]{:S(2)}) copy-start(f32[16,16,128]{2,1,0:T(8,128)} %rate_ref.3) | copy-start | bytes 393220
  2.8 9.0 %copy-start.2 = (f32[16,16,128]{2,1,0:T(8,128)S(1)}, f32[16,16,128]{2,1,0:T(8,128)}, u32[]{:S(2)}) copy-start(f32[16,16,128]{2,1,0:T(8,128)} %res_ref.1) | copy-start | bytes 393220
  2.9 12.2 %collective-permute-start = (f32[9,16,128]{2,1,0:T(8,128)S(1)}, f32[9,16,128]{2,1,0:T(8,128)S(1)}, u32[]{:S(2)}, u32[]{:S(2)}) collective-permute-start(f32[9,16,128]{2,1,0:T(8,128)S(1)} %get-tuple-element.10), channel_id=1, source_target_pairs={{0,16},{16,32},{32,48},{48,64},{64,80},{80,96},{96,112},{112,128},... | collective-permute-start | bytes 221192 | tf_op jit(solution)/shard_map/ppermute | solution.py:290
  6.0 9.0 %collective-permute-start.1 = (f32[9,16,128]{2,1,0:T(8,128)S(1)}, f32[9,16,128]{2,1,0:T(8,128)S(1)}, u32[]{:S(2)}, u32[]{:S(2)}) collective-permute-start(f32[9,16,128]{2,1,0:T(8,128)S(1)} %get-tuple-element.11), channel_id=1, source_target_pairs={{0,1},{1,2},{2,3},{3,4},{4,5},{5,6},{6,7},{7,8},{8,9},{9,10},{10,1... | collective-permute-start | bytes 221192 | tf_op jit(solution)/shard_map/ppermute | solution.py:291
  27.5 5.3 %collective-permute-start.3 = (f32[8,1,256]{2,1,0:T(1,128)S(1)}, f32[8,1,256]{2,1,0:T(1,128)S(1)}, u32[]{:S(2)}, u32[]{:S(2)}) collective-permute-start(f32[8,1,256]{2,1,0:T(1,128)S(1)} %all_to_all.10.line_ref), channel_id=1, source_target_pairs={{128,0},{144,16},{160,32},{176,48},{192,64},{208,80},{224,96},{240... | collective-permute-start | bytes 24584 | tf_op jit(solution)/shard_map/ppermute | solution.py:314
  29.4 5.6 %collective-permute-start.2 = (f32[8,1,256]{2,1,0:T(1,128)S(1)}, f32[8,1,256]{2,1,0:T(1,128)S(1)}, u32[]{:S(2)}, u32[]{:S(2)}) collective-permute-start(f32[8,1,256]{2,1,0:T(1,128)S(1)} %all_to_all.10.line_ref), channel_id=1, source_target_pairs={{0,128},{16,144},{32,160},{48,176},{64,192},{80,208},{96,224},{112... | collective-permute-start | bytes 24584 | tf_op jit(solution)/shard_map/ppermute | solution.py:313

commit v8 on v7

--- a/solution.py
+++ b/solution.py
@@ -41,26 +41,25 @@
     return x[:8] + x[8:]
 
 
-def pack_kernel(rate_ref, vec_ref, last_x_ref, last_y_ref, first_x_ref, first_y_ref):
-    cx, cy, _ = rate_ref.shape
+def pack_kernel(visc_ref, vec_ref, last_x_ref, last_y_ref, first_x_ref, first_y_ref):
+    cx, cy, _ = visc_ref.shape
     for a in range(NVEC):
         last_x_ref[a] = vec_ref[a, cx - 1]
         first_x_ref[a] = vec_ref[a, 0]
         last_y_ref[a] = vec_ref[a, :, cy - 1, :]
         first_y_ref[a] = vec_ref[a, :, 0, :]
-    last_x_ref[NVEC] = rate_ref[cx - 1]
-    first_x_ref[NVEC] = rate_ref[0]
-    last_y_ref[NVEC] = rate_ref[:, cy - 1, :]
-    first_y_ref[NVEC] = rate_ref[:, 0, :]
-
-
-def self_kernel(rate_ref, vec_ref, res_ref, out_ref, visc_ref, acc_ref, rhs_ref):
+    last_x_ref[NVEC] = visc_ref[cx - 1]
+    first_x_ref[NVEC] = visc_ref[0]
+    last_y_ref[NVEC] = visc_ref[:, cy - 1, :]
+    first_y_ref[NVEC] = visc_ref[:, 0, :]
+
+
+def self_kernel(visc_ref, vec_ref, res_ref, out_ref, acc_ref, rhs_ref):
     at_top_x = lax.axis_index("sx") == lax.axis_size("sx") - 1
     at_top_y = lax.axis_index("sy") == lax.axis_size("sy") - 1
-    visc_ref[...] = viscosity(rate_ref[...])
     acc_ref[...] = jnp.zeros_like(acc_ref)
     rhs_ref[...] = jnp.zeros_like(rhs_ref)
-    cx, cy, cz = rate_ref.shape
+    cx, cy, cz = visc_ref.shape
     row = lax.broadcasted_iota(jnp.int32, (cy, cz), 0)
     lane = lax.broadcasted_iota(jnp.int32, (cy, cz), 1)
     top_x = jnp.where(at_top_x, 1.0, 0.5)
@@ -122,8 +121,8 @@
 
 def face_columns(axis, own, below):
     inner = lax.axis_index(axis) > 0
-    visc = viscosity(own[NVEC])
-    visc_below = viscosity(jnp.where(inner, below[NVEC], 1.0))
+    visc = own[NVEC]
+    visc_below = below[NVEC]
     coupling = jnp.where(inner, -0.5 * (visc + visc_below), 0.0)
     beside = 0.5 * jnp.where(inner, visc_below, visc)
     shared = jnp.where(inner, 0.5 * visc, 0.0)
@@ -281,26 +280,26 @@
 def per_device(strain_rate, deflation, residual):
     count_x, count_y = lax.axis_size("sx"), lax.axis_size("sy")
     cz = strain_rate.shape[-1]
+    viscous = viscosity(strain_rate)
     last_x, last_y, first_x, first_y = pl.pallas_call(
         pack_kernel,
         out_shape=(shape(NVEC + 1, *strain_rate.shape[1:]), shape(NVEC + 1, strain_rate.shape[0], cz)) * 2,
         compiler_params=PARAMS,
         name="faces",
-    )(strain_rate, deflation)
+    )(viscous, deflation)
     below_x = lax.ppermute(last_x, "sx", [(i, i + 1) for i in range(count_x - 1)])
     below_y = lax.ppermute(last_y, "sy", [(i, i + 1) for i in range(count_y - 1)])
     own_rows = pl.pallas_call(
         self_kernel,
         out_shape=shape(72, cz),
         scratch_shapes=[
-            pltpu.VMEM(strain_rate.shape, jnp.float32),
             pltpu.VMEM((64, 8, cz), jnp.float32),
             pltpu.VMEM((NVEC, 8, cz), jnp.float32),
         ],
         compiler_params=PARAMS,
         cost_estimate=pl.CostEstimate(flops=10000000, bytes_accessed=1400000, transcendentals=0),
         name="own_block",
-    )(strain_rate, deflation, residual)
+    )(viscous, deflation, residual)
     messages = pl.pallas_call(
         face_kernel,
         out_shape=shape(ROW, 1, WORDS),

time: 65.9 us -> 65.9 us (level)
  other arithmetic: 0 us -> 0.97 us
  local copies, waits for them, and re-layouts: 2.13 us -> 1.22 us
    add x0 -> x1, other arithmetic: none -> 0.97 us  [viscosity(): return lax.rsqrt(rate) + 0.5 * (1.0 - jnp.exp(-10.0 * rate)) / rate]
    unnamed x6 -> x4, local copies, waits for them, and re-layouts: 2.13 us -> 1.22 us
where the time goes in v8:
time: 65.9 us; the launch traced here: 65.6 us
  blocking collectives  40.7 us (62%)
  starting transfers between devices  14.1 us (21%)
  Pallas kernels  5.6 us (8%)
  waiting for transfers between devices  2.28 us (3%)
  local copies, waits for them, and re-layouts  1.22 us (2%)
  other arithmetic  0.97 us (1%)
  between operations  0.72 us (1%)
    all_to_all x1, blocking collectives, per_device(): got = lax.all_to_all(near, 'sy', 0, 0)  28.7 us
    all_to_all x1, blocking collectives, per_device(): line = lax.all_to_all(messages, 'sx', 0, 0, axis_index_groups=rows)  12 us
    ppermute x1, starting transfers between devices, per_device(): lax.ppermute(last_y, 'sy', [(i, i + 1) for i in range(count_y - 1)])  5.75 us
    ppermute x1, starting transfers between devices, per_device(): lax.ppermute(line, 'sx', [(i, i + ROW) for i in range(count_x - ROW)])  3.32 us
    pallas_call x1, Pallas kernels, per_device(): pl.pallas_call(self_kernel, out_shape=shape(72, cz), scratch_shapes=[pltp...  3.17 us
    ppermute x1, starting transfers between devices, per_device(): lax.ppermute(last_x, 'sx', [(i, i + 1) for i in range(count_x - 1)])  3.12 us
    ppermute x1, waiting for transfers between devices, per_device(): lax.ppermute(line, 'sx', [(i, i + ROW) for i in range(count_x - ROW)])  2.27 us
    ppermute x1, starting transfers between devices, per_device(): lax.ppermute(line, 'sx', [(i + ROW, i) for i in range(count_x - ROW)])  1.95 us
  transfers between devices with their start and end apart: 4, of which 1 were waited for; matrix products, arithmetic and copies ran while one was open for 0% of the time, Pallas kernels for 5%

profile of v8, /device:TPU:65, one launch (start us, length us, event | category | flops | bytes accessed | tf_op | source)
XLA Modules:
  0.0 65.6 jit_solution(16728495225713199029)
XLA Ops:
  0.6 1.0 %divide_add_fusion.visc_ref = f32[16,16,128]{2,1,0:T(8,128)S(1)} fusion(f32[16,16,128]{2,1,0:T(8,128)} %param.3), kind=kLoop, calls=%fused_computation | loop fusion | flops 163840 | bytes 262144 | tf_op jit(solution)/shard_map/add | solution.py:21
  1.6 0.0 copy-start
  1.6 1.2 %copy-done = f32[8,16,16,128]{3,2,1,0:T(8,128)S(1)} copy-done((f32[8,16,16,128]{3,2,1,0:T(8,128)S(1)}, f32[8,16,16,128]{3,2,1,0:T(8,128)}, u32[]{:S(2)}) %copy-start) | copy-done | bytes 1048600
  2.8 0.0 copy-start.1
  2.8 0.1 faces.1
  2.9 3.1 %collective-permute-start = (f32[9,16,128]{2,1,0:T(8,128)S(1)}, f32[9,16,128]{2,1,0:T(8,128)S(1)}, u32[]{:S(2)}, u32[]{:S(2)}) collective-permute-start(f32[9,16,128]{2,1,0:T(8,128)S(1)} %get-tuple-element.10), channel_id=1, source_target_pairs={{0,16},{16,32},{32,48},{48,64},{64,80},{80,96},{96,112},{112,128},... | collective-permute-start | bytes 221192 | tf_op jit(solution)/shard_map/ppermute | solution.py:290
  6.0 5.8 %collective-permute-start.1 = (f32[9,16,128]{2,1,0:T(8,128)S(1)}, f32[9,16,128]{2,1,0:T(8,128)S(1)}, u32[]{:S(2)}, u32[]{:S(2)}) collective-permute-start(f32[9,16,128]{2,1,0:T(8,128)S(1)} %get-tuple-element.11), channel_id=1, source_target_pairs={{0,1},{1,2},{2,3},{3,4},{4,5},{5,6},{6,7},{7,8},{8,9},{9,10},{10,1... | collective-permute-start | bytes 221192 | tf_op jit(solution)/shard_map/ppermute | solution.py:291
  11.8 0.0 copy-done.1
  11.8 3.2 %own_block.1.self_ref = f32[72,128]{1,0:T(8,128)S(1)} custom-call(f32[16,16,128]{2,1,0:T(8,128)S(1)} %divide_add_fusion.visc_ref, f32[8,16,16,128]{3,2,1,0:T(8,128)S(1)} %copy-done, f32[16,16,128]{2,1,0:T(8,128)S(1)} %copy-done.1), custom_call_target="tpu_custom_call" | custom-call | flops 10000000 | bytes 1400000 | tf_op jit(solution)/shard_map/own_block/pallas_call | solution.py:292
  15.0 0.0 collective-permute-done.below_x_ref
  15.0 0.0 collective-permute-done.1.below_y_ref
  15.0 0.5 face_blocks.1
  15.5 12.0 %all_to_all.10.line_ref = f32[8,1,256]{2,1,0:T(1,128)S(1)} all-to-all(f32[8,1,256]{2,1,0:T(1,128)S(1)} %face_blocks.1), channel_id=1, replica_groups={{0,16,32,48,64,80,96,112},{128,144,160,176,192,208,224,240},{256,272,28..., dimensions={0} | all-to-all | bytes 16384 | tf_op jit(solution)/shard_map/all_to_all | solution.py:311
  27.5 2.0 %collective-permute-start.3 = (f32[8,1,256]{2,1,0:T(1,128)S(1)}, f32[8,1,256]{2,1,0:T(1,128)S(1)}, u32[]{:S(2)}, u32[]{:S(2)}) collective-permute-start(f32[8,1,256]{2,1,0:T(1,128)S(1)} %all_to_all.10.line_ref), channel_id=1, source_target_pairs={{128,0},{144,16},{160,32},{176,48},{192,64},{208,80},{224,96},{240... | collective-permute-start | bytes 24584 | tf_op jit(solution)/shard_map/ppermute | solution.py:313
  29.4 3.3 %collective-permute-start.2 = (f32[8,1,256]{2,1,0:T(1,128)S(1)}, f32[8,1,256]{2,1,0:T(1,128)S(1)}, u32[]{:S(2)}, u32[]{:S(2)}) collective-permute-start(f32[8,1,256]{2,1,0:T(1,128)S(1)} %all_to_all.10.line_ref), channel_id=1, source_target_pairs={{0,128},{16,144},{32,160},{48,176},{64,192},{80,208},{96,224},{112... | collective-permute-start | bytes 24584 | tf_op jit(solution)/shard_map/ppermute | solution.py:312
  32.8 0.0 collective-permute-done.3.upper_ref
  32.8 2.3 %collective-permute-done.2.lower_ref = f32[8,1,256]{2,1,0:T(1,128)S(1)} collective-permute-done((f32[8,1,256]{2,1,0:T(1,128)S(1)}, f32[8,1,256]{2,1,0:T(1,128)S(1)}, u32[]{:S(2)}, u32[]{:S(2)}) %collective-permute-start.2) | collective-permute-done | bytes 8224 | tf_op jit(solution)/shard_map/ppermute | solution.py:312
  35.0 0.1 window.1
  35.1 28.7 %all_to_all.11.got_ref = f32[16,16,256]{2,1,0:T(8,128)S(1)} all-to-all(f32[16,16,256]{2,1,0:T(8,128)S(1)} %window.1), channel_id=1, replica_groups=mesh['sx'=64,'sy'=16] {'sy'}, dimensions={0} | all-to-all | bytes 524288 | tf_op jit(solution)/shard_map/all_to_all | solution.py:321
  63.8 1.8 %coarse_sweeps.1 = (f32[5,8,8]{2,1,0:T(8,128)}, f32[1,8]{1,0:T(1,128)}) custom-call(f32[16,16,256]{2,1,0:T(8,128)S(1)} %all_to_all.11.got_ref), custom_call_target="tpu_custom_call" | custom-call | tf_op jit(solution)/shard_map/coarse_sweeps/pallas_call | solution.py:322
Async XLA Ops:
  1.6 1.2 %copy-start = (f32[8,16,16,128]{3,2,1,0:T(8,128)S(1)}, f32[8,16,16,128]{3,2,1,0:T(8,128)}, u32[]{:S(2)}) copy-start(f32[8,16,16,128]{3,2,1,0:T(8,128)} %vec_ref.3) | copy-start | bytes 3145732
  2.8 9.0 %copy-start.1 = (f32[16,16,128]{2,1,0:T(8,128)S(1)}, f32[16,16,128]{2,1,0:T(8,128)}, u32[]{:S(2)}) copy-start(f32[16,16,128]{2,1,0:T(8,128)} %res_ref.1) | copy-start | bytes 393220
  2.9 12.1 %collective-permute-start = (f32[9,16,128]{2,1,0:T(8,128)S(1)}, f32[9,16,128]{2,1,0:T(8,128)S(1)}, u32[]{:S(2)}, u32[]{:S(2)}) collective-permute-start(f32[9,16,128]{2,1,0:T(8,128)S(1)} %get-tuple-element.10), channel_id=1, source_target_pairs={{0,16},{16,32},{32,48},{48,64},{64,80},{80,96},{96,112},{112,128},... | collective-permute-start | bytes 221192 | tf_op jit(solution)/shard_map/ppermute | solution.py:290
  6.0 9.0 %collective-permute-start.1 = (f32[9,16,128]{2,1,0:T(8,128)S(1)}, f32[9,16,128]{2,1,0:T(8,128)S(1)}, u32[]{:S(2)}, u32[]{:S(2)}) collective-permute-start(f32[9,16,128]{2,1,0:T(8,128)S(1)} %get-tuple-element.11), channel_id=1, source_target_pairs={{0,1},{1,2},{2,3},{3,4},{4,5},{5,6},{6,7},{7,8},{8,9},{9,10},{10,1... | collective-permute-start | bytes 221192 | tf_op jit(solution)/shard_map/ppermute | solution.py:291
  27.5 5.3 %collective-permute-start.3 = (f32[8,1,256]{2,1,0:T(1,128)S(1)}, f32[8,1,256]{2,1,0:T(1,128)S(1)}, u32[]{:S(2)}, u32[]{:S(2)}) collective-permute-start(f32[8,1,256]{2,1,0:T(1,128)S(1)} %all_to_all.10.line_ref), channel_id=1, source_target_pairs={{128,0},{144,16},{160,32},{176,48},{192,64},{208,80},{224,96},{240... | collective-permute-start | bytes 24584 | tf_op jit(solution)/shard_map/ppermute | solution.py:313
  29.4 5.6 %collective-permute-start.2 = (f32[8,1,256]{2,1,0:T(1,128)S(1)}, f32[8,1,256]{2,1,0:T(1,128)S(1)}, u32[]{:S(2)}, u32[]{:S(2)}) collective-permute-start(f32[8,1,256]{2,1,0:T(1,128)S(1)} %all_to_all.10.line_ref), channel_id=1, source_target_pairs={{0,128},{16,144},{32,160},{48,176},{64,192},{80,208},{96,224},{112... | collective-permute-start | bytes 24584 | tf_op jit(solution)/shard_map/ppermute | solution.py:312
